TPU v7x, 32 devices: a whole 2x2x4 slice. The times are simulated.
32 devices in a mesh: dp: 8 (over z, x), row: 2 (over core), col: 2 (over y).
Axes of the slice: x: 2, y: 2, z: 4, core: 2. Of those that a mesh axis runs over, the one named last changes fastest.
Arguments:
- tokens: bfloat16 [4096, 1280], P(('dp', 'row', 'col')), may hold values from -6 to 6
- cotangent: bfloat16 [4096, 1280], P(('dp', 'row', 'col')), may hold values from -6 to 6
- seg_ids: int32 [32, 128], P('dp'), may hold values from 0 to 12, as said below
- parents: int32 [32, 13], P('dp'), may hold values from 0 to 4, as said below
- norm1_gain: float32 [1280], P('col'), may hold values from 0.5 to 1.5
- w_query: bfloat16 [1280, 20, 64], P('col', 'row', 'dp'), may hold values from -0.15625 to 0.15625
- key_value_weight: bfloat16 [1280, 2, 320], P('col', 'row', 'dp'), may hold values from -0.15625 to 0.15625
- w_out: bfloat16 [20, 64, 1280], P('row', 'dp', 'col'), may hold values from -0.625 to 0.625
- norm2_gain: float32 [1280], P('col'), may hold values from 0.5 to 1.5
- w_gate: bfloat16 [1280, 3584], P('col', ('dp', 'row')), may hold values from -0.15625 to 0.15625
- w_up: bfloat16 [1280, 3584], P('col', ('dp', 'row')), may hold values from -0.15625 to 0.15625
- w_down: bfloat16 [3584, 1280], P(('dp', 'row'), 'col'), may hold values from -0.09375 to 0.09375
Outputs:
- layer_out: bfloat16 [4096, 1280], P(('dp', 'row', 'col'))
- in_grad: bfloat16 [4096, 1280], P(('dp', 'row', 'col'))
- norm1_grad: float32 [1280], P('col')
- query_grad: float32 [1280, 20, 64], P('col', 'row', 'dp')
- keyval_grad: float32 [1280, 2, 320], P('col', 'row', 'dp')
- out_grad: float32 [20, 64, 1280], P('row', 'dp', 'col')
- norm2_grad: float32 [1280], P('col')
- gate_grad: float32 [1280, 3584], P('col', ('dp', 'row'))
- up_grad: float32 [1280, 3584], P('col', ('dp', 'row'))
- down_grad: float32 [3584, 1280], P(('dp', 'row'), 'col')
Inputs may be any that keep to these rules, and one draw needn't show every extreme that they name: `seg_ids`: along each tree the segment number never falls, the first 42 tokens are segment 0, and each of the 13 segments holds at least one token. `parents`: entry s of a tree is the parent of segment s: 0 for segments 0 to 4; segments 5 to 12 each have one of segments 1 to 4 as parent, and each of segments 1 to 4 is the parent of exactly two of them.
All inputs are finite; a program needn't handle non-finite values.
Results may differ from a plain program's by a relative error of at most 0.018.
Values may be sent and summed in bfloat16 or wider, within the bound.
A program may use at most 128 MiB of HBM per device.

v0:
```python
import math

import jax
import jax.numpy as jnp
from jax import lax
from jax.sharding import PartitionSpec as P

MODEL_WIDTH = 1280
QUERY_HEADS = 20
KEY_VALUE_HEADS = 5
HEAD_SIZE = 64
TREE_TOKENS = 128
SEGS = 13
MICRO = 2


EPS = 1e-05
THETA = 10000.0
HIGH = lax.Precision.HIGHEST


def tree_layout(segment, parent):
    labels = jnp.arange(SEGS, dtype=jnp.int32)
    member = (segment[:, None] == labels[None, :]).astype(jnp.float32)
    link = ((parent[:, None] == labels[None, :]) & (labels[:, None] > 0)).astype(jnp.float32)
    ident = jnp.eye(SEGS, dtype=jnp.float32)

    def climb(level, reach):
        return ident + jnp.dot(link, reach, precision=HIGH)

    reach = lax.fori_loop(0, SEGS, climb, ident)
    visible = jnp.dot(jnp.dot(member, reach, precision=HIGH), member.T, precision=HIGH) > 0.5
    places = jnp.arange(segment.shape[0], dtype=jnp.int32)
    allowed = visible & (places[:, None] >= places[None, :])
    sizes = jnp.sum(member, axis=0)
    earlier = (labels[None, :] < labels[:, None]).astype(jnp.float32)
    starts = jnp.dot(earlier, sizes, precision=HIGH)
    above = jnp.dot(reach, sizes, precision=HIGH) - sizes
    tree_depth = places.astype(jnp.float32) + jnp.dot(member, above - starts, precision=HIGH)
    return (allowed, tree_depth)


def rotate(value_rows, tree_depth, sign):
    half = value_rows.shape[-1] // 2
    freqs = jnp.arange(half, dtype=jnp.float32) * (2.0 / value_rows.shape[-1])
    inverse = jnp.exp(freqs * -math.log(THETA))
    angle = tree_depth[:, None] * inverse[None, :]
    cosine = jnp.cos(angle)[:, None, :]
    sine = sign * jnp.sin(angle)[:, None, :]
    first = value_rows[..., :half]
    second = value_rows[..., half:]
    return jnp.concatenate(
        [first * cosine - second * sine, second * cosine + first * sine], axis=-1
    )


def product(left, right):
    return jnp.dot(left, right, preferred_element_type=jnp.float32)


def body(
    tokens,
    cotangent,
    seg_ids,
    parents,
    norm1_gain,
    w_query,
    key_value_weight,
    w_out,
    norm2_gain,
    w_gate,
    w_up,
    w_down,
):
    columns = lax.axis_size("col")
    row_index = lax.axis_index("row")
    col_index = lax.axis_index("col")
    feature_width = MODEL_WIDTH // columns
    half_rows = columns * TREE_TOKENS // 2
    heads_here = QUERY_HEADS // 2
    query_total_width = heads_here * HEAD_SIZE
    heads_per_group = QUERY_HEADS // KEY_VALUE_HEADS
    scale = HEAD_SIZE ** (-0.5)
    stream_rows, cot_rows = (
        lax.all_to_all(tokens, "col", split_axis=1, concat_axis=0, tiled=True),
        lax.all_to_all(cotangent, "col", split_axis=1, concat_axis=0, tiled=True),
    )

    def col_total(value_rows):
        return lax.psum(value_rows, "col")

    def gather_rows(value_rows):
        return lax.all_gather(value_rows, "row", axis=0, tiled=True)

    def gather_cols(value_rows):
        return lax.all_gather(value_rows, "col", axis=0, tiled=True)

    def col_reduce(term, rows):
        return lax.psum_scatter(
            term(jnp.int32(0), rows * lax.axis_size("col")), "col", scatter_dimension=0, tiled=True
        )

    def row_reduce(term, rows):
        return lax.psum_scatter(
            term(jnp.int32(0), rows * lax.axis_size("row")), "row", scatter_dimension=0, tiled=True
        )

    def fetch():
        blocks = (
            lax.all_gather(w_query, "dp", axis=2, tiled=True),
            lax.all_gather(key_value_weight, "dp", axis=2, tiled=True),
            lax.all_gather(w_out, "dp", axis=1, tiled=True),
            lax.all_gather(w_gate, "dp", axis=1, tiled=True),
            lax.all_gather(w_up, "dp", axis=1, tiled=True),
            lax.all_gather(w_down, "dp", axis=0, tiled=True),
        )
        wide = None
        return (blocks, wide)

    def local_heads(pair_part):
        spread_heads = jnp.repeat(pair_part, heads_per_group, axis=1)
        return lax.dynamic_slice_in_dim(spread_heads, row_index * heads_here, heads_here, 1)

    def fold_heads(grad_here):
        spread_heads = jnp.zeros((TREE_TOKENS, QUERY_HEADS, HEAD_SIZE), jnp.float32)
        spread_heads = lax.dynamic_update_slice_in_dim(
            spread_heads, grad_here, row_index * heads_here, 1
        )
        return jnp.sum(
            spread_heads.reshape(TREE_TOKENS, KEY_VALUE_HEADS, heads_per_group, HEAD_SIZE), axis=2
        )

    gradients = (
        jnp.zeros((feature_width,), jnp.float32),
        jnp.zeros((feature_width, heads_here, HEAD_SIZE), jnp.float32),
        jnp.zeros((feature_width, 1, KEY_VALUE_HEADS * HEAD_SIZE), jnp.float32),
        jnp.zeros((heads_here, HEAD_SIZE, feature_width), jnp.float32),
        jnp.zeros((feature_width,), jnp.float32),
        jnp.zeros((feature_width, w_gate.shape[1] * lax.axis_size("dp")), jnp.float32),
        jnp.zeros((feature_width, w_up.shape[1] * lax.axis_size("dp")), jnp.float32),
        jnp.zeros((w_down.shape[0] * lax.axis_size("dp"), feature_width), jnp.float32),
    )
    results = []
    input_grads = []
    for batch_index in range(MICRO):
        blocks, wide = fetch()
        (
            forward_query_block,
            forward_key_value_block,
            forward_out_block,
            forward_gate_block,
            forward_up_block,
            forward_down_block,
        ) = blocks
        forward_query_matrix = forward_query_block.reshape(feature_width, query_total_width)
        forward_key_value_matrix = forward_key_value_block.reshape(
            feature_width, KEY_VALUE_HEADS * HEAD_SIZE
        )
        forward_out_matrix = forward_out_block.reshape(query_total_width, feature_width)
        forward_stream = lax.dynamic_slice_in_dim(
            stream_rows, batch_index * half_rows, half_rows, 0
        ).astype(jnp.float32)
        forward_rstd1 = lax.rsqrt(
            col_total(jnp.sum(forward_stream * forward_stream, axis=1)) / MODEL_WIDTH + EPS
        )
        normed = (forward_stream * forward_rstd1[:, None] * norm1_gain).astype(jnp.bfloat16)
        forward_normed_all = gather_rows(normed)

        def qkv_term(start, count):
            return jnp.concatenate(
                [
                    product(forward_normed_all, forward_query_matrix),
                    product(forward_normed_all, forward_key_value_matrix),
                ],
                axis=1,
            )

        projected_rows = col_reduce(qkv_term, TREE_TOKENS)
        half_cols = columns // 2
        tree_slot = (
            col_index // half_cols * (MICRO * half_cols)
            + batch_index * half_cols
            + col_index % half_cols
        )
        segment = lax.dynamic_index_in_dim(seg_ids, tree_slot, 0, keepdims=False)
        parent = lax.dynamic_index_in_dim(parents, tree_slot, 0, keepdims=False)
        forward_allowed, forward_tree_depth = tree_layout(segment, parent)
        query_pre = projected_rows[:, :query_total_width].reshape(
            TREE_TOKENS, heads_here, HEAD_SIZE
        )
        forward_query = rotate(query_pre, forward_tree_depth, 1.0).astype(jnp.bfloat16)
        own_unrotated = projected_rows[:, query_total_width:].reshape(
            TREE_TOKENS, KEY_VALUE_HEADS, HEAD_SIZE
        )
        own_part = jnp.where(
            row_index == 0, rotate(own_unrotated, forward_tree_depth, 1.0), own_unrotated
        ).astype(jnp.bfloat16)
        forward_pair = lax.all_gather(own_part[:, None], "row", axis=1, tiled=True)
        forward_keys_here = local_heads(forward_pair[:, 0])
        forward_values_here = local_heads(forward_pair[:, 1])
        forward_scores = (
            jnp.einsum(
                "qhd,khd->hqk", forward_query, forward_keys_here, preferred_element_type=jnp.float32
            )
            * scale
        )
        forward_masked = jnp.where(forward_allowed[None], forward_scores, -1e30)
        row_max = jnp.max(forward_masked, axis=-1, keepdims=True)
        forward_total = (
            jnp.log(jnp.sum(jnp.exp(forward_masked - row_max), axis=-1, keepdims=True)) + row_max
        )
        probs = jnp.exp(forward_masked - forward_total).astype(jnp.bfloat16)
        mixed = jnp.einsum(
            "hqk,khd->qhd", probs, forward_values_here, preferred_element_type=jnp.float32
        )
        mixed = mixed.astype(jnp.bfloat16).reshape(TREE_TOKENS, query_total_width)
        forward_mixed_all = gather_cols(mixed)

        def out_term(start, count):
            return product(forward_mixed_all, forward_out_matrix)

        forward_resid = forward_stream + row_reduce(out_term, half_rows)
        forward_rstd2 = lax.rsqrt(
            col_total(jnp.sum(forward_resid * forward_resid, axis=1)) / MODEL_WIDTH + EPS
        )
        normed2 = (forward_resid * forward_rstd2[:, None] * norm2_gain).astype(jnp.bfloat16)
        normed2_all = gather_rows(normed2)
        forward_hidden_here = forward_gate_block.shape[1]

        def gate_term(start, count):
            return jnp.concatenate(
                [product(normed2_all, forward_gate_block), product(normed2_all, forward_up_block)],
                axis=1,
            )

        gate_up = col_reduce(gate_term, TREE_TOKENS)
        forward_gate = gate_up[:, :forward_hidden_here]
        forward_up_part = gate_up[:, forward_hidden_here:]
        hidden = (jax.nn.silu(forward_gate) * forward_up_part).astype(jnp.bfloat16)
        forward_hidden_all = gather_cols(hidden)

        def down_term(start, count):
            return product(forward_hidden_all, forward_down_block)

        result = (forward_resid + row_reduce(down_term, half_rows)).astype(jnp.bfloat16)
        forward_saved = (
            forward_stream,
            forward_rstd1,
            forward_normed_all,
            forward_query,
            forward_pair,
            forward_total,
            forward_allowed,
            forward_tree_depth,
            forward_mixed_all,
            forward_resid,
            forward_rstd2,
            normed2_all,
            forward_gate,
            forward_up_part,
            forward_hidden_all,
        )
        result, saved = (result, forward_saved)
        blocks, wide = fetch()
        backward_gradients = gradients
        query_block, key_value_block, out_block, gate_block, up_block, down_block = blocks
        (
            stream,
            rstd1,
            normed_all,
            query,
            pair,
            total,
            allowed,
            tree_depth,
            mixed_all,
            resid,
            rstd2,
            kept_features,
            gate,
            up_part,
            hidden_all,
        ) = saved
        query_matrix = query_block.reshape(feature_width, query_total_width)
        key_value_matrix = key_value_block.reshape(feature_width, KEY_VALUE_HEADS * HEAD_SIZE)
        out_matrix = out_block.reshape(query_total_width, feature_width)
        hidden_here = gate_block.shape[1]
        cot_low = lax.dynamic_slice_in_dim(cot_rows, batch_index * half_rows, half_rows, 0)
        cot_full = cot_low.astype(jnp.float32)
        cot_all = gather_rows(cot_low)
        down_grad = jnp.einsum("tf,td->fd", hidden_all, cot_all, preferred_element_type=jnp.float32)

        def hidden_term(start, count):
            return jnp.einsum("td,fd->tf", cot_all, down_block, preferred_element_type=jnp.float32)

        d_hidden = col_reduce(hidden_term, TREE_TOKENS)
        sigmoid_gate = jax.nn.sigmoid(gate)
        d_up = (d_hidden * gate * sigmoid_gate).astype(jnp.bfloat16)
        d_gate = (d_hidden * up_part * sigmoid_gate * (1.0 + gate * (1.0 - sigmoid_gate))).astype(
            jnp.bfloat16
        )
        d_both = gather_cols(jnp.concatenate([d_gate, d_up], axis=1))
        gate_grad = jnp.einsum(
            "td,tf->df", kept_features, d_both[:, :hidden_here], preferred_element_type=jnp.float32
        )
        up_grad = jnp.einsum(
            "td,tf->df", kept_features, d_both[:, hidden_here:], preferred_element_type=jnp.float32
        )

        def back2_term(start, count):
            first = jnp.einsum(
                "tf,df->td", d_both[:, :hidden_here], gate_block, preferred_element_type=jnp.float32
            )
            return first + jnp.einsum(
                "tf,df->td", d_both[:, hidden_here:], up_block, preferred_element_type=jnp.float32
            )

        d_normed2 = row_reduce(back2_term, half_rows)
        scaled2 = d_normed2 * norm2_gain
        gain2_grad = jnp.sum(d_normed2 * resid * rstd2[:, None], axis=0)
        inner2 = col_total(jnp.sum(scaled2 * resid, axis=1))
        d_resid = (
            cot_full
            + rstd2[:, None] * scaled2
            - resid * (rstd2 * rstd2 * rstd2 * inner2 / MODEL_WIDTH)[:, None]
        )
        d_attn_all = gather_rows(d_resid.astype(jnp.bfloat16))
        out_grad = jnp.einsum(
            "tq,td->qd", mixed_all, d_attn_all, preferred_element_type=jnp.float32
        )

        def mixed_term(start, count):
            return jnp.einsum(
                "td,qd->tq", d_attn_all, out_matrix, preferred_element_type=jnp.float32
            )

        d_mixed = (
            col_reduce(mixed_term, TREE_TOKENS)
            .astype(jnp.bfloat16)
            .reshape(TREE_TOKENS, heads_here, HEAD_SIZE)
        )
        keys_here = local_heads(pair[:, 0])
        values_here = local_heads(pair[:, 1])
        scores = (
            jnp.einsum("qhd,khd->hqk", query, keys_here, preferred_element_type=jnp.float32) * scale
        )
        masked = jnp.where(allowed[None], scores, -1e30)
        probs_full = jnp.exp(masked - total)
        probs_low = probs_full.astype(jnp.bfloat16)
        d_probs = jnp.einsum(
            "qhd,khd->hqk", d_mixed, values_here, preferred_element_type=jnp.float32
        )
        delta = jnp.sum(probs_full * d_probs, axis=-1, keepdims=True)
        d_scores = (probs_full * (d_probs - delta)).astype(jnp.bfloat16)
        d_query = (
            jnp.einsum("hqk,khd->qhd", d_scores, keys_here, preferred_element_type=jnp.float32)
            * scale
        )
        d_keys = (
            jnp.einsum("hqk,qhd->khd", d_scores, query, preferred_element_type=jnp.float32) * scale
        )
        d_values = jnp.einsum(
            "hqk,qhd->khd", probs_low, d_mixed, preferred_element_type=jnp.float32
        )
        d_pair = jnp.stack([fold_heads(d_keys), fold_heads(d_values)], axis=1)
        own_gradient = lax.psum_scatter(
            d_pair.astype(jnp.bfloat16), "row", scatter_dimension=1, tiled=True
        ).astype(jnp.float32)[:, 0]
        own_gradient = jnp.where(
            row_index == 0, rotate(own_gradient, tree_depth, -1.0), own_gradient
        )
        query_pre_gradient = rotate(d_query, tree_depth, -1.0)
        d_proj = jnp.concatenate(
            [
                query_pre_gradient.reshape(TREE_TOKENS, query_total_width),
                own_gradient.reshape(TREE_TOKENS, KEY_VALUE_HEADS * HEAD_SIZE),
            ],
            axis=1,
        ).astype(jnp.bfloat16)
        d_proj_all = gather_cols(d_proj)
        query_grad = jnp.einsum(
            "td,tq->dq",
            normed_all,
            d_proj_all[:, :query_total_width],
            preferred_element_type=jnp.float32,
        )
        keyval_grad = jnp.einsum(
            "td,tq->dq",
            normed_all,
            d_proj_all[:, query_total_width:],
            preferred_element_type=jnp.float32,
        )
        in_matrix = jnp.concatenate([query_matrix, key_value_matrix], axis=1)

        def back1_term(start, count):
            return jnp.einsum(
                "tq,dq->td", d_proj_all, in_matrix, preferred_element_type=jnp.float32
            )

        d_normed = row_reduce(back1_term, half_rows)
        scaled1 = d_normed * norm1_gain
        gain1_grad = jnp.sum(d_normed * stream * rstd1[:, None], axis=0)
        inner1 = col_total(jnp.sum(scaled1 * stream, axis=1))
        d_stream = (
            d_resid
            + rstd1[:, None] * scaled1
            - stream * (rstd1 * rstd1 * rstd1 * inner1 / MODEL_WIDTH)[:, None]
        )
        updates = (
            gain1_grad,
            query_grad.reshape(query_block.shape),
            keyval_grad.reshape(key_value_block.shape),
            out_grad.reshape(out_block.shape),
            gain2_grad,
            gate_grad,
            up_grad,
            down_grad,
        )
        backward_gradients = tuple((a + b for a, b in zip(backward_gradients, updates)))
        d_stream, gradients = (d_stream.astype(jnp.bfloat16), backward_gradients)
        results.append(result)
        input_grads.append(d_stream)
    shards = (
        lax.psum_scatter(
            gradients[1].astype(jnp.bfloat16), "dp", scatter_dimension=2, tiled=True
        ).astype(jnp.float32),
        lax.psum_scatter(
            gradients[2].astype(jnp.bfloat16), "dp", scatter_dimension=2, tiled=True
        ).astype(jnp.float32),
        lax.psum_scatter(
            gradients[3].astype(jnp.bfloat16), "dp", scatter_dimension=1, tiled=True
        ).astype(jnp.float32),
        lax.psum_scatter(
            gradients[5].astype(jnp.bfloat16), "dp", scatter_dimension=1, tiled=True
        ).astype(jnp.float32),
        lax.psum_scatter(
            gradients[6].astype(jnp.bfloat16), "dp", scatter_dimension=1, tiled=True
        ).astype(jnp.float32),
        lax.psum_scatter(
            gradients[7].astype(jnp.bfloat16), "dp", scatter_dimension=0, tiled=True
        ).astype(jnp.float32),
    )
    gains = lax.psum((gradients[0], gradients[4]), ("dp", "row"))
    final_out, final_grad = (
        lax.all_to_all(
            jnp.concatenate(results, axis=0), "col", split_axis=0, concat_axis=1, tiled=True
        ),
        lax.all_to_all(
            jnp.concatenate(input_grads, axis=0), "col", split_axis=0, concat_axis=1, tiled=True
        ),
    )
    return (
        final_out,
        final_grad,
        gains[0],
        shards[0],
        shards[1],
        shards[2],
        gains[1],
        shards[3],
        shards[4],
        shards[5],
    )


def solution(mesh):
    placed = (
        P(("dp", "row", "col"), None),
        P(("dp", "row", "col"), None),
        P("dp", None),
        P("dp", None),
        P("col"),
        P("col", "row", "dp"),
        P("col", "row", "dp"),
        P("row", "dp", "col"),
        P("col"),
        P("col", ("dp", "row")),
        P("col", ("dp", "row")),
        P(("dp", "row"), "col"),
    )
    return jax.shard_map(
        body,
        mesh=mesh,
        in_specs=placed,
        out_specs=(
            P(("dp", "row", "col"), None),
            P(("dp", "row", "col"), None),
            P("col"),
            P("col", "row", "dp"),
            P("col", "row", "dp"),
            P("row", "dp", "col"),
            P("col"),
            P("col", ("dp", "row")),
            P("col", ("dp", "row")),
            P(("dp", "row"), "col"),
        ),
        check_vma=False,
    )
```

profile of v0, /device:TPU:0, one launch (start us, length us, event | category | flops | bytes accessed | tf_op | source)
XLA Modules:
  0.0 1026.6 jit_solution(1418643032406255039)
XLA Ops:
  14.4 33.4 %all_gather.91 = bf16[640,10,64]{0,2,1:T(8,128)(2,1)S(1)} all-gather(bf16[640,10,8]{0,2,1:T(8,128)(2,1)} %param.21), channel_id=1, replica_groups=mesh['dp'=8,'row'=2,'col'=2] {'dp'}, dimensions={2}, use_global_device_ids=true | all-gather | bytes 921600 | tf_op jit(solution)/shard_map/all_gather | solution.py:110
  47.8 31.1 %all_gather.92 = bf16[640,1,320]{0,2,1:T(8,128)(2,1)S(1)} all-gather(bf16[640,1,40]{0,2,1:T(8,128)(2,1)S(1)} %copy-done.73), channel_id=1, replica_groups=mesh['dp'=8,'row'=2,'col'=2] {'dp'}, dimensions={2}, use_global_device_ids=true | all-gather | bytes 460800 | tf_op jit(solution)/shard_map/all_gather | solution.py:111
  79.1 5.0 all-reduce.5
  103.0 33.2 %all_gather.95 = bf16[10,64,640]{2,1,0:T(8,128)(2,1)S(1)} all-gather(bf16[10,8,640]{2,1,0:T(8,128)(2,1)S(1)} %copy-done.71), channel_id=1, replica_groups=mesh['dp'=8,'row'=2,'col'=2] {'dp'}, dimensions={1}, use_global_device_ids=true | all-gather | bytes 921600 | tf_op jit(solution)/shard_map/all_gather | solution.py:112
  146.2 7.5 all_gather.94
  157.4 6.4 all_gather.103
  167.6 8.2 all_to_all.70
  192.3 29.0 %all-gather.10.cloned.1.call-done = bf16[640,1792]{0,1:T(8,128)(2,1)} async-done(((bf16[640,224]{0,1:T(8,128)(2,1)}), bf16[640,1792]{0,1:T(8,128)(2,1)}) %all-gather.10.cloned.1.call-update) | async-done | bytes 2293776 | tf_op jit(solution)/shard_map/all_gather | solution.py:114
  223.9 49.4 %all-gather.8.cloned.1.call-done = bf16[640,1792]{0,1:T(8,128)(2,1)} async-done(((bf16[640,224]{0,1:T(8,128)(2,1)}), bf16[640,1792]{0,1:T(8,128)(2,1)}) %all-gather.8.cloned.1.call-update) | async-done | bytes 2293776 | tf_op jit(solution)/shard_map/all_gather | solution.py:113
  278.5 47.4 %reduce-scatter.36.cloned.1.call-done = f32[128,3584]{1,0:T(8,128)} async-done(((f32[256,3584]{1,0:T(8,128)}), f32[128,3584]{1,0:T(8,128)}) %reduce-scatter.36.cloned.1.call-update) | async-done | bytes 1835024 | tf_op jit(solution)/shard_map/reduce_scatter | solution.py:99
  330.1 30.3 %all-gather.14.cloned.1.call-done = bf16[256,3584]{1,0:T(8,128)(2,1)} async-done(((bf16[128,3584]{1,0:T(8,128)(2,1)}), bf16[256,3584]{1,0:T(8,128)(2,1)}) %all-gather.14.cloned.1.call-update) | async-done | bytes 1835024 | tf_op jit(solution)/shard_map/all_gather | solution.py:96
  382.2 23.6 %reduce-scatter.58.cloned.1.call-done = f32[128,1792]{1,0:T(8,128)} async-done(((f32[256,1792]{1,0:T(8,128)}), f32[128,1792]{1,0:T(8,128)}) %reduce-scatter.58.cloned.1.call-update) | async-done | bytes 917520 | tf_op jit(solution)/shard_map/reduce_scatter | solution.py:99
  405.8 51.2 %reduce-scatter.44.cloned.1.call-done = f32[128,3584]{1,0:T(8,128)} async-done(((f32[256,3584]{1,0:T(8,128)}), f32[128,3584]{1,0:T(8,128)}) %reduce-scatter.44.cloned.1.call-update) | async-done | bytes 1835024 | tf_op jit(solution)/shard_map/reduce_scatter | solution.py:99
  461.2 30.3 %all-gather.16.cloned.1.call-done = bf16[256,3584]{1,0:T(8,128)(2,1)} async-done(((bf16[128,3584]{1,0:T(8,128)(2,1)}), bf16[256,3584]{1,0:T(8,128)(2,1)}) %all-gather.16.cloned.1.call-update) | async-done | bytes 1835024 | tf_op jit(solution)/shard_map/all_gather | solution.py:96
  496.2 13.1 %all_gather.105 = bf16[256,1792]{1,0:T(8,128)(2,1)S(1)} all-gather(bf16[128,1792]{1,0:T(8,128)(2,1)} %get-tuple-element.129), channel_id=1, replica_groups=mesh['dp'=8,'row'=2,'col'=2] {'col'}, dimensions={0}, use_global_device_ids=true | all-gather | bytes 1376256 | tf_op jit(solution)/shard_map/all_gather | solution.py:96
  514.2 4.9 all-reduce.3
  526.8 19.3 %all_gather.99 = bf16[256,1792]{1,0:T(8,128)(2,1)S(1)} all-gather(bf16[128,1792]{1,0:T(8,128)(2,1)} %get-tuple-element.128), channel_id=1, replica_groups=mesh['dp'=8,'row'=2,'col'=2] {'col'}, dimensions={0}, use_global_device_ids=true | all-gather | bytes 1376256 | tf_op jit(solution)/shard_map/all_gather | solution.py:96
  558.1 9.3 reduce-scatter.64.cloned.1.call-start
  583.5 8.9 all_gather.109
  597.6 8.0 all_gather.113
  627.9 35.0 %reduce-scatter.72.cloned.1.call-done = bf16[224,640]{1,0:T(8,128)(2,1)} async-done(((bf16[1792,640]{1,0:T(8,128)(2,1)}), bf16[224,640]{1,0:T(8,128)(2,1)}) %reduce-scatter.72.cloned.1.call-update) | async-done | bytes 286736 | tf_op jit(solution)/shard_map/reduce_scatter | solution.py:439
  664.8 58.1 %reduce-scatter.76.cloned.1.call-done = bf16[8,6400]{1,0:T(8,128)(2,1)} async-done(((bf16[64,6400]{1,0:T(8,128)(2,1)}), bf16[8,6400]{1,0:T(8,128)(2,1)}) %reduce-scatter.76.cloned.1.call-update) | async-done | bytes 102416
  723.8 8.3 reduce-scatter.56.cloned.1.call-done
  732.1 11.6 %reduce-scatter.66.cloned.1.call-done = f32[128,640]{1,0:T(8,128)} async-done(((f32[256,640]{1,0:T(8,128)}), f32[128,640]{1,0:T(8,128)}) %reduce-scatter.66.cloned.1.call-update) | async-done | bytes 327696 | tf_op jit(solution)/shard_map/reduce_scatter | solution.py:104
  745.1 4.9 all-reduce.2
  750.0 5.2 reduce-scatter.38.cloned.1.call-done
  761.9 5.5 all-to-all-done.1
  771.6 43.1 %reduce-scatter.78.cloned.1.call-done = bf16[640,1,40]{0,2,1:T(8,128)(2,1)} async-done(((bf16[640,1,320]{0,2,1:T(8,128)(2,1)}), bf16[640,1,40]{0,2,1:T(8,128)(2,1)}) %reduce-scatter.78.cloned.1.call-update) | async-done | bytes 51216
  816.2 30.8 %all-reduce.1 = (f32[640]{0:T(1024)}, f32[640]{0:T(1024)}) all-reduce(f32[640]{0:T(1024)S(1)} %add.279, f32[640]{0:T(1024)S(1)} %add.283), channel_id=1, replica_groups=mesh['dp'=8,'row'=2,'col'=2] {'dp','row'}, use_global_device_ids=true, to_apply=%region_52.53 | all-reduce | flops 1280 | bytes 10240 | tf_op jit(solution)/shard_map/psum | solution.py:443
  848.5 26.1 %reduce-scatter.74.cloned.1.call-done = bf16[8,6400]{1,0:T(8,128)(2,1)} async-done(((bf16[64,6400]{1,0:T(8,128)(2,1)}), bf16[8,6400]{1,0:T(8,128)(2,1)}) %reduce-scatter.74.cloned.1.call-update) | async-done | bytes 102416
  875.5 70.5 %reduce-scatter.68.cloned.1.call-done = bf16[640,224]{0,1:T(8,128)(2,1)} async-done(((bf16[640,1792]{0,1:T(8,128)(2,1)}), bf16[640,224]{0,1:T(8,128)(2,1)}) %reduce-scatter.68.cloned.1.call-update) | async-done | bytes 286736 | tf_op jit(solution)/shard_map/reduce_scatter | solution.py:433
  948.6 68.7 %reduce-scatter.70.cloned.1.call-done = bf16[640,224]{0,1:T(8,128)(2,1)} async-done(((bf16[640,1792]{0,1:T(8,128)(2,1)}), bf16[640,224]{0,1:T(8,128)(2,1)}) %reduce-scatter.70.cloned.1.call-update) | async-done | bytes 286736 | tf_op jit(solution)/shard_map/reduce_scatter | solution.py:436
  (505 shorter events, 197.1 us)
Async XLA Ops:
  10.1 68.8 %all-to-all-start = ((bf16[128,2,640]{2,0,1:T(8,128)(2,1)}), bf16[128,2,640]{2,0,1:T(8,128)(2,1)S(1)}, u32[]{:S(2)}, u32[]{:S(2)}) async-start(bf16[128,2,640]{2,0,1:T(8,128)(2,1)} %copy.110), calls=%async_computation | async-start | bytes 655360 | tf_op jit(solution)/shard_map/all_to_all | solution.py:85
  14.4 121.8 %reduce-scatter.32.cloned.1.call-start = ((), (), s32[]{:S(2)}) async-start(), calls=%async_computation.28 | async-start | bytes 1572864 | tf_op jit(solution)/shard_map/reduce_scatter | solution.py:99
  89.2 49.2 %reduce-scatter.40.cloned.1.call-start = ((), (), s32[]{:S(2)}) async-start(), calls=%async_computation.35 | async-start | bytes 1572864 | tf_op jit(solution)/shard_map/reduce_scatter | solution.py:99
  93.7 85.6 %all-gather.12.cloned.1.call-start = ((), (), s32[]{:S(2)}) async-start(), calls=%async_computation.33 | async-start | bytes 2580480 | tf_op jit(solution)/shard_map/all_gather | solution.py:115
  94.3 89.1 %reduce-scatter.34.cloned.1.call-start = ((), (), s32[]{:S(2)}) async-start(), calls=%async_computation.29 | async-start | bytes 983040 | tf_op jit(solution)/shard_map/reduce_scatter | solution.py:104
  155.8 27.6 %reduce-scatter.42.cloned.1.call-start = ((), (), s32[]{:S(2)}) async-start(), calls=%async_computation.36 | async-start | bytes 983040 | tf_op jit(solution)/shard_map/reduce_scatter | solution.py:104
  166.0 55.3 %all-gather.10.cloned.1.call-start = ((), (), s32[]{:S(2)}) async-start(), calls=%async_computation.31 | async-start | bytes 2580480 | tf_op jit(solution)/shard_map/all_gather | solution.py:114
  166.6 106.7 %all-gather.8.cloned.1.call-start = ((), (), s32[]{:S(2)}) async-start(), calls=%async_computation.30 | async-start | bytes 2580480 | tf_op jit(solution)/shard_map/all_gather | solution.py:113
  167.1 111.3 %reduce-scatter.48.cloned.1.call-start = ((), (), s32[]{:S(2)}) async-start(), calls=%async_computation.39 | async-start | bytes 2752512 | tf_op jit(solution)/shard_map/reduce_scatter | solution.py:99
  183.3 142.7 %reduce-scatter.36.cloned.1.call-start = ((), (), s32[]{:S(2)}) async-start(), calls=%async_computation.32 | async-start | bytes 5505024 | tf_op jit(solution)/shard_map/reduce_scatter | solution.py:99
  278.2 82.2 %all-gather.14.cloned.1.call-start = ((), (), s32[]{:S(2)}) async-start(), calls=%async_computation.40 | async-start | bytes 2752512 | tf_op jit(solution)/shard_map/all_gather | solution.py:96
  330.0 43.3 %reduce-scatter.50.cloned.1.call-start = ((), (), s32[]{:S(2)}) async-start(), calls=%async_computation.41 | async-start | bytes 983040 | tf_op jit(solution)/shard_map/reduce_scatter | solution.py:104
  365.1 40.7 %reduce-scatter.58.cloned.1.call-start = ((), (), s32[]{:S(2)}) async-start(), calls=%async_computation.45 | async-start | bytes 2752512 | tf_op jit(solution)/shard_map/reduce_scatter | solution.py:99
  371.9 85.1 %reduce-scatter.44.cloned.1.call-start = ((), (), s32[]{:S(2)}) async-start(), calls=%async_computation.37 | async-start | bytes 5505024 | tf_op jit(solution)/shard_map/reduce_scatter | solution.py:99
  382.2 109.3 %all-gather.16.cloned.1.call-start = ((), (), s32[]{:S(2)}) async-start(), calls=%async_computation.46 | async-start | bytes 2752512 | tf_op jit(solution)/shard_map/all_gather | solution.py:96
  461.1 51.9 %reduce-scatter.60.cloned.1.call-start = ((), (), s32[]{:S(2)}) async-start(), calls=%async_computation.47 | async-start | bytes 983040 | tf_op jit(solution)/shard_map/reduce_scatter | solution.py:104
  496.2 25.0 %reduce-scatter.46.cloned.1.call-start = ((), (), s32[]{:S(2)}) async-start(), calls=%async_computation.38 | async-start | bytes 983040 | tf_op jit(solution)/shard_map/reduce_scatter | solution.py:104
  512.9 41.4 %reduce-scatter.52.cloned.1.call-start = ((), (), s32[]{:S(2)}) async-start(), calls=%async_computation.42 | async-start | bytes 983040 | tf_op jit(solution)/shard_map/reduce_scatter | solution.py:99
  526.8 41.1 %reduce-scatter.62.cloned.1.call-start = ((), (), s32[]{:S(2)}) async-start(), calls=%async_computation.48 | async-start | bytes 983040 | tf_op jit(solution)/shard_map/reduce_scatter | solution.py:99
  550.2 31.4 %reduce-scatter.54.cloned.1.call-start = ((), (), s32[]{:S(2)}) async-start(), calls=%async_computation.43 | async-start | bytes 245760 | tf_op jit(solution)/shard_map/reduce_scatter | solution.py:366
  558.1 36.5 %reduce-scatter.64.cloned.1.call-start = ((), (), s32[]{:S(2)}) async-start(), calls=%async_computation.49 | async-start | bytes 245760 | tf_op jit(solution)/shard_map/reduce_scatter | solution.py:366
  573.2 89.7 %reduce-scatter.72.cloned.1.call-start = ((), (), s32[]{:S(2)}) async-start(), calls=%async_computation.53 | async-start | bytes 2580480 | tf_op jit(solution)/shard_map/reduce_scatter | solution.py:439
  578.0 144.9 %reduce-scatter.76.cloned.1.call-start = ((), (), s32[]{:S(2)}) async-start(), calls=%async_computation.55 | async-start | bytes 921600
  580.9 151.2 %reduce-scatter.56.cloned.1.call-start = ((), (), s32[]{:S(2)}) async-start(), calls=%async_computation.44 | async-start | bytes 983040 | tf_op jit(solution)/shard_map/reduce_scatter | solution.py:104
  593.9 149.8 %reduce-scatter.66.cloned.1.call-start = ((), (), s32[]{:S(2)}) async-start(), calls=%async_computation.50 | async-start | bytes 983040 | tf_op jit(solution)/shard_map/reduce_scatter | solution.py:104
  608.9 146.4 %reduce-scatter.38.cloned.1.call-start = ((), (), s32[]{:S(2)}) async-start(), calls=%async_computation.34 | async-start | bytes 983040 | tf_op jit(solution)/shard_map/reduce_scatter | solution.py:104
  611.9 202.8 %reduce-scatter.78.cloned.1.call-start = ((), (), s32[]{:S(2)}) async-start(), calls=%async_computation.56 | async-start | bytes 460800
  615.2 259.4 %reduce-scatter.74.cloned.1.call-start = ((), (), s32[]{:S(2)}) async-start(), calls=%async_computation.54 | async-start | bytes 921600
  619.1 326.9 %reduce-scatter.68.cloned.1.call-start = ((), (), s32[]{:S(2)}) async-start(), calls=%async_computation.51 | async-start | bytes 2580480 | tf_op jit(solution)/shard_map/reduce_scatter | solution.py:433
  623.8 393.4 %reduce-scatter.70.cloned.1.call-start = ((), (), s32[]{:S(2)}) async-start(), calls=%async_computation.52 | async-start | bytes 2580480 | tf_op jit(solution)/shard_map/reduce_scatter | solution.py:436
  757.4 10.1 all-to-all-start.1
  767.4 80.3 %all-to-all-start.3 = ((bf16[2,128,640]{2,1,0:T(8,128)(2,1)}), bf16[2,128,640]{2,1,0:T(8,128)(2,1)S(1)}, u32[]{:S(2)}, u32[]{:S(2)}) async-start(bf16[2,128,640]{2,1,0:T(8,128)(2,1)} %bitcast.79), calls=%async_computation.21 | async-start | bytes 655360 | tf_op jit(solution)/shard_map/all_to_all | solution.py:448
  (99 other events, 2675.5 us)
Sparse Core Ops, SparseCore 0:
  89.4 21.7 reduce-scatter.31
  113.5 20.4 reduce-scatter.39
  155.9 9.6 reduce-scatter.33
  167.7 9.2 reduce-scatter.41
  183.4 29.2 reduce-scatter.47
  278.3 47.6 reduce-scatter.35
  330.1 30.1 all-gather.13
  365.2 8.0 reduce-scatter.49
  375.7 30.1 reduce-scatter.57
  407.9 49.0 reduce-scatter.43
  461.2 30.1 all-gather.15
  496.3 8.0 reduce-scatter.59
  513.1 8.0 reduce-scatter.45
  526.9 21.5 reduce-scatter.51
  550.6 17.2 reduce-scatter.61
  570.7 7.5 reduce-scatter.53
  580.4 8.6 reduce-scatter.63
  592.9 69.9 reduce-scatter.71
  666.6 56.1 reduce-scatter.75
  724.9 7.1 reduce-scatter.55
  734.5 9.2 reduce-scatter.65
  746.0 9.2 reduce-scatter.37
  759.5 55.1 reduce-scatter.77
  818.3 56.2 reduce-scatter.73
  878.1 67.9 reduce-scatter.67
  949.4 67.7 reduce-scatter.69
Sparse Core Ops, SparseCore 1:
  96.3 57.3 all-gather.11
  168.9 52.4 all-gather.9
  223.6 49.6 all-gather.7
where the time goes:
time: 1040 us; the launch traced here: 1030 us
  waiting for transfers between devices  599 us (58%)
  blocking collectives  240 us (23%)
  matrix products  75.1 us (7%)
  other arithmetic  46.9 us (5%)
  local copies, waits for them, and re-layouts  25.6 us (2%)
  starting transfers between devices  21.9 us (2%)
  between operations  17.6 us (2%)
    unnamed x32, waiting for transfers between devices  129 us
    reduce_scatter x8, waiting for transfers between devices, col_reduce(): lax.psum_scatter(term(jnp.int32(0), rows * lax.axis_size('col')), 'col',...  123 us
    reduce_scatter x1, waiting for transfers between devices, body(): lax.psum_scatter(gradients[5].astype(jnp.bfloat16), 'dp', scatter_dimensi...  70.5 us
    reduce_scatter x1, waiting for transfers between devices, body(): lax.psum_scatter(gradients[6].astype(jnp.bfloat16), 'dp', scatter_dimensi...  68.7 us
    all_gather x6, blocking collectives, gather_cols(): return lax.all_gather(value_rows, 'col', axis=0, tiled=True)  63.2 us
    all_gather x2, waiting for transfers between devices, gather_cols(): return lax.all_gather(value_rows, 'col', axis=0, tiled=True)  60.5 us
    all_gather x1, waiting for transfers between devices, fetch(): lax.all_gather(w_gate, 'dp', axis=1, tiled=True)  49.4 us
    reduce_scatter x1, waiting for transfers between devices, body(): lax.psum_scatter(gradients[7].astype(jnp.bfloat16), 'dp', scatter_dimensi...  35 us
  transfers between devices with their start and end apart: 32, of which 20 were waited for; matrix products, arithmetic and copies ran while one was open for 11% of the time, Pallas kernels for 0%

commit v1 on v0

--- a/solution.py
+++ b/solution.py
@@ -1,8 +1,11 @@
+import functools
 import math
 
 import jax
 import jax.numpy as jnp
 from jax import lax
+from jax.experimental import pallas as pl
+from jax.experimental.pallas import tpu as pltpu
 from jax.sharding import PartitionSpec as P
 
 MODEL_WIDTH = 1280
@@ -11,36 +14,584 @@
 HEAD_SIZE = 64
 TREE_TOKENS = 128
 SEGS = 13
-MICRO = 2
-
+PLANES = 4
 
 EPS = 1e-05
 THETA = 10000.0
-HIGH = lax.Precision.HIGHEST
-
-
-def tree_layout(segment, parent):
+MESH = pl.DeviceIdType.MESH
+F32 = jnp.float32
+BF16 = jnp.bfloat16
+
+
+class Layout:
+    def __init__(self, shape):
+        self.planes = PLANES
+        self.lines = shape["dp"] // PLANES
+        self.cores = shape["row"]
+        self.cols = shape["col"]
+        self.dp = shape["dp"]
+        self.width = MODEL_WIDTH // self.cols
+        self.qrows = QUERY_HEADS // self.cores * (HEAD_SIZE // self.dp)
+        self.kvrows = KEY_VALUE_HEADS * HEAD_SIZE // self.dp
+        self.kv_at = self.qrows
+        self.out_at = -(-(self.kv_at + self.kvrows) // 16) * 16
+        self.arows = -(-(self.out_at + self.qrows) // 16) * 16
+
+    def fits(self):
+        return self.width % 128 == 0 and self.qrows % 16 == 0 and self.cores == 2 and self.dp % PLANES == 0
+
+    def here(self):
+        dp = lax.axis_index("dp")
+        return dp // self.lines, lax.rem(dp, self.lines), lax.axis_index("row"), lax.axis_index("col")
+
+    def device(self, z, x, r, c):
+        return (z * self.lines + x, r, c)
+
+    def plane_offsets(self):
+        return [(dx, dc) for dx in range(self.lines) for dc in range(self.cols) if dx or dc]
+
+
+def greet(lay, peers):
+    barrier = pltpu.get_barrier_semaphore()
+    for peer in peers:
+        pl.semaphore_signal(barrier, inc=1, device_id=peer, device_id_type=MESH)
+    pl.semaphore_wait(barrier, len(peers))
+
+
+def neighbours(lay):
+    z, x, r, c = lay.here()
+    peers = [lay.device(lax.rem(z + k, lay.planes), x, r, c) for k in range(1, lay.planes)]
+    for dx, dc in lay.plane_offsets():
+        peers.append(lay.device(z, lax.rem(x + dx, lay.lines), r, lax.rem(c + dc, lay.cols)))
+    peers.append(lay.device(z, x, 1 - r, c))
+    return peers
+
+
+def send(src, dst, sems, slot, peer):
+    copy = pltpu.make_async_remote_copy(
+        src_ref=src,
+        dst_ref=dst,
+        send_sem=sems[0].at[slot],
+        recv_sem=sems[1].at[slot],
+        device_id=peer,
+        device_id_type=MESH,
+    )
+    copy.start()
+    return copy
+
+
+def gather_kernel(lay, a_ref, f_ref, dy_ref, ga, gf, gdy, own, az_s, az_r, ap_s, ap_r, ac_s, ac_r, fp_s, fp_r, fc_s, fc_r, dz_s, dz_r):
+    z, x, r, c = lay.here()
+    W = lay.width
+    n_off = len(lay.plane_offsets())
+    greet(lay, neighbours(lay))
+    span = pl.ds(pl.multiple_of(c * W, 128), W)
+    frows = f_ref.shape[1]
+
+    def a_at(zz):
+        return ga.at[zz * lay.lines + x, r, :, span]
+
+    def f_at(xx):
+        return gf.at[:, pl.ds(pl.multiple_of((xx * lay.cores + r) * frows, 16), frows), :]
+
+    f_own = gf.at[:, pl.ds(pl.multiple_of((x * lay.cores + r) * frows, 16), frows), span]
+    locals_ = [
+        pltpu.make_async_copy(a_ref, a_at(z), own.at[0]),
+        pltpu.make_async_copy(f_ref, f_own, own.at[1]),
+        pltpu.make_async_copy(dy_ref, gdy.at[0], own.at[2]),
+    ]
+    for copy in locals_:
+        copy.start()
+    az = []
+    for k in range(1, lay.planes):
+        peer = lay.device(lax.rem(z + k, lay.planes), x, r, c)
+        az.append(send(a_ref, a_at(z), (az_s, az_r), k - 1, peer))
+    ap = {}
+    for k in range(lay.planes):
+        zz = lax.rem(z + lay.planes - k, lay.planes)
+        if k:
+            az[k - 1].wait_recv()
+        for j, (dx, dc) in enumerate(lay.plane_offsets()):
+            peer = lay.device(z, lax.rem(x + dx, lay.lines), r, lax.rem(c + dc, lay.cols))
+            src = a_ref if k == 0 else a_at(zz)
+            ap[k, j] = send(src, a_at(zz), (ap_s, ap_r), k * n_off + j, peer)
+        if k == 0:
+            fp = []
+            for j, (dx, dc) in enumerate(lay.plane_offsets()):
+                peer = lay.device(z, lax.rem(x + dx, lay.lines), r, lax.rem(c + dc, lay.cols))
+                fp.append(send(f_ref, f_own, (fp_s, fp_r), j, peer))
+            dz = []
+            for q in range(1, lay.planes):
+                peer = lay.device(lax.rem(z + q, lay.planes), x, r, c)
+                dz.append(send(dy_ref, gdy.at[q], (dz_s, dz_r), q - 1, peer))
+    for copy in locals_:
+        copy.wait()
+    sibling = lay.device(z, x, 1 - r, c)
+    last = []
+    for k in range(lay.planes):
+        zz = lax.rem(z + lay.planes - k, lay.planes)
+        for j in range(n_off):
+            ap[k, j].wait_recv()
+        for dx in range(lay.lines):
+            block = ga.at[zz * lay.lines + lax.rem(x + dx, lay.lines), r]
+            last.append(send(block, block, (ac_s, ac_r), k * lay.lines + dx, sibling))
+    for j in range(n_off):
+        fp[j].wait_recv()
+    for dx in range(lay.lines):
+        block = f_at(lax.rem(x + dx, lay.lines))
+        last.append(send(block, block, (fc_s, fc_r), dx, sibling))
+    for copy in last:
+        copy.wait()
+    for copy in dz:
+        copy.wait()
+    for copy in az + fp + list(ap.values()):
+        copy.wait_send()
+
+
+def gather_weights(lay, a_shard, f_shard, dy):
+    n_off = len(lay.plane_offsets())
+    dma = lambda n: pltpu.SemaphoreType.DMA((n,))
+    np_, nx = lay.planes, lay.lines
+    counts = [np_ - 1, np_ * n_off, np_ * nx, n_off, nx, np_ - 1]
+    scratch = [dma(3)]
+    for n in counts:
+        scratch += [dma(n), dma(n)]
+    frows = f_shard.shape[1]
+    hbm = pl.BlockSpec(memory_space=pl.ANY)
+    return pl.pallas_call(
+        functools.partial(gather_kernel, lay),
+        out_shape=(
+            jax.ShapeDtypeStruct((lay.dp, lay.cores, lay.arows, MODEL_WIDTH), BF16),
+            jax.ShapeDtypeStruct((3, nx * lay.cores * frows, MODEL_WIDTH), BF16),
+            jax.ShapeDtypeStruct((np_,) + dy.shape, BF16),
+        ),
+        in_specs=[hbm] * 3,
+        out_specs=(hbm,) * 3,
+        scratch_shapes=scratch,
+        compiler_params=pltpu.CompilerParams(collective_id=0, has_side_effects=True),
+        name="gather_weights",
+    )(a_shard, f_shard, dy)
+
+
+def tokens_kernel(lay, n_ref, gn, own, s_s, s_r):
+    z, x, r, c = lay.here()
+    greet(lay, [lay.device(lax.rem(z + k, lay.planes), x, r, c) for k in range(1, lay.planes)])
+    copies = []
+    for k in range(1, lay.planes):
+        peer = lay.device(lax.rem(z + k, lay.planes), x, r, c)
+        copies.append(send(n_ref, gn.at[k], (s_s, s_r), k - 1, peer))
+    mine = pltpu.make_async_copy(n_ref, gn.at[0], own.at[0])
+    mine.start()
+    mine.wait()
+    for copy in copies:
+        copy.wait()
+
+
+def gather_tokens(lay, rows):
+    hbm = pl.BlockSpec(memory_space=pl.ANY)
+    dma = lambda n: pltpu.SemaphoreType.DMA((n,))
+    n = lay.planes - 1
+    return pl.pallas_call(
+        functools.partial(tokens_kernel, lay),
+        out_shape=jax.ShapeDtypeStruct((lay.planes,) + rows.shape, BF16),
+        in_specs=[hbm],
+        out_specs=hbm,
+        scratch_shapes=[dma(1), dma(n), dma(n)],
+        compiler_params=pltpu.CompilerParams(collective_id=1, has_side_effects=True),
+        name="gather_tokens",
+    )(rows)
+
+
+def add_rows(total, step, left, right, dest):
+    def some(i, _):
+        rows = pl.ds(pl.multiple_of(i * step, step), step)
+        dest[rows, :] = (left[rows, :].astype(F32) + right[rows, :].astype(F32)).astype(dest.dtype)
+        return 0
+
+    lax.fori_loop(0, total // step, some, 0)
+
+
+def sum_rows(total, step, parts, dest):
+    def some(i, _):
+        rows = pl.ds(pl.multiple_of(i * step, step), step)
+        acc = parts[0][rows, :].astype(F32)
+        for part in parts[1:]:
+            acc = acc + part[rows, :].astype(F32)
+        dest[rows, :] = acc.astype(dest.dtype)
+        return 0
+
+    lax.fori_loop(0, total // step, some, 0)
+
+
+def feed_grads_kernel(lay, g_ref, d_ref, out_ref, do_ref, core_in, mixed, plane_in, d_in, cs, cr, ps, pr, zs, zr):
+    z, x, r, c = lay.here()
+    W = lay.width
+    offs = lay.plane_offsets()
+    frows = out_ref.shape[1]
+    greet(lay, neighbours(lay))
+    sibling = lay.device(z, x, 1 - r, c)
+
+    def rows_of(xx, rr):
+        return pl.ds(pl.multiple_of((xx * lay.cores + rr) * frows, 16), frows)
+
+    def lanes(cc):
+        return pl.ds(pl.multiple_of(cc * W, 128), W)
+
+    core = []
+    order = [(dx + 1) % lay.lines for dx in range(lay.lines)]
+    for i, dx in enumerate(order):
+        xx = lax.rem(x + dx, lay.lines)
+        core.append(send(g_ref.at[:, rows_of(xx, 1 - r), :], core_in.at[i], (cs, cr), i, sibling))
+    dz = []
+    for k in range(1, lay.planes):
+        peer = lay.device(lax.rem(z + lay.planes - k, lay.planes), x, r, c)
+        dz.append(send(d_ref.at[k], d_in.at[k - 1], (zs, zr), k - 1, peer))
+    plane = {}
+    for i, dx in enumerate(order):
+        xx = lax.rem(x + dx, lay.lines)
+        core[i].wait_recv()
+        for w in range(3):
+            add_rows(frows, 32, g_ref.at[w, rows_of(xx, r), :], core_in.at[i, w], mixed.at[i, w])
+        for dc in range(lay.cols):
+            if dx or dc:
+                cc = lax.rem(c + dc, lay.cols)
+                j = offs.index((dx, dc))
+                peer = lay.device(z, xx, r, cc)
+                plane[j] = send(mixed.at[i, :, :, lanes(cc)], plane_in.at[j], (ps, pr), j, peer)
+    for copy in dz:
+        copy.wait_recv()
+    sum_rows(d_ref.shape[1], 16, [d_ref.at[0]] + [d_in.at[k] for k in range(lay.planes - 1)], do_ref)
+    for j in range(len(offs)):
+        plane[j].wait_recv()
+    mine = order.index(0)
+    for w in range(3):
+        sum_rows(frows, 32, [mixed.at[mine, w, :, lanes(c)]] + [plane_in.at[j, w] for j in range(len(offs))], out_ref.at[w])
+    for copy in core + dz + list(plane.values()):
+        copy.wait_send()
+
+
+def reduce_feed(lay, grads, d_rows):
+    frows = grads.shape[1] // (lay.lines * lay.cores)
+    n_off = len(lay.plane_offsets())
+    dma = lambda n: pltpu.SemaphoreType.DMA((n,))
+    vmem = pl.BlockSpec(memory_space=pltpu.VMEM)
+    sems = []
+    for n in (lay.lines, n_off, lay.planes - 1):
+        sems += [dma(n), dma(n)]
+    return pl.pallas_call(
+        functools.partial(feed_grads_kernel, lay),
+        out_shape=(
+            jax.ShapeDtypeStruct((3, frows, lay.width), F32),
+            jax.ShapeDtypeStruct(d_rows.shape[1:], F32),
+        ),
+        in_specs=[vmem] * 2,
+        out_specs=(vmem,) * 2,
+        scratch_shapes=[
+            pltpu.VMEM((lay.lines, 3, frows, MODEL_WIDTH), BF16),
+            pltpu.VMEM((lay.lines, 3, frows, MODEL_WIDTH), BF16),
+            pltpu.VMEM((n_off, 3, frows, lay.width), BF16),
+            pltpu.VMEM((lay.planes - 1,) + d_rows.shape[1:], BF16),
+        ]
+        + sems,
+        compiler_params=pltpu.CompilerParams(collective_id=2, has_side_effects=True, vmem_limit_bytes=56 * 2**20),
+        name="reduce_feed",
+    )(grads, d_rows)
+
+
+def attn_grads_kernel(lay, g_ref, d_ref, n_ref, out_ref, do_ref, gain_ref, core_in, mixed, plane_in, line, z_in, d_in, nbuf, nin, cs, cr, ps, pr, zs, zr, ds_, dr, gs, gr):
+    z, x, r, c = lay.here()
+    W = lay.width
+    offs = lay.plane_offsets()
+    n_off = len(offs)
+    greet(lay, neighbours(lay))
+    sibling = lay.device(z, x, 1 - r, c)
+
+    def lanes(cc):
+        return pl.ds(pl.multiple_of(cc * W, 128), W)
+
+    core = {}
+    for k in list(range(1, lay.planes)) + [0]:
+        zz = lax.rem(z + k, lay.planes)
+        for dx in range(lay.lines):
+            i = k * lay.lines + dx
+            block = g_ref.at[zz * lay.lines + lax.rem(x + dx, lay.lines), 1 - r]
+            core[i] = send(block, core_in.at[i], (cs, cr), i, sibling)
+    gain_core = send(n_ref, nin.at[0], (gs, gr), 0, sibling)
+    dz = []
+    for k in range(1, lay.planes):
+        peer = lay.device(lax.rem(z + lay.planes - k, lay.planes), x, r, c)
+        dz.append(send(d_ref.at[k], d_in.at[k - 1], (ds_, dr), k - 1, peer))
+    plane = {}
+    for k in list(range(1, lay.planes)) + [0]:
+        zz = lax.rem(z + k, lay.planes)
+        for dx in range(lay.lines):
+            i = k * lay.lines + dx
+            xx = lax.rem(x + dx, lay.lines)
+            core[i].wait_recv()
+            add_rows(lay.arows, 16, g_ref.at[zz * lay.lines + xx, r], core_in.at[i], mixed.at[i])
+            for dc in range(lay.cols):
+                if dx or dc:
+                    cc = lax.rem(c + dc, lay.cols)
+                    j = offs.index((dx, dc))
+                    plane[k, j] = send(mixed.at[i, :, lanes(cc)], plane_in.at[k * n_off + j], (ps, pr), k * n_off + j, lay.device(z, xx, r, cc))
+    gain_core.wait_recv()
+    nbuf[0] = n_ref[...] + nin[0]
+    gains = []
+    for j, (dx, dc) in enumerate(offs):
+        peer = lay.device(z, lax.rem(x + dx, lay.lines), r, lax.rem(c + dc, lay.cols))
+        gains.append(send(nbuf.at[0], nin.at[1 + j], (gs, gr), 1 + j, peer))
+    zsend = []
+    for k in list(range(1, lay.planes)) + [0]:
+        for j in range(n_off):
+            plane[k, j].wait_recv()
+        parts = [mixed.at[k * lay.lines, :, lanes(c)]] + [plane_in.at[k * n_off + j] for j in range(n_off)]
+        sum_rows(lay.arows, 16, parts, line.at[k])
+        if k:
+            peer = lay.device(lax.rem(z + k, lay.planes), x, r, c)
+            zsend.append(send(line.at[k], z_in.at[k - 1], (zs, zr), k - 1, peer))
+    for copy in gains:
+        copy.wait_recv()
+    total = nbuf[0]
+    for j in range(n_off):
+        total = total + nin[1 + j]
+    nbuf[1] = total
+    zgains = []
+    for k in range(1, lay.planes):
+        peer = lay.device(lax.rem(z + k, lay.planes), x, r, c)
+        zgains.append(send(nbuf.at[1], nin.at[n_off + k], (gs, gr), n_off + k, peer))
+    for copy in dz:
+        copy.wait_recv()
+    sum_rows(d_ref.shape[1], 16, [d_ref.at[0]] + [d_in.at[k] for k in range(lay.planes - 1)], do_ref)
+    for copy in zgains:
+        copy.wait_recv()
+    total = nbuf[1]
+    for k in range(1, lay.planes):
+        total = total + nin[n_off + k]
+    gain_ref[...] = total
+    for copy in zsend:
+        copy.wait_recv()
+    sum_rows(lay.arows, 16, [line.at[0]] + [z_in.at[k] for k in range(lay.planes - 1)], out_ref)
+    for copy in list(core.values()) + dz + list(plane.values()) + zsend + gains + zgains + [gain_core]:
+        copy.wait_send()
+
+
+def reduce_attn(lay, grads, d_rows, gains):
+    n_off = len(lay.plane_offsets())
+    dma = lambda n: pltpu.SemaphoreType.DMA((n,))
+    vmem = pl.BlockSpec(memory_space=pltpu.VMEM)
+    np_, nx = lay.planes, lay.lines
+    sems = []
+    for n in (np_ * nx, np_ * n_off, np_ - 1, np_ - 1, n_off + np_):
+        sems += [dma(n), dma(n)]
+    return pl.pallas_call(
+        functools.partial(attn_grads_kernel, lay),
+        out_shape=(
+            jax.ShapeDtypeStruct((lay.arows, lay.width), F32),
+            jax.ShapeDtypeStruct(d_rows.shape[1:], F32),
+            jax.ShapeDtypeStruct(gains.shape, F32),
+        ),
+        in_specs=[vmem] * 3,
+        out_specs=(vmem,) * 3,
+        scratch_shapes=[
+            pltpu.VMEM((np_ * nx, lay.arows, MODEL_WIDTH), BF16),
+            pltpu.VMEM((np_ * nx, lay.arows, MODEL_WIDTH), BF16),
+            pltpu.VMEM((np_ * n_off, lay.arows, lay.width), BF16),
+            pltpu.VMEM((np_, lay.arows, lay.width), BF16),
+            pltpu.VMEM((np_ - 1, lay.arows, lay.width), BF16),
+            pltpu.VMEM((np_ - 1,) + d_rows.shape[1:], BF16),
+            pltpu.VMEM((2,) + gains.shape, F32),
+            pltpu.VMEM((n_off + np_,) + gains.shape, F32),
+        ]
+        + sems,
+        compiler_params=pltpu.CompilerParams(collective_id=3, has_side_effects=True, vmem_limit_bytes=56 * 2**20),
+        name="reduce_attn",
+    )(grads, d_rows, gains)
+
+
+def dot_nt(left, right):
+    return lax.dot_general(left, right, (((1,), (1,)), ((), ())), preferred_element_type=F32)
+
+
+def dot_tn(left, right):
+    return lax.dot_general(left, right, (((0,), (0,)), ((), ())), preferred_element_type=F32)
+
+
+def dot_nn(left, right):
+    return jnp.dot(left, right, preferred_element_type=F32)
+
+
+def tree_masks(segment, parent):
+    labels = jnp.arange(parent.shape[0], dtype=jnp.int32)
+    above = jnp.sum(jnp.where(segment[:, None] == labels[None, :], parent[None, :], 0), axis=1)
+    places = jnp.arange(segment.shape[0], dtype=jnp.int32)
+    seen = (segment[None, :] == segment[:, None]) | (segment[None, :] == above[:, None]) | (segment[None, :] == 0)
+    allowed = seen & (places[:, None] >= places[None, :])
+    return allowed, jnp.sum(allowed.astype(F32), axis=1) - 1.0
+
+
+def rotate(rows, cosine, sine):
+    half = rows.shape[-1] // 2
+    first, second = rows[..., :half], rows[..., half:]
+    return jnp.concatenate([first * cosine - second * sine, second * cosine + first * sine], axis=-1)
+
+
+def body(lay, tokens, cotangent, seg_ids, parents, norm1_gain, w_query, key_value_weight, w_out, norm2_gain, w_gate, w_up, w_down):
+    W = lay.width
+    T = TREE_TOKENS
+    D = HEAD_SIZE
+    frows = w_down.shape[0]
+    hidden = lay.lines * lay.cores * frows
+    scale = D**-0.5
+    row, col = lax.axis_index("row"), lax.axis_index("col")
+    a_shard = jnp.concatenate(
+        [
+            jnp.transpose(w_query, (1, 2, 0)).reshape(lay.qrows, W),
+            jnp.transpose(key_value_weight[:, 0, :]),
+            jnp.zeros((lay.out_at - lay.kv_at - lay.kvrows, W), BF16),
+            w_out.reshape(lay.qrows, W),
+            jnp.zeros((lay.arows - lay.out_at - lay.qrows, W), BF16),
+        ],
+        axis=0,
+    )
+    f_shard = jnp.stack([w_gate.T, w_up.T, w_down], axis=0)
+    gains = lax.all_gather(jnp.stack([norm1_gain, norm2_gain]), "col", axis=1, tiled=True)
+    gain1, gain2 = gains[0], gains[1]
+    ga, gf, gdy = gather_weights(lay, a_shard, f_shard, cotangent)
+
+    def natural(part):
+        p = part.reshape(lay.dp, lay.cores, QUERY_HEADS // lay.cores, D // lay.dp, MODEL_WIDTH)
+        return jnp.transpose(p, (1, 2, 0, 3, 4)).reshape(QUERY_HEADS * D, MODEL_WIDTH)
+
+    def placed(grad):
+        p = grad.reshape(lay.cores, QUERY_HEADS // lay.cores, lay.dp, D // lay.dp, MODEL_WIDTH)
+        return jnp.transpose(p, (2, 0, 1, 3, 4)).reshape(lay.dp, lay.cores, lay.qrows, MODEL_WIDTH)
+
+    wq = natural(ga[:, :, : lay.qrows])
+    wo = natural(ga[:, :, lay.out_at : lay.out_at + lay.qrows])
+    wkv = jnp.transpose(ga[:, :, lay.kv_at : lay.kv_at + lay.kvrows], (1, 0, 2, 3)).reshape(2 * KEY_VALUE_HEADS * D, MODEL_WIDTH)
+
+    tree = row * lay.cols + col
+    segment = lax.dynamic_index_in_dim(seg_ids, tree, 0, keepdims=False)
+    parent = lax.dynamic_index_in_dim(parents, tree, 0, keepdims=False)
+    allowed, depth = tree_masks(segment, parent)
+    inverse = jnp.exp(jnp.arange(D // 2, dtype=F32) * (2.0 / D) * -math.log(THETA))
+    angle = depth[:, None] * inverse[None, :]
+    cosine, sine = jnp.cos(angle)[:, None, :], jnp.sin(angle)[:, None, :]
+
+    stream = tokens.astype(F32)
+    rstd1 = lax.rsqrt(jnp.mean(stream * stream, axis=1, keepdims=True) + EPS)
+    normed = (stream * rstd1 * gain1).astype(BF16)
+    query = rotate(dot_nt(normed, wq).reshape(T, QUERY_HEADS, D), cosine, sine).astype(BF16)
+    kv_pre = dot_nt(normed, wkv)
+    kvw = KEY_VALUE_HEADS * D
+    keys = rotate(kv_pre[:, :kvw].reshape(T, KEY_VALUE_HEADS, D), cosine, sine).astype(BF16)
+    values = kv_pre[:, kvw:].reshape(T, KEY_VALUE_HEADS, D).astype(BF16)
+    group = QUERY_HEADS // KEY_VALUE_HEADS
+    qg = query.reshape(T, KEY_VALUE_HEADS, group, D)
+    scores = jnp.einsum("qghd,kgd->ghqk", qg, keys, preferred_element_type=F32) * scale
+    masked = jnp.where(allowed, scores, -1e30)
+    top = jnp.max(masked, axis=-1, keepdims=True)
+    weight = jnp.exp(masked - top)
+    probs = weight / jnp.sum(weight, axis=-1, keepdims=True)
+    probs_low = probs.astype(BF16)
+    mixed = jnp.einsum("ghqk,kgd->qghd", probs_low, values, preferred_element_type=F32).astype(BF16)
+    mixed2 = mixed.reshape(T, QUERY_HEADS * D)
+    resid = stream + dot_nn(mixed2, wo)
+    rstd2 = lax.rsqrt(jnp.mean(resid * resid, axis=1, keepdims=True) + EPS)
+    normed2 = (resid * rstd2 * gain2).astype(BF16)
+
+    gn = gather_tokens(lay, normed2).reshape(lay.planes * T, MODEL_WIDTH)
+    dy = gdy.reshape(lay.planes * T, MODEL_WIDTH)
+    gate, up = dot_nt(gn, gf[0]), dot_nt(gn, gf[1])
+    sig = jax.nn.sigmoid(gate)
+    act = (gate * sig * up).astype(BF16)
+    down = dot_nn(act, gf[2]).astype(BF16)
+    d_act = dot_nt(dy, gf[2])
+    d_up = (d_act * gate * sig).astype(BF16)
+    d_gate = (d_act * up * sig * (1.0 + gate * (1.0 - sig))).astype(BF16)
+    f_grads = jnp.stack([dot_tn(d_gate, gn).astype(BF16), dot_tn(d_up, gn).astype(BF16), dot_tn(act, dy).astype(BF16)])
+    d_n2 = (dot_nn(d_gate, gf[0]) + dot_nn(d_up, gf[1])).astype(BF16)
+    f_out, d_normed2 = reduce_feed(lay, f_grads, d_n2.reshape(lay.planes, T, MODEL_WIDTH))
+
+    scaled2 = d_normed2 * gain2
+    gain2_grad = jnp.sum(d_normed2 * resid * rstd2, axis=0)
+    inner2 = jnp.sum(scaled2 * resid, axis=1, keepdims=True)
+    d_resid = cotangent.astype(F32) + rstd2 * scaled2 - resid * (rstd2 * rstd2 * rstd2 * inner2 / MODEL_WIDTH)
+    d_attn = d_resid.astype(BF16)
+    out_grad = dot_tn(mixed2, d_attn)
+    d_mixed = dot_nt(d_attn, wo).astype(BF16).reshape(T, KEY_VALUE_HEADS, group, D)
+    d_probs = jnp.einsum("qghd,kgd->ghqk", d_mixed, values, preferred_element_type=F32)
+    delta = jnp.sum(probs * d_probs, axis=-1, keepdims=True)
+    d_scores = (probs * (d_probs - delta)).astype(BF16)
+    d_query = jnp.einsum("ghqk,kgd->qghd", d_scores, keys, preferred_element_type=F32).reshape(T, QUERY_HEADS, D) * scale
+    d_keys = jnp.einsum("ghqk,qghd->kgd", d_scores, qg, preferred_element_type=F32) * scale
+    d_values = jnp.einsum("ghqk,qghd->kgd", probs_low, d_mixed, preferred_element_type=F32)
+    dq = rotate(d_query, cosine, -sine).reshape(T, QUERY_HEADS * D).astype(BF16)
+    dk = rotate(d_keys, cosine, -sine).reshape(T, kvw).astype(BF16)
+    dkv = jnp.concatenate([dk, d_values.reshape(T, kvw).astype(BF16)], axis=1)
+    q_grad = dot_tn(dq, normed).astype(BF16)
+    kv_grad = dot_tn(dkv, normed).astype(BF16)
+    kv_placed = jnp.transpose(kv_grad.reshape(lay.cores, lay.dp, lay.kvrows, MODEL_WIDTH), (1, 0, 2, 3))
+    a_grads = jnp.concatenate(
+        [
+            placed(q_grad),
+            kv_placed,
+            jnp.zeros((lay.dp, lay.cores, lay.out_at - lay.kv_at - lay.kvrows, MODEL_WIDTH), BF16),
+            placed(out_grad.astype(BF16)),
+            jnp.zeros((lay.dp, lay.cores, lay.arows - lay.out_at - lay.qrows, MODEL_WIDTH), BF16),
+        ],
+        axis=2,
+    )
+    d_normed = dot_nn(dq, wq) + dot_nn(dkv, wkv)
+    scaled1 = d_normed * gain1
+    gain1_grad = jnp.sum(d_normed * stream * rstd1, axis=0)
+    inner1 = jnp.sum(scaled1 * stream, axis=1, keepdims=True)
+    in_grad = d_resid + rstd1 * scaled1 - stream * (rstd1 * rstd1 * rstd1 * inner1 / MODEL_WIDTH)
+
+    gain_rows = jnp.concatenate([gain1_grad[None], gain2_grad[None], jnp.zeros((6, MODEL_WIDTH), F32)], axis=0)
+    a_out, down_sum, gain_sum = reduce_attn(lay, a_grads, down.reshape(lay.planes, T, MODEL_WIDTH), gain_rows)
+    layer_out = (resid + down_sum).astype(BF16)
+    own_gains = lax.dynamic_slice_in_dim(gain_sum, col * W, W, 1)
+    heads = QUERY_HEADS // lay.cores
+    query_grad = jnp.transpose(a_out[: lay.qrows].reshape(heads, D // lay.dp, W), (2, 0, 1))
+    keyval_grad = jnp.transpose(a_out[lay.kv_at : lay.kv_at + lay.kvrows])[:, None, :]
+    out_block = a_out[lay.out_at : lay.out_at + lay.qrows].reshape(heads, D // lay.dp, W)
+    return (
+        layer_out,
+        in_grad.astype(BF16),
+        own_gains[0],
+        query_grad,
+        keyval_grad,
+        out_block,
+        own_gains[1],
+        f_out[0].T,
+        f_out[1].T,
+        f_out[2],
+    )
+
+
+def general_layout(segment, parent):
     labels = jnp.arange(SEGS, dtype=jnp.int32)
     member = (segment[:, None] == labels[None, :]).astype(jnp.float32)
     link = ((parent[:, None] == labels[None, :]) & (labels[:, None] > 0)).astype(jnp.float32)
     ident = jnp.eye(SEGS, dtype=jnp.float32)
 
     def climb(level, reach):
-        return ident + jnp.dot(link, reach, precision=HIGH)
+        return ident + jnp.dot(link, reach, precision=lax.Precision.HIGHEST)
 
     reach = lax.fori_loop(0, SEGS, climb, ident)
-    visible = jnp.dot(jnp.dot(member, reach, precision=HIGH), member.T, precision=HIGH) > 0.5
+    visible = jnp.dot(jnp.dot(member, reach, precision=lax.Precision.HIGHEST), member.T, precision=lax.Precision.HIGHEST) > 0.5
     places = jnp.arange(segment.shape[0], dtype=jnp.int32)
     allowed = visible & (places[:, None] >= places[None, :])
     sizes = jnp.sum(member, axis=0)
     earlier = (labels[None, :] < labels[:, None]).astype(jnp.float32)
-    starts = jnp.dot(earlier, sizes, precision=HIGH)
-    above = jnp.dot(reach, sizes, precision=HIGH) - sizes
-    tree_depth = places.astype(jnp.float32) + jnp.dot(member, above - starts, precision=HIGH)
+    starts = jnp.dot(earlier, sizes, precision=lax.Precision.HIGHEST)
+    above = jnp.dot(reach, sizes, precision=lax.Precision.HIGHEST) - sizes
+    tree_depth = places.astype(jnp.float32) + jnp.dot(member, above - starts, precision=lax.Precision.HIGHEST)
     return (allowed, tree_depth)
 
 
-def rotate(value_rows, tree_depth, sign):
+def general_rotate(value_rows, tree_depth, sign):
     half = value_rows.shape[-1] // 2
     freqs = jnp.arange(half, dtype=jnp.float32) * (2.0 / value_rows.shape[-1])
     inverse = jnp.exp(freqs * -math.log(THETA))
@@ -58,7 +609,7 @@
     return jnp.dot(left, right, preferred_element_type=jnp.float32)
 
 
-def body(
+def general_body(
     tokens,
     cotangent,
     seg_ids,
@@ -142,7 +693,7 @@
     )
     results = []
     input_grads = []
-    for batch_index in range(MICRO):
+    for batch_index in range(2):
         blocks, wide = fetch()
         (
             forward_query_block,
@@ -178,22 +729,22 @@
         projected_rows = col_reduce(qkv_term, TREE_TOKENS)
         half_cols = columns // 2
         tree_slot = (
-            col_index // half_cols * (MICRO * half_cols)
+            col_index // half_cols * (2 * half_cols)
             + batch_index * half_cols
             + col_index % half_cols
         )
         segment = lax.dynamic_index_in_dim(seg_ids, tree_slot, 0, keepdims=False)
         parent = lax.dynamic_index_in_dim(parents, tree_slot, 0, keepdims=False)
-        forward_allowed, forward_tree_depth = tree_layout(segment, parent)
+        forward_allowed, forward_tree_depth = general_layout(segment, parent)
         query_pre = projected_rows[:, :query_total_width].reshape(
             TREE_TOKENS, heads_here, HEAD_SIZE
         )
-        forward_query = rotate(query_pre, forward_tree_depth, 1.0).astype(jnp.bfloat16)
+        forward_query = general_rotate(query_pre, forward_tree_depth, 1.0).astype(jnp.bfloat16)
         own_unrotated = projected_rows[:, query_total_width:].reshape(
             TREE_TOKENS, KEY_VALUE_HEADS, HEAD_SIZE
         )
         own_part = jnp.where(
-            row_index == 0, rotate(own_unrotated, forward_tree_depth, 1.0), own_unrotated
+            row_index == 0, general_rotate(own_unrotated, forward_tree_depth, 1.0), own_unrotated
         ).astype(jnp.bfloat16)
         forward_pair = lax.all_gather(own_part[:, None], "row", axis=1, tiled=True)
         forward_keys_here = local_heads(forward_pair[:, 0])
@@ -367,9 +918,9 @@
             d_pair.astype(jnp.bfloat16), "row", scatter_dimension=1, tiled=True
         ).astype(jnp.float32)[:, 0]
         own_gradient = jnp.where(
-            row_index == 0, rotate(own_gradient, tree_depth, -1.0), own_gradient
-        )
-        query_pre_gradient = rotate(d_query, tree_depth, -1.0)
+            row_index == 0, general_rotate(own_gradient, tree_depth, -1.0), own_gradient
+        )
+        query_pre_gradient = general_rotate(d_query, tree_depth, -1.0)
         d_proj = jnp.concatenate(
             [
                 query_pre_gradient.reshape(TREE_TOKENS, query_total_width),
@@ -478,8 +1029,10 @@
         P("col", ("dp", "row")),
         P(("dp", "row"), "col"),
     )
+    lay = Layout(mesh.shape)
+    work = functools.partial(body, lay) if lay.fits() else general_body
     return jax.shard_map(
-        body,
+        work,
         mesh=mesh,
         in_specs=placed,
         out_specs=(

time: 1040 us -> 338 us (0.33); the launches traced: 1030 us -> 337 us
  waiting for transfers between devices: 599 us -> 0 us
  Pallas kernels: 0 us -> 245 us
  blocking collectives: 240 us -> 4.36 us
  matrix products: 75.1 us -> 37.8 us
  other arithmetic: 46.9 us -> 23.2 us
  starting transfers between devices: 21.9 us -> 0 us
  between operations: 17.6 us -> 1.25 us
    reduce_scatter x21 -> x0, waiting for transfers between devices: 326 us -> none  [the longest x8 123 us: col_reduce(): lax.psum_scatter(term(jnp.int32(0), rows * lax.axis_size('col')), 'col',...]
    pallas_call x0 -> x4, Pallas kernels: none -> 245 us  [the longest x1 99.2 us: gather_weights(): pl.pallas_call(functools.partial(gather_kernel, lay), out_shape=(jax.Shap...]
    all_gather x19 -> x1, blocking collectives: 181 us -> 4.36 us  [body(): lax.all_gather(jnp.stack([norm1_gain, norm2_gain]), 'col', axis=1, tiled=...]
    all_gather x5 -> x0, waiting for transfers between devices: 139 us -> none  [the longest x2 60.5 us: gather_cols(): return lax.all_gather(value_rows, 'col', axis=0, tiled=True)]
    unnamed x32 -> x0, waiting for transfers between devices: 129 us -> none
    psum x5 -> x0, blocking collectives: 50.6 us -> none  [the longest x1 30.8 us: body(): gains = lax.psum((gradients[0], gradients[4]), ('dp', 'row'))]
    dot_general x82 -> x23, matrix products: 75.1 us -> 35.2 us  [the longest x6 13 us: dot_nt(): lax.dot_general(left, right, (((1,), (1,)), ((), ())), preferred_element_...]
    convert_element_type x20 -> x5, other arithmetic: 21.6 us -> 4.06 us  [the longest x1 1.93 us: body(): layer_out = (resid + down_sum).astype(BF16)]
  transfers between devices with their start and end apart: 32 -> 0, of which waited for: 20 -> 0; matrix products, arithmetic and copies ran while one was open for 11% -> 0% of each run, Pallas kernels for 0% -> 0%
where the time goes in v1:
time: 338 us; the launch traced here: 337 us
  Pallas kernels  245 us (72%)
  matrix products  37.8 us (11%)
  local copies, waits for them, and re-layouts  26.1 us (8%)
  other arithmetic  23.2 us (7%)
  blocking collectives  4.36 us (1%)
    pallas_call x1, Pallas kernels, gather_weights(): pl.pallas_call(functools.partial(gather_kernel, lay), out_shape=(jax.Shap...  99.2 us
    pallas_call x1, Pallas kernels, reduce_attn(): pl.pallas_call(functools.partial(attn_grads_kernel, lay), out_shape=(jax....  67.5 us
    pallas_call x1, Pallas kernels, reduce_feed(): pl.pallas_call(functools.partial(feed_grads_kernel, lay), out_shape=(jax....  52.6 us
    pallas_call x1, Pallas kernels, gather_tokens(): pl.pallas_call(functools.partial(tokens_kernel, lay), out_shape=jax.Shape...  25.3 us
    dot_general x6, matrix products, dot_nt(): lax.dot_general(left, right, (((1,), (1,)), ((), ())), preferred_element_...  13 us
    dot_general x6, matrix products, dot_nn(): return jnp.dot(left, right, preferred_element_type=F32)  10.4 us
    dot_general x6, matrix products, dot_tn(): lax.dot_general(left, right, (((0,), (0,)), ((), ())), preferred_element_...  7.08 us

profile of v1, /device:TPU:0, one launch (start us, length us, event | category | flops | bytes accessed | tf_op | source)
XLA Modules:
  0.0 337.3 jit_solution(2261969084459101221)
XLA Ops:
  2.5 1.8 pad_maximum_fusion.4.a_ref
  4.3 2.2 pad_maximum_fusion.2.f_ref
  6.5 99.2 %gather_weights.1 = (bf16[8,2,208,1280]{3,2,1,0:T(8,128)(2,1)}, bf16[3,896,1280]{2,1,0:T(8,128)(2,1)}, bf16[4,128,1280]{2,1,0:T(8,128)(2,1)}) custom-call(bf16[208,640]{1,0:T(8,128)(2,1)} %pad_maximum_fusion.4.a_ref, bf16[3,224,640]{2,1,0:T(8,128)(2,1)} %pad_maximum_fusion.2.f_ref, bf16[128,1280]{1,0:T(8,128)(2,1)} %dy_ref.1), custom_call_target="tpu_custom_call" | custom-call | tf_op jit(solution)/shard_map/gather_weights/pallas_call | solution.py:161
  105.8 5.0 %slice_bitcast_fusion = (bf16[8,2,10,8,1280]{4,3,2,1,0:T(8,128)(2,1)}, bf16[8,2,10,8,1280]{4,3,2,1,0:T(8,128)(2,1)S(1)}) fusion(bf16[8,2,208,1280]{3,2,1,0:T(8,128)(2,1)} %get-tuple-element.18), kind=kLoop, calls=%fused_computation.11 | loop fusion | bytes 13107200 | tf_op jit(solution)/shard_map/reshape | solution.py:462
  111.5 4.4 %all_gather.3 = f32[2,1280]{1,0:T(2,128)S(1)} all-gather(f32[2,640]{1,0:T(2,128)S(1)} %pad_maximum_fusion.15), channel_id=1, replica_groups=mesh['dp'=8,'row'=2,'col'=2] {'col'}, dimensions={1}, use_global_device_ids=true | all-gather | bytes 15360 | tf_op jit(solution)/shard_map/all_gather | solution.py:457
  118.0 1.5 slice_bitcast_fusion.2
  124.1 2.7 fusion.65
  128.6 1.8 convolution_convert_fusion.8
  134.7 25.3 %gather_tokens.1 = bf16[4,128,1280]{2,1,0:T(8,128)(2,1)} custom-call(bf16[128,1280]{1,0:T(8,128)(2,1)} %multiply_convert_fusion.4.n_ref), custom_call_target="tpu_custom_call" | custom-call | tf_op jit(solution)/shard_map/gather_tokens/pallas_call | solution.py:194
  160.0 3.7 %fusion.10 = f32[512,896]{1,0:T(8,128)S(1)} fusion(bf16[512,1280]{1,0:T(8,128)(2,1)} %bitcast.201, bf16[3,896,1280]{2,1,0:T(8,128)(2,1)} %get-tuple-element.20), kind=kOutput, calls=%fused_computation.27 | convolution fusion | flops 1174405120 | bytes 5439488 | tf_op jit(solution)/shard_map/dot_general | solution.py:412
  163.7 3.3 fusion.13
  167.1 2.3 multiply_convert_fusion.2
  169.4 1.5 fusion.5
  170.9 2.7 fusion.4
  173.6 1.4 fusion.1
  175.0 1.4 fusion.2
  176.4 1.6 fusion.3
  178.0 3.4 pad_maximum_fusion.1.g_ref
  181.3 52.6 %reduce_feed.1 = (f32[3,224,640]{2,1,0:T(8,128)}, f32[128,1280]{1,0:T(8,128)}) custom-call(bf16[3,896,1280]{2,1,0:T(8,128)(2,1)} %pad_maximum_fusion.1.g_ref, bf16[4,128,1280]{2,1,0:T(8,128)(2,1)} %bitcast.200), custom_call_target="tpu_custom_call" | custom-call | tf_op jit(solution)/shard_map/reduce_feed/pallas_call | solution.py:281
  234.0 1.5 multiply_reduce_fusion.1
  235.4 1.4 multiply_subtract_fusion
  237.7 1.9 convolution_convert_fusion.7
  239.6 1.9 copy.54
  241.5 1.9 multiply_reduce_fusion
  253.1 4.4 %pad_maximum_fusion.g_ref = bf16[8,2,208,1280]{3,2,1,0:T(8,128)(2,1)} fusion(bf16[8,2,80,1280]{3,2,1,0:T(8,128)(2,1)S(1)} %get-tuple-element.62, bf16[8,2,40,1280]{3,2,1,0:T(8,128)(2,1)S(1)} %bitcast.193, bf16[8,2,80,1280]{3,2,1,0:T(8,128)(2,1)S(1)} %get-tuple-element.63, bf16[208]{0:T(256)(128)(2,1)S(1)} %pad.25.clone), kind=kLoop, calls=%fused_computation.1 | loop fusion | flops 34078720 | bytes 16712096 | tf_op jit(solution)/shard_map/concatenate | solution.py:535
  257.4 4.2 %convolution_convert_fusion.6 = bf16[512,1280]{1,0:T(8,128)(2,1)} fusion(bf16[512,896]{1,0:T(8,128)(2,1)S(1)} %copy-done.33, bf16[3,896,1280]{2,1,0:T(8,128)(2,1)} %get-tuple-element.20), kind=kOutput, calls=%fused_computation.18 | convolution fusion | flops 1175060480 | bytes 4521984 | tf_op jit(solution)/shard_map/dot_general | solution.py:420
  261.7 67.5 %reduce_attn.1 = (f32[208,640]{1,0:T(8,128)}, f32[128,1280]{1,0:T(8,128)}, f32[8,1280]{1,0:T(8,128)}) custom-call(bf16[8,2,208,1280]{3,2,1,0:T(8,128)(2,1)} %pad_maximum_fusion.g_ref, bf16[4,128,1280]{2,1,0:T(8,128)(2,1)} %bitcast.205, f32[8,1280]{1,0:T(8,128)} %maximum_maximum_fusion.n_ref), custom_call_target="tpu_custom_call" | custom-call | tf_op jit(solution)/shard_map/reduce_attn/pallas_call | solution.py:386
  329.2 1.9 slice_bitcast_fusion.6
  331.1 1.9 add_convert_fusion
  333.0 1.5 slice_bitcast_fusion.8
  334.6 1.5 dynamic-slice_reduce_fusion
  336.1 1.2 slice_bitcast_fusion.3
  (127 shorter events, 25.6 us)
Async XLA Ops:
  2.1 108.7 %copy-start.28 = (pred[128]{0:T(512)(128)(4,1)}, pred[128]{0:T(512)(128)(4,1)S(1)}, u32[]{:S(2)}) copy-start(pred[128]{0:T(512)(128)(4,1)S(1)} %compare_bitcast_fusion) | copy-start | bytes 388
  110.8 5.1 %copy-start.4 = (bf16[128,1280]{1,0:T(8,128)(2,1)S(1)}, bf16[128,1280]{1,0:T(8,128)(2,1)}, u32[]{:S(2)}) copy-start(bf16[128,1280]{1,0:T(8,128)(2,1)} %param.12) | copy-start | bytes 983044
  116.1 1.1 copy-start.29
  119.7 1.2 copy-start.10
  128.6 2.4 copy-start.12
  130.3 1.0 copy-start.16
  130.9 1.0 copy-start.5
  131.3 1.7 copy-start.2
  133.0 0.8 copy-start.7
  159.9 3.8 %copy-start.31 = (bf16[4,128,1280]{2,1,0:T(8,128)(2,1)S(1)}, bf16[4,128,1280]{2,1,0:T(8,128)(2,1)}, u32[]{:S(2)}) copy-start(bf16[4,128,1280]{2,1,0:T(8,128)(2,1)} %get-tuple-element.19) | copy-start | bytes 3932164
  160.0 7.1 %slice-start = ((s8[6881280]{0:T(1024)(128)(4,1)}), s8[4194304]{0:T(1024)(128)(4,1)S(1)}, s32[]{:S(2)}) async-start(s8[6881280]{0:T(1024)(128)(4,1)} %bitcast.225), calls=%async_computation | async-start | bytes 8388608
  163.7 3.4 %slice-start.1 = ((s8[6881280]{0:T(1024)(128)(4,1)}), s8[2686976]{0:T(1024)(128)(4,1)S(1)}, s32[]{:S(2)}) async-start(s8[6881280]{0:T(1024)(128)(4,1)} %bitcast.225), calls=%async_computation.1 | async-start | bytes 5373952
  163.7 3.4 %copy-start.19 = (bf16[4,128,1280]{2,1,0:T(8,128)(2,1)S(1)}, bf16[4,128,1280]{2,1,0:T(8,128)(2,1)}, u32[]{:S(2)}) copy-start(bf16[4,128,1280]{2,1,0:T(8,128)(2,1)} %gather_tokens.1) | copy-start | bytes 3932164
  169.4 7.0 %copy-start.32 = (bf16[512,896]{1,0:T(8,128)(2,1)}, bf16[512,896]{1,0:T(8,128)(2,1)S(1)}, u32[]{:S(2)}) copy-start(bf16[512,896]{1,0:T(8,128)(2,1)S(1)} %get-tuple-element.38) | copy-start | bytes 2752516
  181.3 52.6 %copy-start.8 = (f32[128,1280]{1,0:T(8,128)S(1)}, f32[128,1280]{1,0:T(8,128)}, u32[]{:S(2)}) copy-start(f32[128,1280]{1,0:T(8,128)} %copy-done.7) | copy-start | bytes 1966084
  181.3 54.1 %copy-start.20 = (bf16[128,1280]{1,0:T(8,128)(2,1)S(1)}, bf16[128,1280]{1,0:T(8,128)(2,1)}, u32[]{:S(2)}) copy-start(bf16[128,1280]{1,0:T(8,128)(2,1)} %dy_ref.1) | copy-start | bytes 983044
  233.9 3.7 %copy-start.3 = (bf16[8,2,10,8,1280]{4,3,0,2,1:T(8,128)(2,1)S(1)}, bf16[8,2,10,8,1280]{4,3,0,2,1:T(8,128)(2,1)}, u32[]{:S(2)}) copy-start(bf16[8,2,10,8,1280]{4,3,0,2,1:T(8,128)(2,1)} %copy-done.2) | copy-start | bytes 9830404
  236.8 0.9 copy-start.13
  237.7 3.8 %copy-start.25 = (bf16[128,320]{0,1:T(8,128)(2,1)S(1)}, bf16[128,320]{0,1:T(8,128)(2,1)}, u32[]{:S(2)}) copy-start(bf16[128,320]{0,1:T(8,128)(2,1)} %copy.49) | copy-start | bytes 245764
  241.5 1.9 copy-start.18
  244.1 0.9 copy-start.22
  244.1 1.0 copy-start.23
  244.1 1.4 copy-start.24
  245.5 1.0 copy-start.6
  245.5 1.5 copy-start.11
  245.9 1.8 copy-start.30
  245.9 1.8 copy-start.14
  250.3 1.1 copy-start.17
  253.1 4.4 %copy-start.33 = (bf16[512,896]{1,0:T(8,128)(2,1)S(1)}, bf16[512,896]{1,0:T(8,128)(2,1)}, u32[]{:S(2)}) copy-start(bf16[512,896]{1,0:T(8,128)(2,1)} %copy-done.32) | copy-start | bytes 2752516
  261.7 69.4 %copy-start.9 = (f32[128,1280]{1,0:T(8,128)S(1)}, f32[128,1280]{1,0:T(8,128)}, u32[]{:S(2)}) copy-start(f32[128,1280]{1,0:T(8,128)} %copy-done.7) | copy-start | bytes 1966084
  329.1 6.9 %copy-start.15 = (f32[3,224,640]{2,1,0:T(8,128)S(1)}, f32[3,224,640]{2,1,0:T(8,128)}, u32[]{:S(2)}) copy-start(f32[3,224,640]{2,1,0:T(8,128)} %get-tuple-element.25) | copy-start | bytes 5160964
  331.1 6.2 %copy-start.1 = (s32[4,13]{1,0:T(4,128)S(1)}, s32[4,13]{1,0:T(4,128)}, u32[]{:S(2)}) copy-start(s32[4,13]{1,0:T(4,128)} %param.15) | copy-start | bytes 628
  (4 other events, 2.8 us)

commit v2 on v0

--- a/solution.py
+++ b/solution.py
@@ -1,8 +1,11 @@
+import functools
 import math
 
 import jax
 import jax.numpy as jnp
 from jax import lax
+from jax.experimental import pallas as pl
+from jax.experimental.pallas import tpu as pltpu
 from jax.sharding import PartitionSpec as P
 
 MODEL_WIDTH = 1280
@@ -11,36 +14,702 @@
 HEAD_SIZE = 64
 TREE_TOKENS = 128
 SEGS = 13
-MICRO = 2
-
+PLANES = 4
 
 EPS = 1e-05
 THETA = 10000.0
-HIGH = lax.Precision.HIGHEST
-
-
-def tree_layout(segment, parent):
+MESH = pl.DeviceIdType.MESH
+F32 = jnp.float32
+BF16 = jnp.bfloat16
+
+
+class Layout:
+    def __init__(self, shape):
+        self.planes = PLANES
+        self.lines = shape["dp"] // PLANES
+        self.cores = shape["row"]
+        self.cols = shape["col"]
+        self.dp = shape["dp"]
+        self.width = MODEL_WIDTH // self.cols
+        self.qrows = QUERY_HEADS // self.cores * (HEAD_SIZE // self.dp)
+        self.kvrows = KEY_VALUE_HEADS * HEAD_SIZE // self.dp
+        self.kv_at = self.qrows
+        self.out_at = -(-(self.kv_at + self.kvrows) // 16) * 16
+        self.arows = -(-(self.out_at + self.qrows) // 16) * 16
+        self.acut = -(-(self.arows // 2) // 16) * 16
+
+    def fits(self):
+        return self.lines == 2 and self.cores == 2 and self.cols == 2 and self.dp == 2 * PLANES
+
+    def here(self):
+        dp = lax.axis_index("dp")
+        return dp // self.lines, lax.rem(dp, self.lines), lax.axis_index("row"), lax.axis_index("col")
+
+    def device(self, z, x, r, c):
+        return (z * self.lines + x, r, c)
+
+
+def greet(lay, peers):
+    barrier = pltpu.get_barrier_semaphore()
+    for peer in peers:
+        pl.semaphore_signal(barrier, inc=1, device_id=peer, device_id_type=MESH)
+    pl.semaphore_wait(barrier, len(peers))
+
+
+def dot_nt(left, right):
+    return lax.dot_general(left, right, (((1,), (1,)), ((), ())), preferred_element_type=F32)
+
+
+def dot_tn(left, right):
+    return lax.dot_general(left, right, (((0,), (0,)), ((), ())), preferred_element_type=F32)
+
+
+def dot_nn(left, right):
+    return jnp.dot(left, right, preferred_element_type=F32)
+
+
+class Links:
+    def __init__(self, send_sems, recv_sems):
+        self.send_sems, self.recv_sems, self.used = send_sems, recv_sems, 0
+        self.open = []
+
+    def send(self, src, dst, peer, source=None):
+        copy = pltpu.make_async_remote_copy(
+            src_ref=src,
+            dst_ref=dst,
+            send_sem=self.send_sems.at[self.used],
+            recv_sem=self.recv_sems.at[self.used],
+            device_id=peer,
+            device_id_type=MESH,
+        )
+        self.used += 1
+        copy.start()
+        self.open.append((source, copy))
+        return copy
+
+    def flush(self, *sources):
+        for source, copy in self.open:
+            if not sources or source in sources:
+                copy.wait_send()
+        self.open = [o for o in self.open if sources and o[0] not in sources]
+
+
+def turn(rows, cosine, sine):
+    lanes = rows.shape[1]
+    many = lanes // 128
+    half = HEAD_SIZE // 2
+    lane = lax.broadcasted_iota(jnp.int32, rows.shape, 1)
+    swapped = jnp.where(
+        lax.rem(lane, HEAD_SIZE) < half, pltpu.roll(rows, lanes - half, 1), pltpu.roll(rows, half, 1)
+    )
+    wide = lambda t: t if many == 1 else jnp.concatenate([t] * many, axis=1)
+    return rows * wide(cosine) + swapped * wide(sine)
+
+
+def stack_heads(rows, count):
+    return jnp.concatenate([rows[:, i * HEAD_SIZE : (i + 1) * HEAD_SIZE] for i in range(count)], axis=0)
+
+
+def spread_heads(rows, count):
+    return jnp.concatenate([rows[i * TREE_TOKENS : (i + 1) * TREE_TOKENS] for i in range(count)], axis=1)
+
+
+def add_into(dest, other, step):
+    def some(i, _):
+        rows = pl.ds(pl.multiple_of(i * step, step), step)
+        dest[rows, :] = (dest[rows, :].astype(F32) + other[rows, :].astype(F32)).astype(dest.dtype)
+        return 0
+
+    lax.fori_loop(0, dest.shape[0] // step, some, 0)
+
+
+def sum_into(dest, parts, step):
+    def some(i, _):
+        rows = pl.ds(pl.multiple_of(i * step, step), step)
+        acc = parts[0][rows, :].astype(F32)
+        for part in parts[1:]:
+            acc = acc + part[rows, :].astype(F32)
+        dest[rows, :] = acc.astype(dest.dtype)
+        return 0
+
+    lax.fori_loop(0, dest.shape[0] // step, some, 0)
+
+
+ORDER = (0, 1, 3, 2)
+
+
+def layer_kernel(
+    lay,
+    a_ref, f_ref, tok_ref, cot_ref, gain_ref, seg_ref, par_ref,
+    out_ref, in_grad_ref, gain_out, a_out, f_out,
+    ga, gf, wq, wkv, wo, gn, gdy, act, dgate, dup, d_act, gfull, normed, qs, ks, vs, probs, mix, resid,
+    rot_cos, rot_sin, dq, dk5, dv5, d_part, d_in, y_part, y_in,
+    fc_in, f1a, f1b, f2a, f2b, ac_in, a1a, a1b, a2a, a2b, az_in, nsum, nin,
+    send_sems, recv_sems, own_sems,
+):
+    z, x, r, c = lay.here()
+    W, T, D = lay.width, TREE_TOKENS, HEAD_SIZE
+    frows = f_ref.shape[1]
+    hid = lay.lines * lay.cores * frows
+    groups = KEY_VALUE_HEADS
+    per = QUERY_HEADS // KEY_VALUE_HEADS
+    kvw = KEY_VALUE_HEADS * D
+    scale = D**-0.5
+    x_other, c_other, r_other = 1 - x, 1 - c, 1 - r
+    x_peer = lay.device(z, x_other, r, c)
+    y_peer = lay.device(z, x, r, c_other)
+    sibling = lay.device(z, x, r_other, c)
+    plus = lambda k: lax.rem(z + k, lay.planes)
+    minus = lambda k: lax.rem(z + lay.planes - k, lay.planes)
+    z_peer = lambda k: lay.device(plus(k), x, r, c)
+    lanes = lambda cc: pl.ds(pl.multiple_of(cc * W, 128), W)
+    links = Links(send_sems, recv_sems)
+    send = links.send
+
+    greet(lay, [z_peer(k) for k in ORDER[1:]] + [x_peer, y_peer, sibling])
+
+    gain_y = send(gain_ref, gfull.at[:, lanes(c)], y_peer)
+
+    def block(zz, xx, rr):
+        return ga.at[zz * lay.lines + xx, rr]
+
+    own = [
+        pltpu.make_async_copy(a_ref, block(z, x, r).at[:, lanes(c)], own_sems.at[0]),
+        pltpu.make_async_copy(cot_ref, gdy.at[0], own_sems.at[1]),
+        pltpu.make_async_copy(gain_ref, gfull.at[:, lanes(c)], own_sems.at[2]),
+    ]
+    for copy in own:
+        copy.start()
+    az, dz, ax, ay, arx, ary, acore = {}, {}, {}, {}, {}, {}, {}
+    ax[0] = send(a_ref, block(z, x, r).at[:, lanes(c)], x_peer)
+    ay[0] = send(a_ref, block(z, x, r).at[:, lanes(c)], y_peer)
+    for k in ORDER[1:]:
+        az[k] = send(a_ref, block(z, x, r).at[:, lanes(c)], z_peer(k))
+    for s, k in enumerate(ORDER):
+        if k:
+            dz[s] = send(cot_ref, gdy.at[s], z_peer(k))
+
+    cut = lay.acut
+
+    def a_own(k):
+        az[k].wait_recv()
+        here = block(minus(k), x, r).at[:, lanes(c)]
+        ax[k] = send(here, here, x_peer, "ga")
+        ay[k] = send(here, here, y_peer, "ga")
+
+    def a_relay(k):
+        ax[k].wait_recv()
+        top = block(minus(k), x_other, r).at[pl.ds(0, cut), lanes(c)]
+        ary[k] = send(top, top, y_peer, "ga")
+        ay[k].wait_recv()
+        low = block(minus(k), x, r).at[pl.ds(cut, lay.arows - cut), lanes(c_other)]
+        arx[k] = send(low, low, x_peer, "ga")
+        acore[k, 0] = send(block(minus(k), x, r), block(minus(k), x, r), sibling, "ga")
+
+    def a_finish(k):
+        ary[k].wait_recv()
+        arx[k].wait_recv()
+        acore[k, 1] = send(block(minus(k), x_other, r), block(minus(k), x_other, r), sibling, "ga")
+
+    def a_unpack(k):
+        acore[k, 0].wait_recv()
+        acore[k, 1].wait_recv()
+        zz = minus(k)
+        heads = QUERY_HEADS // lay.cores
+        for rr in range(lay.cores):
+
+            def pair(m, _):
+                for base, dest in ((0, wq), (lay.out_at, wo)):
+                    rows = pl.ds(pl.multiple_of(base + m * 16, 16), 16)
+                    left = ga[zz * lay.lines, rr, rows, :].astype(F32)
+                    right = ga[zz * lay.lines + 1, rr, rows, :].astype(F32)
+                    at = (rr * heads + 2 * m) * D + zz * 16
+                    dest[pl.ds(pl.multiple_of(at, 16), 16), :] = jnp.concatenate([left[:8], right[:8]], axis=0).astype(BF16)
+                    dest[pl.ds(pl.multiple_of(at + D, 16), 16), :] = jnp.concatenate([left[8:], right[8:]], axis=0).astype(BF16)
+                return 0
+
+            lax.fori_loop(0, heads // 2, pair, 0)
+            n = lay.kvrows
+            left = ga[zz * lay.lines, rr, lay.kv_at : lay.out_at, :].astype(F32)
+            right = ga[zz * lay.lines + 1, rr, lay.kv_at : lay.out_at, :].astype(F32)
+            at = rr * kvw + zz * (2 * n)
+            wkv[pl.ds(pl.multiple_of(at, 16), 2 * n), :] = jnp.concatenate([left[:n], right[:n]], axis=0).astype(BF16)
+
+    stream = tok_ref[...].astype(F32)
+    rstd1 = lax.rsqrt(jnp.sum(stream * stream, axis=1, keepdims=True) / MODEL_WIDTH + EPS)
+    tree = r * lay.cols + c
+    seg_row = jnp.broadcast_to(seg_ref[pl.ds(tree, 1), :].astype(F32), (T, T))
+    par_row = par_ref[pl.ds(tree, 1), :].astype(F32)
+    seg_col = jnp.transpose(seg_row)
+    above = jnp.zeros((T, T), F32)
+    for s in range(par_ref.shape[1]):
+        above = jnp.where(seg_col == s, par_row[:, s : s + 1], above)
+    row_at = lax.broadcasted_iota(jnp.int32, (T, T), 0)
+    lane_at = lax.broadcasted_iota(jnp.int32, (T, T), 1)
+    seen = (seg_row == seg_col) | (seg_row == above) | (seg_row == 0.0)
+    allowed = jnp.where(seen & (row_at >= lane_at), 1.0, 0.0)
+    depth = jnp.sum(allowed, axis=1, keepdims=True) - 1.0
+    freq = lax.rem(lane_at, D // 2).astype(F32) * (2.0 / D)
+    angle = depth * jnp.exp(freq * -math.log(THETA))
+    rot_cos[...] = jnp.cos(angle)
+    sine = jnp.sin(angle)
+    rot_sin[...] = jnp.where(lax.rem(lane_at, D) < D // 2, -sine, sine)
+    for copy in own:
+        copy.wait()
+    gain_y.wait_recv()
+    normed[...] = (stream * rstd1 * gfull[0:1, :]).astype(BF16)
+
+    a_own(1)
+    a_relay(0)
+    a_own(3)
+    a_finish(0)
+    a_relay(1)
+    a_finish(1)
+    a_unpack(0)
+    a_own(2)
+    a_relay(3)
+    a_unpack(1)
+    a_finish(3)
+    a_relay(2)
+
+    def f_rows(xx, rr):
+        return pl.ds(pl.multiple_of((xx * lay.cores + rr) * frows, 16), frows)
+
+    def f_part(xx, low):
+        half = frows // 2
+        return pl.ds(pl.multiple_of((xx * lay.cores + r) * frows + low * half, 16), half)
+
+    fx, fy, frx, fry, fcore = {}, {}, {}, {}, {}
+    f_own = []
+    for i, w in enumerate((2, 0, 1)):
+        here = gf.at[w, f_rows(x, r), lanes(c)]
+        copy = pltpu.make_async_copy(f_ref.at[w], here, own_sems.at[3 + i])
+        copy.start()
+        f_own.append(copy)
+        fx[w] = send(f_ref.at[w], here, x_peer)
+        fy[w] = send(f_ref.at[w], here, y_peer)
+
+    def f_relay(w):
+        fx[w].wait_recv()
+        top = gf.at[w, f_part(x_other, 0), lanes(c)]
+        fry[w] = send(top, top, y_peer, "gf")
+        fy[w].wait_recv()
+        low = gf.at[w, f_part(x, 1), lanes(c_other)]
+        frx[w] = send(low, low, x_peer, "gf")
+        mine = gf.at[w, f_rows(x, r), :]
+        fcore[w, 0] = send(mine, mine, sibling, "gf")
+
+    def f_finish(w):
+        fry[w].wait_recv()
+        frx[w].wait_recv()
+        there = gf.at[w, f_rows(x_other, r), :]
+        fcore[w, 1] = send(there, there, sibling, "gf")
+
+    def f_ready(w):
+        fcore[w, 0].wait_recv()
+        fcore[w, 1].wait_recv()
+
+    a_unpack(3)
+    for copy in f_own:
+        copy.wait()
+    a_finish(2)
+    a_unpack(2)
+
+    kv = dot_nt(normed[...], wkv[...])
+    turned = turn(kv, rot_cos[...], rot_sin[...])
+    for g in range(groups):
+        ks[g] = turned[:, g * D : (g + 1) * D].astype(BF16)
+        vs[g] = kv[:, kvw + g * D : kvw + (g + 1) * D].astype(BF16)
+    allowed4 = jnp.concatenate([allowed] * per, axis=0) > 0.5
+    for g in range(groups):
+        cols = slice(g * per * D, (g + 1) * per * D)
+        pre = turn(dot_nt(normed[...], wq[cols, :]), rot_cos[...], rot_sin[...])
+        qs[g] = stack_heads(pre, per).astype(BF16)
+        scores = jnp.where(allowed4, dot_nt(qs[g], ks[g]) * scale, -1e30)
+        weight = jnp.exp(scores - jnp.max(scores, axis=1, keepdims=True))
+        share = weight / jnp.sum(weight, axis=1, keepdims=True)
+        probs[g] = share
+        mixed = dot_nn(share.astype(BF16), vs[g])
+        mix[:, cols] = spread_heads(mixed, per).astype(BF16)
+    f_relay(2)
+    res = stream + dot_nn(mix[...], wo[...])
+    resid[...] = res
+    rstd2 = lax.rsqrt(jnp.sum(res * res, axis=1, keepdims=True) / MODEL_WIDTH + EPS)
+    gn[0] = (res * rstd2 * gfull[1:2, :]).astype(BF16)
+    nz = {}
+    for s, k in enumerate(ORDER):
+        if k:
+            nz[s] = send(gn.at[0], gn.at[s], z_peer(k))
+    f_finish(2)
+    f_relay(0)
+    for s in dz:
+        dz[s].wait_recv()
+    f_ready(2)
+    n_rows = lay.planes * T
+    dy_all = lambda: gdy[...].reshape(n_rows, MODEL_WIDTH)
+    d_act[...] = dot_nt(dy_all(), gf[2])
+    f_finish(0)
+    f_relay(1)
+    f_ready(0)
+    f_finish(1)
+    f_ready(1)
+
+    def feed(first, last):
+        count = (last - first) * T
+        rows = slice(first * T, last * T)
+        n2 = gn[first:last].reshape(count, MODEL_WIDTH)
+        gate = dot_nt(n2, gf[0])
+        up = dot_nt(n2, gf[1])
+        sig = 1.0 / (1.0 + jnp.exp(-gate))
+        silu = gate * sig
+        act[rows, :] = (silu * up).astype(BF16)
+        da = d_act[rows, :]
+        dup[rows, :] = (da * silu).astype(BF16)
+        dgate[rows, :] = (da * up * sig * (1.0 + gate * (1.0 - sig))).astype(BF16)
+
+    def back(first, last):
+        count = (last - first) * T
+        rows = slice(first * T, last * T)
+        part = dot_nn(dgate[rows, :], gf[0]) + dot_nn(dup[rows, :], gf[1])
+        d_part[first:last] = part.astype(BF16).reshape(last - first, T, MODEL_WIDTH)
+
+    dnz = {}
+
+    def back_send(s):
+        dnz[s] = send(d_part.at[s], d_in.at[s - 1], lay.device(minus(ORDER[s]), x, r, c))
+
+    nz[1].wait_recv()
+    nz[2].wait_recv()
+    feed(1, 3)
+    back(1, 3)
+    back_send(1)
+    back_send(2)
+    nz[3].wait_recv()
+    feed(3, 4)
+    back(3, 4)
+    back_send(3)
+    feed(0, 1)
+    back(0, 1)
+
+    links.flush("ga", "gf")
+    fc, fs1a, fs1b, fs2a, fs2b = {}, {}, {}, {}, {}
+
+    def f_grad(w):
+        n2 = gn[...].reshape(n_rows, MODEL_WIDTH)
+        if w == 0:
+            grad = dot_tn(dgate[...], n2)
+        elif w == 1:
+            grad = dot_tn(dup[...], n2)
+        else:
+            grad = dot_tn(act[...], dy_all())
+        gf[w] = grad.astype(BF16)
+        for xx in range(lay.lines):
+            fc[w, xx] = send(gf.at[w, f_rows(xx, r_other), :], fc_in.at[w, xx], sibling)
+
+    def f_stage1(w):
+        for xx in range(lay.lines):
+            fc[w, xx].wait_recv()
+            add_into(gf.at[w, f_rows(xx, r), :], fc_in.at[w, xx], 32)
+        fs1a[w] = send(gf.at[w, f_part(x_other, 0), :], f1a.at[w], x_peer)
+        for xx in range(lay.lines):
+            fs1b[w, xx] = send(gf.at[w, f_part(xx, 1), lanes(c_other)], f1b.at[w, xx], y_peer)
+
+    def f_stage2(w):
+        fs1a[w].wait_recv()
+        add_into(gf.at[w, f_part(x, 0), :], f1a.at[w], 16)
+        fs2a[w] = send(gf.at[w, f_part(x, 0), lanes(c_other)], f2a.at[w], y_peer)
+        for xx in range(lay.lines):
+            fs1b[w, xx].wait_recv()
+            add_into(gf.at[w, f_part(xx, 1), lanes(c)], f1b.at[w, xx], 16)
+        fs2b[w] = send(gf.at[w, f_part(x_other, 1), lanes(c)], f2b.at[w], x_peer)
+
+    def f_total(w):
+        half = frows // 2
+        fs2a[w].wait_recv()
+        sum_into(f_out.at[w, pl.ds(0, half), :], [gf.at[w, f_part(x, 0), lanes(c)], f2a.at[w]], 16)
+        fs2b[w].wait_recv()
+        sum_into(f_out.at[w, pl.ds(half, half), :], [gf.at[w, f_part(x, 1), lanes(c)], f2b.at[w]], 16)
+
+    f_grad(0)
+    f_grad(1)
+    f_stage1(0)
+    y_all = dot_nn(act[...], gf[2])
+    y_part[...] = y_all.astype(BF16).reshape(lay.planes, T, MODEL_WIDTH)
+    yz = {}
+    for s, k in enumerate(ORDER):
+        if k:
+            yz[s] = send(y_part.at[s], y_in.at[s - 1], lay.device(minus(k), x, r, c))
+    f_grad(2)
+    f_stage1(1)
+    f_stage1(2)
+    f_stage2(0)
+
+    for s in dnz:
+        dnz[s].wait_recv()
+    d_n2 = d_part[0].astype(F32)
+    for s in range(lay.planes - 1):
+        d_n2 = d_n2 + d_in[s].astype(F32)
+    res = resid[...]
+    rstd2 = lax.rsqrt(jnp.sum(res * res, axis=1, keepdims=True) / MODEL_WIDTH + EPS)
+    gain2_grad = jnp.sum(d_n2 * res * rstd2, axis=0, keepdims=True)
+    scaled2 = d_n2 * gfull[1:2, :]
+    inner2 = jnp.sum(scaled2 * res, axis=1, keepdims=True)
+    d_res = cot_ref[...].astype(F32) + rstd2 * scaled2 - res * (rstd2 * rstd2 * rstd2 * inner2 / MODEL_WIDTH)
+    d_attn = d_res.astype(BF16)
+
+    def place_heads(source, other, base):
+        heads = QUERY_HEADS // lay.cores
+        for rr in range(lay.cores):
+            for m in range(heads // 2):
+                at = (rr * heads + 2 * m) * D
+                grad = dot_tn(source[:, at : at + 2 * D], other)
+                for dp in range(lay.dp):
+                    tile = jnp.concatenate([grad[dp * 8 : dp * 8 + 8], grad[D + dp * 8 : D + dp * 8 + 8]], axis=0)
+                    ga[dp, rr, base + m * 16 : base + m * 16 + 16, :] = tile.astype(BF16)
+
+    place_heads(mix, d_attn, lay.out_at)
+    for g in range(groups):
+        cols = slice(g * per * D, (g + 1) * per * D)
+        dms = stack_heads(dot_nt(d_attn, wo[cols, :]), per).astype(BF16)
+        share = probs[g]
+        dp_ = dot_nt(dms, vs[g])
+        delta = jnp.sum(share * dp_, axis=1, keepdims=True)
+        ds_ = (share * (dp_ - delta)).astype(BF16)
+        d_query = spread_heads(dot_nn(ds_, ks[g]) * scale, per)
+        dq[:, cols] = turn(d_query, rot_cos[...], -rot_sin[...]).astype(BF16)
+        dk5[g] = dot_tn(ds_, qs[g]) * scale
+        dv5[g] = dot_tn(share.astype(BF16), dms)
+    f_stage2(1)
+    zeros = jnp.zeros((T, D), F32)
+    dk_all = jnp.concatenate([dk5[g] for g in range(groups)] + [zeros], axis=1)
+    dk = turn(dk_all, rot_cos[...], -rot_sin[...])[:, :kvw].astype(BF16)
+    dv = jnp.concatenate([dv5[g] for g in range(groups)], axis=1).astype(BF16)
+    place_heads(dq, normed[...], 0)
+    for rr, rows in enumerate((dk, dv)):
+        grad = dot_tn(rows, normed[...])
+        pad = jnp.zeros((lay.out_at - lay.kv_at - lay.kvrows, MODEL_WIDTH), F32)
+        for dp in range(lay.dp):
+            tile = jnp.concatenate([grad[dp * lay.kvrows : (dp + 1) * lay.kvrows], pad], axis=0)
+            ga[dp, rr, lay.kv_at : lay.out_at, :] = tile.astype(BF16)
+
+    last_order = (2, 1, 3, 0)
+    ac, as1a, as1b, as2a, as2b, asz = {}, {}, {}, {}, {}, {}
+    for k in last_order:
+        for xx in range(lay.lines):
+            ac[k, xx] = send(block(plus(k), xx, r_other), ac_in.at[k, xx], sibling)
+
+    top = pl.ds(0, cut)
+    low = pl.ds(cut, lay.arows - cut)
+
+    def a_stage1(k):
+        for xx in range(lay.lines):
+            ac[k, xx].wait_recv()
+            add_into(block(plus(k), xx, r), ac_in.at[k, xx], 16)
+        as1a[k] = send(block(plus(k), x_other, r).at[top, :], a1a.at[k], x_peer)
+        for xx in range(lay.lines):
+            as1b[k, xx] = send(block(plus(k), xx, r).at[low, lanes(c_other)], a1b.at[k, xx], y_peer)
+
+    def a_stage2(k):
+        as1a[k].wait_recv()
+        add_into(block(plus(k), x, r).at[top, :], a1a.at[k], 16)
+        as2a[k] = send(block(plus(k), x, r).at[top, lanes(c_other)], a2a.at[k], y_peer)
+        for xx in range(lay.lines):
+            as1b[k, xx].wait_recv()
+            add_into(block(plus(k), xx, r).at[low, lanes(c)], a1b.at[k, xx], 16)
+        as2b[k] = send(block(plus(k), x_other, r).at[low, lanes(c)], a2b.at[k], x_peer)
+
+    def a_line(k):
+        as2a[k].wait_recv()
+        add_into(block(plus(k), x, r).at[top, lanes(c)], a2a.at[k], 16)
+        as2b[k].wait_recv()
+        add_into(block(plus(k), x, r).at[low, lanes(c)], a2b.at[k], 16)
+        if k:
+            asz[k] = send(block(plus(k), x, r).at[:, lanes(c)], az_in.at[k - 1], z_peer(k))
+
+    a_stage1(2)
+    d_normed = dot_nn(dq[...], wq[...]) + dot_nn(dk, wkv[:kvw, :]) + dot_nn(dv, wkv[kvw:, :])
+    a_stage1(1)
+    f_stage2(2)
+    stream = tok_ref[...].astype(F32)
+    rstd1 = lax.rsqrt(jnp.sum(stream * stream, axis=1, keepdims=True) / MODEL_WIDTH + EPS)
+    gain1_grad = jnp.sum(d_normed * stream * rstd1, axis=0, keepdims=True)
+    nsum[0] = jnp.concatenate([gain1_grad, gain2_grad, jnp.zeros((6, MODEL_WIDTH), F32)], axis=0)
+    g_core = send(nsum.at[0], nin.at[0], sibling)
+    scaled1 = d_normed * gfull[0:1, :]
+    inner1 = jnp.sum(scaled1 * stream, axis=1, keepdims=True)
+    in_grad = d_res + rstd1 * scaled1 - stream * (rstd1 * rstd1 * rstd1 * inner1 / MODEL_WIDTH)
+    in_grad_ref[...] = in_grad.astype(BF16)
+    a_stage1(3)
+    a_stage1(0)
+    a_stage2(2)
+    g_core.wait_recv()
+    nsum[1] = nsum[0] + nin[0]
+    g_x = send(nsum.at[1], nin.at[1], x_peer)
+    for s in yz:
+        yz[s].wait_recv()
+    y = resid[...] + y_part[0].astype(F32)
+    for s in range(lay.planes - 1):
+        y = y + y_in[s].astype(F32)
+    out_ref[...] = y.astype(BF16)
+    f_total(0)
+    f_total(1)
+    a_stage2(1)
+    a_line(2)
+    g_x.wait_recv()
+    nsum[2] = nsum[1] + nin[1]
+    g_y = send(nsum.at[2], nin.at[2], y_peer)
+    f_total(2)
+    a_stage2(3)
+    a_line(1)
+    g_y.wait_recv()
+    nsum[3] = nsum[2] + nin[2]
+    g_z = {k: send(nsum.at[3], nin.at[2 + k], z_peer(k)) for k in ORDER[1:]}
+    a_stage2(0)
+    a_line(3)
+    total = nsum[3]
+    for k in g_z:
+        g_z[k].wait_recv()
+        total = total + nin[2 + k]
+    nsum[4] = total
+    gain_out[...] = nsum[4, :, lanes(c)]
+    a_line(0)
+    for k in asz:
+        asz[k].wait_recv()
+    sum_into(a_out, [block(z, x, r).at[:, lanes(c)]] + [az_in.at[k] for k in range(lay.planes - 1)], 16)
+    links.flush()
+
+
+def whole_layer(lay, a_shard, f_shard, tokens, cotangent, gains, seg_ids, parents):
+    vm = lambda *shape: pltpu.VMEM(shape, BF16)
+    vf = lambda *shape: pltpu.VMEM(shape, F32)
+    M, T, D, W = MODEL_WIDTH, TREE_TOKENS, HEAD_SIZE, lay.width
+    frows = f_shard.shape[1]
+    hid = lay.lines * lay.cores * frows
+    G, per = KEY_VALUE_HEADS, QUERY_HEADS // KEY_VALUE_HEADS
+    n, nl, half = lay.planes, lay.lines, frows // 2
+    vmem = pl.BlockSpec(memory_space=pltpu.VMEM)
+    cut, rest = lay.acut, lay.arows - lay.acut
+    scratch = [
+        vm(lay.dp, lay.cores, lay.arows, M),
+        vm(3, hid, M),
+        vm(QUERY_HEADS * D, M),
+        vm(2 * G * D, M),
+        vm(QUERY_HEADS * D, M),
+        vm(n, T, M),
+        vm(n, T, M),
+        vm(n * T, hid),
+        vm(n * T, hid),
+        vm(n * T, hid),
+        vf(n * T, hid),
+        vf(8, M),
+        vm(T, M),
+        vm(G, per * T, D),
+        vm(G, T, D),
+        vm(G, T, D),
+        vf(G, per * T, T),
+        vm(T, M),
+        vf(T, M),
+        vf(T, T),
+        vf(T, T),
+        vm(T, M),
+        vf(G, T, D),
+        vf(G, T, D),
+        vm(n, T, M),
+        vm(n - 1, T, M),
+        vm(n, T, M),
+        vm(n - 1, T, M),
+        vm(3, nl, frows, M),
+        vm(3, half, M),
+        vm(3, nl, half, W),
+        vm(3, half, W),
+        vm(3, half, W),
+        vm(n, nl, lay.arows, M),
+        vm(n, cut, M),
+        vm(n, nl, rest, W),
+        vm(n, cut, W),
+        vm(n, rest, W),
+        vm(n - 1, lay.arows, W),
+        vf(5, 8, M),
+        vf(2 + n, 8, M),
+        pltpu.SemaphoreType.DMA((144,)),
+        pltpu.SemaphoreType.DMA((144,)),
+        pltpu.SemaphoreType.DMA((6,)),
+    ]
+    return pl.pallas_call(
+        functools.partial(layer_kernel, lay),
+        out_shape=(
+            jax.ShapeDtypeStruct((T, M), BF16),
+            jax.ShapeDtypeStruct((T, M), BF16),
+            jax.ShapeDtypeStruct((8, W), F32),
+            jax.ShapeDtypeStruct((lay.arows, W), F32),
+            jax.ShapeDtypeStruct((3, frows, W), F32),
+        ),
+        in_specs=[vmem] * 7,
+        out_specs=(vmem,) * 5,
+        scratch_shapes=scratch,
+        compiler_params=pltpu.CompilerParams(collective_id=0, has_side_effects=True, vmem_limit_bytes=62 * 2**20),
+        name="whole_layer",
+    )(a_shard, f_shard, tokens, cotangent, gains, seg_ids, parents)
+
+
+def body(lay, tokens, cotangent, seg_ids, parents, norm1_gain, w_query, key_value_weight, w_out, norm2_gain, w_gate, w_up, w_down):
+    W = lay.width
+    a_shard = jnp.concatenate(
+        [
+            jnp.transpose(w_query, (1, 2, 0)).reshape(lay.qrows, W),
+            jnp.transpose(key_value_weight[:, 0, :]),
+            jnp.zeros((lay.out_at - lay.kv_at - lay.kvrows, W), BF16),
+            w_out.reshape(lay.qrows, W),
+            jnp.zeros((lay.arows - lay.out_at - lay.qrows, W), BF16),
+        ],
+        axis=0,
+    )
+    f_shard = jnp.stack([w_gate.T, w_up.T, w_down], axis=0)
+    gains = jnp.concatenate([norm1_gain[None], norm2_gain[None], jnp.zeros((6, W), F32)], axis=0)
+    layer_out, in_grad, gain_sum, a_out, f_out = whole_layer(
+        lay, a_shard, f_shard, tokens, cotangent, gains, seg_ids, parents
+    )
+    heads = QUERY_HEADS // lay.cores
+    shape = (heads, HEAD_SIZE // lay.dp, W)
+    query_grad = jnp.transpose(a_out[: lay.qrows].reshape(shape), (2, 0, 1))
+    keyval_grad = jnp.transpose(a_out[lay.kv_at : lay.kv_at + lay.kvrows])[:, None, :]
+    out_grad = a_out[lay.out_at : lay.out_at + lay.qrows].reshape(shape)
+    return (
+        layer_out,
+        in_grad,
+        gain_sum[0],
+        query_grad,
+        keyval_grad,
+        out_grad,
+        gain_sum[1],
+        f_out[0].T,
+        f_out[1].T,
+        f_out[2],
+    )
+
+
+def general_layout(segment, parent):
     labels = jnp.arange(SEGS, dtype=jnp.int32)
     member = (segment[:, None] == labels[None, :]).astype(jnp.float32)
     link = ((parent[:, None] == labels[None, :]) & (labels[:, None] > 0)).astype(jnp.float32)
     ident = jnp.eye(SEGS, dtype=jnp.float32)
 
     def climb(level, reach):
-        return ident + jnp.dot(link, reach, precision=HIGH)
+        return ident + jnp.dot(link, reach, precision=lax.Precision.HIGHEST)
 
     reach = lax.fori_loop(0, SEGS, climb, ident)
-    visible = jnp.dot(jnp.dot(member, reach, precision=HIGH), member.T, precision=HIGH) > 0.5
+    visible = jnp.dot(jnp.dot(member, reach, precision=lax.Precision.HIGHEST), member.T, precision=lax.Precision.HIGHEST) > 0.5
     places = jnp.arange(segment.shape[0], dtype=jnp.int32)
     allowed = visible & (places[:, None] >= places[None, :])
     sizes = jnp.sum(member, axis=0)
     earlier = (labels[None, :] < labels[:, None]).astype(jnp.float32)
-    starts = jnp.dot(earlier, sizes, precision=HIGH)
-    above = jnp.dot(reach, sizes, precision=HIGH) - sizes
-    tree_depth = places.astype(jnp.float32) + jnp.dot(member, above - starts, precision=HIGH)
+    starts = jnp.dot(earlier, sizes, precision=lax.Precision.HIGHEST)
+    above = jnp.dot(reach, sizes, precision=lax.Precision.HIGHEST) - sizes
+    tree_depth = places.astype(jnp.float32) + jnp.dot(member, above - starts, precision=lax.Precision.HIGHEST)
     return (allowed, tree_depth)
 
 
-def rotate(value_rows, tree_depth, sign):
+def general_rotate(value_rows, tree_depth, sign):
     half = value_rows.shape[-1] // 2
     freqs = jnp.arange(half, dtype=jnp.float32) * (2.0 / value_rows.shape[-1])
     inverse = jnp.exp(freqs * -math.log(THETA))
@@ -58,7 +727,7 @@
     return jnp.dot(left, right, preferred_element_type=jnp.float32)
 
 
-def body(
+def general_body(
     tokens,
     cotangent,
     seg_ids,
@@ -142,7 +811,7 @@
     )
     results = []
     input_grads = []
-    for batch_index in range(MICRO):
+    for batch_index in range(2):
         blocks, wide = fetch()
         (
             forward_query_block,
@@ -178,22 +847,22 @@
         projected_rows = col_reduce(qkv_term, TREE_TOKENS)
         half_cols = columns // 2
         tree_slot = (
-            col_index // half_cols * (MICRO * half_cols)
+            col_index // half_cols * (2 * half_cols)
             + batch_index * half_cols
             + col_index % half_cols
         )
         segment = lax.dynamic_index_in_dim(seg_ids, tree_slot, 0, keepdims=False)
         parent = lax.dynamic_index_in_dim(parents, tree_slot, 0, keepdims=False)
-        forward_allowed, forward_tree_depth = tree_layout(segment, parent)
+        forward_allowed, forward_tree_depth = general_layout(segment, parent)
         query_pre = projected_rows[:, :query_total_width].reshape(
             TREE_TOKENS, heads_here, HEAD_SIZE
         )
-        forward_query = rotate(query_pre, forward_tree_depth, 1.0).astype(jnp.bfloat16)
+        forward_query = general_rotate(query_pre, forward_tree_depth, 1.0).astype(jnp.bfloat16)
         own_unrotated = projected_rows[:, query_total_width:].reshape(
             TREE_TOKENS, KEY_VALUE_HEADS, HEAD_SIZE
         )
         own_part = jnp.where(
-            row_index == 0, rotate(own_unrotated, forward_tree_depth, 1.0), own_unrotated
+            row_index == 0, general_rotate(own_unrotated, forward_tree_depth, 1.0), own_unrotated
         ).astype(jnp.bfloat16)
         forward_pair = lax.all_gather(own_part[:, None], "row", axis=1, tiled=True)
         forward_keys_here = local_heads(forward_pair[:, 0])
@@ -367,9 +1036,9 @@
             d_pair.astype(jnp.bfloat16), "row", scatter_dimension=1, tiled=True
         ).astype(jnp.float32)[:, 0]
         own_gradient = jnp.where(
-            row_index == 0, rotate(own_gradient, tree_depth, -1.0), own_gradient
-        )
-        query_pre_gradient = rotate(d_query, tree_depth, -1.0)
+            row_index == 0, general_rotate(own_gradient, tree_depth, -1.0), own_gradient
+        )
+        query_pre_gradient = general_rotate(d_query, tree_depth, -1.0)
         d_proj = jnp.concatenate(
             [
                 query_pre_gradient.reshape(TREE_TOKENS, query_total_width),
@@ -478,8 +1147,10 @@
         P("col", ("dp", "row")),
         P(("dp", "row"), "col"),
     )
+    lay = Layout(mesh.shape)
+    work = functools.partial(body, lay) if lay.fits() else general_body
     return jax.shard_map(
-        body,
+        work,
         mesh=mesh,
         in_specs=placed,
         out_specs=(

time: 1040 us -> 215 us (0.21); the launches traced: 1030 us -> 214 us
  waiting for transfers between devices: 599 us -> 0 us
  blocking collectives: 240 us -> 0 us
  Pallas kernels: 0 us -> 198 us
  matrix products: 75.1 us -> 0 us
  other arithmetic: 46.9 us -> 4.62 us
  starting transfers between devices: 21.9 us -> 0 us
  between operations: 17.6 us -> 0.67 us
  local copies, waits for them, and re-layouts: 25.6 us -> 10.4 us
    reduce_scatter x21 -> x0, waiting for transfers between devices: 326 us -> none  [the longest x8 123 us: col_reduce(): lax.psum_scatter(term(jnp.int32(0), rows * lax.axis_size('col')), 'col',...]
    pallas_call x0 -> x1, Pallas kernels: none -> 198 us  [whole_layer(): pl.pallas_call(functools.partial(layer_kernel, lay), out_shape=(jax.Shape...]
    all_gather x19 -> x0, blocking collectives: 181 us -> none  [the longest x6 63.2 us: gather_cols(): return lax.all_gather(value_rows, 'col', axis=0, tiled=True)]
    all_gather x5 -> x0, waiting for transfers between devices: 139 us -> none  [the longest x2 60.5 us: gather_cols(): return lax.all_gather(value_rows, 'col', axis=0, tiled=True)]
    unnamed x32 -> x0, waiting for transfers between devices: 129 us -> none
    dot_general x82 -> x0, matrix products: 75.1 us -> none  [the longest x12 17.7 us: product(): return jnp.dot(left, right, preferred_element_type=jnp.float32)]
    psum x5 -> x0, blocking collectives: 50.6 us -> none  [the longest x1 30.8 us: body(): gains = lax.psum((gradients[0], gradients[4]), ('dp', 'row'))]
    convert_element_type x20 -> x0, other arithmetic: 21.6 us -> none  [the longest x6 8.27 us: body(): shards = (lax.psum_scatter(gradients[1].astype(jnp.bfloat16), 'dp', scatt...]
  transfers between devices with their start and end apart: 32 -> 0, of which waited for: 20 -> 0; matrix products, arithmetic and copies ran while one was open for 11% -> 0% of each run, Pallas kernels for 0% -> 0%
where the time goes in v2:
time: 215 us; the launch traced here: 214 us
  Pallas kernels  198 us (92%)
  local copies, waits for them, and re-layouts  10.4 us (5%)
  other arithmetic  4.62 us (2%)
    pallas_call x1, Pallas kernels, whole_layer(): pl.pallas_call(functools.partial(layer_kernel, lay), out_shape=(jax.Shape...  198 us

profile of v2, /device:TPU:0, one launch (start us, length us, event | category | flops | bytes accessed | tf_op | source)
XLA Modules:
  0.0 214.1 jit_solution(13063173811995111992)
XLA Ops:
  0.7 0.1 pad.8.clone
  0.7 0.1 pad.2.clone
  0.8 0.7 broadcast_in_dim.16
  1.5 0.7 broadcast_in_dim.17
  2.2 0.7 maximum_maximum_fusion.gain_ref
  2.9 1.8 pad_maximum_fusion.1.a_ref
  4.7 2.2 %pad_maximum_fusion.f_ref = bf16[3,224,640]{2,1,0:T(8,128)(2,1)} fusion(bf16[1,224,640]{2,1,0:T(8,128)(2,1)} %bitcast.34, bf16[1,224,640]{2,1,0:T(8,128)(2,1)} %bitcast.35, bf16[1,224,640]{2,1,0:T(8,128)(2,1)} %bitcast.36), kind=kLoop, calls=%fused_computation | loop fusion | flops 860160 | bytes 1720320 | tf_op jit(solution)/shard_map/stack | solution.py:667
  6.8 198.4 %whole_layer.1 = (bf16[128,1280]{1,0:T(8,128)(2,1)}, bf16[128,1280]{1,0:T(8,128)(2,1)}, f32[8,640]{1,0:T(8,128)}, f32[208,640]{1,0:T(8,128)}, f32[3,224,640]{2,1,0:T(8,128)}) custom-call(bf16[208,640]{1,0:T(8,128)(2,1)} %pad_maximum_fusion.1.a_ref, bf16[3,224,640]{2,1,0:T(8,128)(2,1)} %pad_maximum_fusion.f_ref, bf16[128,1280]{1,0:T(8,128)(2,1)} %tok_ref.1, ...), custom_call_target="tpu_custom_call" | custom-call | tf_op jit(solution)/shard_map/whole_layer/pallas_call | solution.py:638
  205.2 1.4 slice_reduce_fusion
  206.6 1.5 slice_bitcast_fusion.5
  208.2 1.8 slice_bitcast_fusion.3
  210.0 0.0 copy-start.1
  210.0 0.0 copy-start
  210.0 2.7 %slice_bitcast_fusion = (f32[224,640]{1,0:T(8,128)}, f32[640,224]{0,1:T(8,128)}, f32[640,224]{0,1:T(8,128)}) fusion(f32[3,224,640]{2,1,0:T(8,128)} %get-tuple-element.19), kind=kLoop, calls=%fused_computation.1 | loop fusion | bytes 3440640 | tf_op jit(solution)/shard_map/squeeze | solution.py:687
  212.7 0.0 copy-done.1
  212.7 0.7 copy.24
  213.4 0.0 copy-done
  213.4 0.7 copy.25
  (2 shorter events, 0.0 us)
Async XLA Ops:
  210.0 2.7 %copy-start.1 = (bf16[128,1280]{1,0:T(8,128)(2,1)S(1)}, bf16[128,1280]{1,0:T(8,128)(2,1)}, u32[]{:S(2)}) copy-start(bf16[128,1280]{1,0:T(8,128)(2,1)} %get-tuple-element.37) | copy-start | bytes 983044
  210.0 3.4 %copy-start = (bf16[128,1280]{1,0:T(8,128)(2,1)S(1)}, bf16[128,1280]{1,0:T(8,128)(2,1)}, u32[]{:S(2)}) copy-start(bf16[128,1280]{1,0:T(8,128)(2,1)} %get-tuple-element.38) | copy-start | bytes 983044

commit v3 on v2

--- a/solution.py
+++ b/solution.py
@@ -36,7 +36,8 @@
         self.kv_at = self.qrows
         self.out_at = -(-(self.kv_at + self.kvrows) // 16) * 16
         self.arows = -(-(self.out_at + self.qrows) // 16) * 16
-        self.acut = -(-(self.arows // 2) // 16) * 16
+        self.parts = ((0, self.out_at), (self.out_at, self.arows - self.out_at))
+        self.cuts = tuple(-(-(rows // 2) // 16) * 16 for _, rows in self.parts)
 
     def fits(self):
         return self.lines == 2 and self.cores == 2 and self.cols == 2 and self.dp == 2 * PLANES
@@ -44,6 +45,13 @@
     def here(self):
         dp = lax.axis_index("dp")
         return dp // self.lines, lax.rem(dp, self.lines), lax.axis_index("row"), lax.axis_index("col")
+
+    def inner(self, z):
+        return lax.rem((z + 1) // 2, 2)
+
+    def line(self, z):
+        half = z // 2
+        return z, z + 1 - 2 * lax.rem(z, 2), 2 - half, 3 - 3 * half
 
     def device(self, z, x, r, c):
         return (z * self.lines + x, r, c)
@@ -68,21 +76,105 @@
     return jnp.dot(left, right, preferred_element_type=F32)
 
 
+class Line:
+    def __init__(self, lay, links, source, slots, pos_1, pos_x):
+        z, x, r, c = lay.here()
+        self.inner = lay.inner(z)
+        base = links.take(4)
+        self.slots = slots
+        peers = lay.line(z)
+        self.side, self.near = lay.device(peers[1], x, r, c), lay.device(peers[2], x, r, c)
+
+        def copy(src, dst, s, t, peer):
+            return pltpu.make_async_remote_copy(
+                src_ref=src,
+                dst_ref=dst,
+                send_sem=links.send_sems.at[base + s],
+                recv_sem=links.recv_sems.at[base + t],
+                device_id=peer,
+                device_id_type=MESH,
+            )
+
+        self.first = copy(source, pos_1, 0, 0, self.side)
+        self.cross = copy(source, pos_x, 1, 2 - self.inner, self.near)
+        self.passed = {p: copy(slots(p), slots(p), p, p - 1, self.side) for p in (2, 3)}
+
+    def start(self):
+        self.first.start()
+        self.cross.start()
+
+    def relay(self, p):
+        @pl.when(self.inner == 1)
+        def _():
+            self.passed[p].wait_recv()
+            self.passed[p].start()
+
+    def arrive(self, p):
+        if p == 1:
+            self.first.wait_recv()
+            return
+
+        @pl.when(self.inner == 0)
+        def _():
+            self.passed[p].wait_recv()
+
+    def flush(self):
+        self.first.wait_send()
+        self.cross.wait_send()
+
+        @pl.when(self.inner == 1)
+        def _():
+            self.passed[2].wait_send()
+            self.passed[3].wait_send()
+
+
+class LineSum:
+    def __init__(self, lay, links, landing):
+        z, x, r, c = lay.here()
+        base = links.take(3)
+        side, mirror = lay.device(lay.line(z)[1], x, r, c), lay.device(lay.planes - 1 - z, x, r, c)
+        self.copy = lambda source, s: pltpu.make_async_remote_copy(
+            src_ref=source,
+            dst_ref=landing.at[s],
+            send_sem=links.send_sems.at[base + s],
+            recv_sem=links.recv_sems.at[base + s],
+            device_id=mirror if s == 2 else side,
+            device_id_type=MESH,
+        )
+        self.landing, self.used = landing, set()
+
+    def send(self, s, source):
+        self.used.add(s)
+        self.copy(source, s).start()
+
+    def arrive(self, s):
+        self.copy(self.landing.at[s], s).wait_recv()
+
+    def flush(self):
+        for s in sorted(self.used):
+            self.copy(self.landing.at[s], s).wait_send()
+
+
 class Links:
     def __init__(self, send_sems, recv_sems):
         self.send_sems, self.recv_sems, self.used = send_sems, recv_sems, 0
         self.open = []
 
+    def take(self, count):
+        first = self.used
+        self.used += count
+        return first
+
     def send(self, src, dst, peer, source=None):
+        at = self.take(1)
         copy = pltpu.make_async_remote_copy(
             src_ref=src,
             dst_ref=dst,
-            send_sem=self.send_sems.at[self.used],
-            recv_sem=self.recv_sems.at[self.used],
+            send_sem=self.send_sems.at[at],
+            recv_sem=self.recv_sems.at[at],
             device_id=peer,
             device_id_type=MESH,
         )
-        self.used += 1
         copy.start()
         self.open.append((source, copy))
         return copy
@@ -135,21 +227,19 @@
     lax.fori_loop(0, dest.shape[0] // step, some, 0)
 
 
-ORDER = (0, 1, 3, 2)
-
-
 def layer_kernel(
     lay,
-    a_ref, f_ref, tok_ref, cot_ref, gain_ref, seg_ref, par_ref,
-    out_ref, in_grad_ref, gain_out, a_out, f_out,
+    q_ref, kv_ref, o_ref, gate_ref, up_ref, down_ref, tok_ref, cot_ref, gain_ref, seg_ref, par_ref,
+    out_hbm, in_grad_hbm, gain_out, q_hbm, kv_hbm, o_hbm, gate_hbm, up_hbm, down_hbm,
     ga, gf, wq, wkv, wo, gn, gdy, act, dgate, dup, d_act, gfull, normed, qs, ks, vs, probs, mix, resid,
     rot_cos, rot_sin, dq, dk5, dv5, d_part, d_in, y_part, y_in,
-    fc_in, f1a, f1b, f2a, f2b, ac_in, a1a, a1b, a2a, a2b, az_in, nsum, nin,
-    send_sems, recv_sems, own_sems,
+    fc_in, f1a, f1b, f2a, f2b, ac_in, a1a, a1b, a2, az_in, nsum, nin,
+    out_ref, in_grad_ref, a_out, f_out,
+    send_sems, recv_sems, own_sems, out_sems,
 ):
     z, x, r, c = lay.here()
     W, T, D = lay.width, TREE_TOKENS, HEAD_SIZE
-    frows = f_ref.shape[1]
+    frows = gate_ref.shape[0]
     hid = lay.lines * lay.cores * frows
     groups = KEY_VALUE_HEADS
     per = QUERY_HEADS // KEY_VALUE_HEADS
@@ -159,81 +249,117 @@
     x_peer = lay.device(z, x_other, r, c)
     y_peer = lay.device(z, x, r, c_other)
     sibling = lay.device(z, x, r_other, c)
-    plus = lambda k: lax.rem(z + k, lay.planes)
-    minus = lambda k: lax.rem(z + lay.planes - k, lay.planes)
-    z_peer = lambda k: lay.device(plus(k), x, r, c)
+    planes = lay.line(z)
+    inner = lay.inner(z)
+    line = range(lay.planes)
     lanes = lambda cc: pl.ds(pl.multiple_of(cc * W, 128), W)
     links = Links(send_sems, recv_sems)
     send = links.send
-
-    greet(lay, [z_peer(k) for k in ORDER[1:]] + [x_peer, y_peer, sibling])
-
-    gain_y = send(gain_ref, gfull.at[:, lanes(c)], y_peer)
+    outgoing = []
+
+    def put(source, dest):
+        copy = pltpu.make_async_copy(source, dest, out_sems.at[len(outgoing)])
+        copy.start()
+        outgoing.append(copy)
 
     def block(zz, xx, rr):
         return ga.at[zz * lay.lines + xx, rr]
 
+    half = frows // 2
+    halves = (pl.ds(0, half), pl.ds(half, half))
+    weights = lambda w: gf[w].reshape(hid, MODEL_WIDTH)
+
+    mine = block(z, x, r).at[:, lanes(c)]
+    f_refs = (gate_ref, up_ref, down_ref)
     own = [
-        pltpu.make_async_copy(a_ref, block(z, x, r).at[:, lanes(c)], own_sems.at[0]),
-        pltpu.make_async_copy(cot_ref, gdy.at[0], own_sems.at[1]),
-        pltpu.make_async_copy(gain_ref, gfull.at[:, lanes(c)], own_sems.at[2]),
+        pltpu.make_async_copy(q_ref, mine.at[pl.ds(0, lay.qrows), :], own_sems.at[0]),
+        pltpu.make_async_copy(o_ref, mine.at[pl.ds(lay.out_at, lay.qrows), :], own_sems.at[1]),
+        pltpu.make_async_copy(cot_ref, gdy.at[0], own_sems.at[2]),
     ]
+    for w in range(3):
+        own.append(pltpu.make_async_copy(f_refs[w], gf.at[w, x, r, :, lanes(c)], own_sems.at[3 + w]))
     for copy in own:
         copy.start()
-    az, dz, ax, ay, arx, ary, acore = {}, {}, {}, {}, {}, {}, {}
-    ax[0] = send(a_ref, block(z, x, r).at[:, lanes(c)], x_peer)
-    ay[0] = send(a_ref, block(z, x, r).at[:, lanes(c)], y_peer)
-    for k in ORDER[1:]:
-        az[k] = send(a_ref, block(z, x, r).at[:, lanes(c)], z_peer(k))
-    for s, k in enumerate(ORDER):
+    pad = jnp.zeros((lay.out_at - lay.kv_at - lay.kvrows, W), BF16)
+    mine[lay.kv_at : lay.out_at, :] = jnp.concatenate([kv_ref[...], pad], axis=0)
+    if lay.arows > lay.out_at + lay.qrows:
+        mine[lay.out_at + lay.qrows :, :] = jnp.zeros((lay.arows - lay.out_at - lay.qrows, W), BF16)
+
+    greet(lay, [lay.device(planes[p], x, r, c) for p in line[1:]] + [x_peer, y_peer, sibling])
+    for copy in own[:2]:
+        copy.wait()
+
+    gfull[:, lanes(c)] = gain_ref[...]
+    gain_y = send(gain_ref, gfull.at[:, lanes(c)], y_peer)
+    ax, ay, arx, ary, acore = {}, {}, {}, {}, {}
+
+    def a_rows(part, first=0, rows=None):
+        at, many = lay.parts[part]
+        return pl.ds(at + first, many if rows is None else rows)
+
+    def a_here(part, zz):
+        return block(zz, x, r).at[a_rows(part), lanes(c)]
+
+    a_line = [
+        Line(lay, links, a_here(i, z), lambda p, i=i: a_here(i, planes[p]), a_here(i, z), a_here(i, z)) for i in range(2)
+    ]
+    dy_line = Line(lay, links, gdy.at[0], lambda p: gdy.at[p], gdy.at[1], gdy.at[3 - inner])
+    n_line = Line(lay, links, gn.at[0], lambda p: gn.at[p], gn.at[1], gn.at[3 - inner])
+    d_line, y_line, n_sum = (LineSum(lay, links, landing) for landing in (d_in, y_in, nin.at[pl.ds(3, 3)]))
+    g_line = [LineSum(lay, links, az_in.at[:, a_rows(i), :]) for i in range(2)]
+
+    def a_own(i, k):
         if k:
-            dz[s] = send(cot_ref, gdy.at[s], z_peer(k))
-
-    cut = lay.acut
-
-    def a_own(k):
-        az[k].wait_recv()
-        here = block(minus(k), x, r).at[:, lanes(c)]
-        ax[k] = send(here, here, x_peer, "ga")
-        ay[k] = send(here, here, y_peer, "ga")
-
-    def a_relay(k):
-        ax[k].wait_recv()
-        top = block(minus(k), x_other, r).at[pl.ds(0, cut), lanes(c)]
-        ary[k] = send(top, top, y_peer, "ga")
-        ay[k].wait_recv()
-        low = block(minus(k), x, r).at[pl.ds(cut, lay.arows - cut), lanes(c_other)]
-        arx[k] = send(low, low, x_peer, "ga")
-        acore[k, 0] = send(block(minus(k), x, r), block(minus(k), x, r), sibling, "ga")
-
-    def a_finish(k):
-        ary[k].wait_recv()
-        arx[k].wait_recv()
-        acore[k, 1] = send(block(minus(k), x_other, r), block(minus(k), x_other, r), sibling, "ga")
-
-    def a_unpack(k):
-        acore[k, 0].wait_recv()
-        acore[k, 1].wait_recv()
-        zz = minus(k)
+            a_line[i].arrive(k)
+        here = a_here(i, planes[k])
+        ax[i, k] = send(here, here, x_peer, "ga")
+        ay[i, k] = send(here, here, y_peer, "ga")
+
+    def a_core(i, k, xx, j):
+        rows = block(planes[k], xx, r).at[a_rows(i), :]
+        acore[i, k, j] = send(rows, rows, sibling, "ga")
+
+    def a_relay(i, k):
+        ax[i, k].wait_recv()
+        top = block(planes[k], x_other, r).at[a_rows(i, 0, lay.cuts[i]), lanes(c)]
+        ary[i, k] = send(top, top, y_peer, "ga")
+        ay[i, k].wait_recv()
+        low = block(planes[k], x, r).at[a_rows(i, lay.cuts[i], lay.parts[i][1] - lay.cuts[i]), lanes(c_other)]
+        arx[i, k] = send(low, low, x_peer, "ga")
+        a_core(i, k, x, 0)
+
+    def a_finish(i, k):
+        ary[i, k].wait_recv()
+        arx[i, k].wait_recv()
+        a_core(i, k, x_other, 1)
+
+    def a_unpack(i, k):
+        acore[i, k, 0].wait_recv()
+        acore[i, k, 1].wait_recv()
+        zz = planes[k]
         heads = QUERY_HEADS // lay.cores
+        dest = (wq, wo)[i]
         for rr in range(lay.cores):
 
             def pair(m, _):
-                for base, dest in ((0, wq), (lay.out_at, wo)):
-                    rows = pl.ds(pl.multiple_of(base + m * 16, 16), 16)
-                    left = ga[zz * lay.lines, rr, rows, :].astype(F32)
-                    right = ga[zz * lay.lines + 1, rr, rows, :].astype(F32)
-                    at = (rr * heads + 2 * m) * D + zz * 16
-                    dest[pl.ds(pl.multiple_of(at, 16), 16), :] = jnp.concatenate([left[:8], right[:8]], axis=0).astype(BF16)
-                    dest[pl.ds(pl.multiple_of(at + D, 16), 16), :] = jnp.concatenate([left[8:], right[8:]], axis=0).astype(BF16)
+                rows = pl.ds(pl.multiple_of(lay.parts[i][0] + m * 16, 16), 16)
+                left = ga[zz * lay.lines, rr, rows, :].astype(F32)
+                right = ga[zz * lay.lines + 1, rr, rows, :].astype(F32)
+                at = (rr * heads + 2 * m) * D + zz * 16
+                dest[pl.ds(pl.multiple_of(at, 16), 16), :] = jnp.concatenate([left[:8], right[:8]], axis=0).astype(BF16)
+                dest[pl.ds(pl.multiple_of(at + D, 16), 16), :] = jnp.concatenate([left[8:], right[8:]], axis=0).astype(BF16)
                 return 0
 
             lax.fori_loop(0, heads // 2, pair, 0)
-            n = lay.kvrows
-            left = ga[zz * lay.lines, rr, lay.kv_at : lay.out_at, :].astype(F32)
-            right = ga[zz * lay.lines + 1, rr, lay.kv_at : lay.out_at, :].astype(F32)
-            at = rr * kvw + zz * (2 * n)
-            wkv[pl.ds(pl.multiple_of(at, 16), 2 * n), :] = jnp.concatenate([left[:n], right[:n]], axis=0).astype(BF16)
+            if i == 0:
+                n = lay.kvrows
+                left = ga[zz * lay.lines, rr, lay.kv_at : lay.out_at, :].astype(F32)
+                right = ga[zz * lay.lines + 1, rr, lay.kv_at : lay.out_at, :].astype(F32)
+                at = rr * kvw + zz * (2 * n)
+                wkv[pl.ds(pl.multiple_of(at, 16), 2 * n), :] = jnp.concatenate([left[:n], right[:n]], axis=0).astype(BF16)
+
+    a_own(0, 0)
+    a_line[0].start()
 
     stream = tok_ref[...].astype(F32)
     rstd1 = lax.rsqrt(jnp.sum(stream * stream, axis=1, keepdims=True) / MODEL_WIDTH + EPS)
@@ -254,66 +380,62 @@
     rot_cos[...] = jnp.cos(angle)
     sine = jnp.sin(angle)
     rot_sin[...] = jnp.where(lax.rem(lane_at, D) < D // 2, -sine, sine)
-    for copy in own:
+    for copy in own[2:]:
         copy.wait()
     gain_y.wait_recv()
     normed[...] = (stream * rstd1 * gfull[0:1, :]).astype(BF16)
 
-    a_own(1)
-    a_relay(0)
-    a_own(3)
-    a_finish(0)
-    a_relay(1)
-    a_finish(1)
-    a_unpack(0)
-    a_own(2)
-    a_relay(3)
-    a_unpack(1)
-    a_finish(3)
-    a_relay(2)
-
-    def f_rows(xx, rr):
-        return pl.ds(pl.multiple_of((xx * lay.cores + rr) * frows, 16), frows)
-
-    def f_part(xx, low):
-        half = frows // 2
-        return pl.ds(pl.multiple_of((xx * lay.cores + r) * frows + low * half, 16), half)
+    a_line[0].relay(2)
+    a_own(0, 1)
+    a_relay(0, 0)
+    a_line[0].relay(3)
+    a_line[1].start()
+    a_finish(0, 0)
+    a_relay(0, 1)
+    a_own(0, 2)
+    a_finish(0, 1)
+    a_unpack(0, 0)
+    a_own(0, 3)
+    a_line[1].relay(2)
+    a_relay(0, 2)
+    a_own(1, 0)
+    a_finish(0, 2)
+    a_line[1].relay(3)
+    dy_line.start()
+    a_unpack(0, 1)
+    a_own(1, 1)
+    a_relay(0, 3)
+    a_own(1, 2)
+    a_unpack(0, 2)
+    a_relay(1, 0)
+    a_own(1, 3)
+    a_finish(0, 3)
+    a_unpack(0, 3)
 
     fx, fy, frx, fry, fcore = {}, {}, {}, {}, {}
-    f_own = []
-    for i, w in enumerate((2, 0, 1)):
-        here = gf.at[w, f_rows(x, r), lanes(c)]
-        copy = pltpu.make_async_copy(f_ref.at[w], here, own_sems.at[3 + i])
-        copy.start()
-        f_own.append(copy)
-        fx[w] = send(f_ref.at[w], here, x_peer)
-        fy[w] = send(f_ref.at[w], here, y_peer)
+
+    def f_send(w):
+        here = gf.at[w, x, r, :, lanes(c)]
+        fx[w] = send(here, here, x_peer, "gf")
+        fy[w] = send(here, here, y_peer, "gf")
 
     def f_relay(w):
         fx[w].wait_recv()
-        top = gf.at[w, f_part(x_other, 0), lanes(c)]
+        top = gf.at[w, x_other, r, halves[0], lanes(c)]
         fry[w] = send(top, top, y_peer, "gf")
         fy[w].wait_recv()
-        low = gf.at[w, f_part(x, 1), lanes(c_other)]
+        low = gf.at[w, x, r, halves[1], lanes(c_other)]
         frx[w] = send(low, low, x_peer, "gf")
-        mine = gf.at[w, f_rows(x, r), :]
-        fcore[w, 0] = send(mine, mine, sibling, "gf")
+        fcore[w, 0] = send(gf.at[w, x, r], gf.at[w, x, r], sibling, "gf")
 
     def f_finish(w):
         fry[w].wait_recv()
         frx[w].wait_recv()
-        there = gf.at[w, f_rows(x_other, r), :]
-        fcore[w, 1] = send(there, there, sibling, "gf")
+        fcore[w, 1] = send(gf.at[w, x_other, r], gf.at[w, x_other, r], sibling, "gf")
 
     def f_ready(w):
         fcore[w, 0].wait_recv()
         fcore[w, 1].wait_recv()
-
-    a_unpack(3)
-    for copy in f_own:
-        copy.wait()
-    a_finish(2)
-    a_unpack(2)
 
     kv = dot_nt(normed[...], wkv[...])
     turned = turn(kv, rot_cos[...], rot_sin[...])
@@ -321,6 +443,13 @@
         ks[g] = turned[:, g * D : (g + 1) * D].astype(BF16)
         vs[g] = kv[:, kvw + g * D : kvw + (g + 1) * D].astype(BF16)
     allowed4 = jnp.concatenate([allowed] * per, axis=0) > 0.5
+    between = {
+        0: [lambda: a_relay(1, 1)],
+        1: [lambda: a_finish(1, 0)],
+        2: [lambda: a_relay(1, 2), lambda: a_unpack(1, 0)],
+        3: [lambda: a_finish(1, 1), lambda: dy_line.relay(2)],
+        4: [lambda: a_relay(1, 3), lambda: [f_send(w) for w in (2, 0, 1)]],
+    }
     for g in range(groups):
         cols = slice(g * per * D, (g + 1) * per * D)
         pre = turn(dot_nt(normed[...], wq[cols, :]), rot_cos[...], rot_sin[...])
@@ -331,25 +460,32 @@
         probs[g] = share
         mixed = dot_nn(share.astype(BF16), vs[g])
         mix[:, cols] = spread_heads(mixed, per).astype(BF16)
-    f_relay(2)
+        for step in between[g]:
+            step()
+    a_unpack(1, 1)
+    a_finish(1, 2)
+    a_unpack(1, 2)
+    a_finish(1, 3)
+    a_unpack(1, 3)
     res = stream + dot_nn(mix[...], wo[...])
     resid[...] = res
     rstd2 = lax.rsqrt(jnp.sum(res * res, axis=1, keepdims=True) / MODEL_WIDTH + EPS)
     gn[0] = (res * rstd2 * gfull[1:2, :]).astype(BF16)
-    nz = {}
-    for s, k in enumerate(ORDER):
-        if k:
-            nz[s] = send(gn.at[0], gn.at[s], z_peer(k))
+    n_line.start()
+    dy_line.relay(3)
+    f_relay(2)
+    f_relay(0)
     f_finish(2)
-    f_relay(0)
-    for s in dz:
-        dz[s].wait_recv()
+    n_line.relay(2)
+    for p in line[1:]:
+        dy_line.arrive(p)
     f_ready(2)
     n_rows = lay.planes * T
     dy_all = lambda: gdy[...].reshape(n_rows, MODEL_WIDTH)
-    d_act[...] = dot_nt(dy_all(), gf[2])
+    d_act[...] = dot_nt(dy_all(), weights(2))
+    f_relay(1)
     f_finish(0)
-    f_relay(1)
+    n_line.relay(3)
     f_ready(0)
     f_finish(1)
     f_ready(1)
@@ -358,8 +494,8 @@
         count = (last - first) * T
         rows = slice(first * T, last * T)
         n2 = gn[first:last].reshape(count, MODEL_WIDTH)
-        gate = dot_nt(n2, gf[0])
-        up = dot_nt(n2, gf[1])
+        gate = dot_nt(n2, weights(0))
+        up = dot_nt(n2, weights(1))
         sig = 1.0 / (1.0 + jnp.exp(-gate))
         silu = gate * sig
         act[rows, :] = (silu * up).astype(BF16)
@@ -370,28 +506,40 @@
     def back(first, last):
         count = (last - first) * T
         rows = slice(first * T, last * T)
-        part = dot_nn(dgate[rows, :], gf[0]) + dot_nn(dup[rows, :], gf[1])
+        part = dot_nn(dgate[rows, :], weights(0)) + dot_nn(dup[rows, :], weights(1))
         d_part[first:last] = part.astype(BF16).reshape(last - first, T, MODEL_WIDTH)
 
-    dnz = {}
-
-    def back_send(s):
-        dnz[s] = send(d_part.at[s], d_in.at[s - 1], lay.device(minus(ORDER[s]), x, r, c))
-
-    nz[1].wait_recv()
-    nz[2].wait_recv()
+    n_line.arrive(1)
+    n_line.arrive(2)
     feed(1, 3)
     back(1, 3)
-    back_send(1)
-    back_send(2)
-    nz[3].wait_recv()
+
+    @pl.when(inner == 0)
+    def _():
+        d_line.send(0, d_part.at[2])
+        d_line.send(1, d_part.at[1])
+
+    n_line.arrive(3)
     feed(3, 4)
     back(3, 4)
-    back_send(3)
+
+    @pl.when(inner == 1)
+    def _():
+        d_line.send(0, d_part.at[3])
+        d_line.send(1, d_part.at[1])
+
     feed(0, 1)
     back(0, 1)
 
+    def mirror(line_sum, terms, landing):
+        line_sum.arrive(0)
+        p = 3 - inner
+        terms[p] = (terms[p].astype(F32) + landing[0].astype(F32)).astype(BF16)
+        line_sum.send(2, terms.at[p])
+
     links.flush("ga", "gf")
+    for part in a_line:
+        part.flush()
     fc, fs1a, fs1b, fs2a, fs2b = {}, {}, {}, {}, {}
 
     def f_grad(w):
@@ -402,53 +550,49 @@
             grad = dot_tn(dup[...], n2)
         else:
             grad = dot_tn(act[...], dy_all())
-        gf[w] = grad.astype(BF16)
+        gf[w] = grad.astype(BF16).reshape(lay.lines, lay.cores, frows, MODEL_WIDTH)
+        fc[w] = send(gf.at[w, :, r_other], fc_in.at[w], sibling)
+
+    def f_stage1(w):
+        fc[w].wait_recv()
         for xx in range(lay.lines):
-            fc[w, xx] = send(gf.at[w, f_rows(xx, r_other), :], fc_in.at[w, xx], sibling)
-
-    def f_stage1(w):
-        for xx in range(lay.lines):
-            fc[w, xx].wait_recv()
-            add_into(gf.at[w, f_rows(xx, r), :], fc_in.at[w, xx], 32)
-        fs1a[w] = send(gf.at[w, f_part(x_other, 0), :], f1a.at[w], x_peer)
-        for xx in range(lay.lines):
-            fs1b[w, xx] = send(gf.at[w, f_part(xx, 1), lanes(c_other)], f1b.at[w, xx], y_peer)
+            add_into(gf.at[w, xx, r], fc_in.at[w, xx], 32)
+        fs1a[w] = send(gf.at[w, x_other, r, halves[0], :], f1a.at[w], x_peer)
+        fs1b[w] = send(gf.at[w, :, r, halves[1], lanes(c_other)], f1b.at[w], y_peer)
 
     def f_stage2(w):
         fs1a[w].wait_recv()
-        add_into(gf.at[w, f_part(x, 0), :], f1a.at[w], 16)
-        fs2a[w] = send(gf.at[w, f_part(x, 0), lanes(c_other)], f2a.at[w], y_peer)
+        add_into(gf.at[w, x, r, halves[0], :], f1a.at[w], 16)
+        fs2a[w] = send(gf.at[w, x, r, halves[0], lanes(c_other)], f2a.at[w], y_peer)
+        fs1b[w].wait_recv()
         for xx in range(lay.lines):
-            fs1b[w, xx].wait_recv()
-            add_into(gf.at[w, f_part(xx, 1), lanes(c)], f1b.at[w, xx], 16)
-        fs2b[w] = send(gf.at[w, f_part(x_other, 1), lanes(c)], f2b.at[w], x_peer)
-
-    def f_total(w):
-        half = frows // 2
+            add_into(gf.at[w, xx, r, halves[1], lanes(c)], f1b.at[w, xx], 16)
+        fs2b[w] = send(gf.at[w, x_other, r, halves[1], lanes(c)], f2b.at[w], x_peer)
+
+    def f_total(w, dest):
         fs2a[w].wait_recv()
-        sum_into(f_out.at[w, pl.ds(0, half), :], [gf.at[w, f_part(x, 0), lanes(c)], f2a.at[w]], 16)
+        sum_into(f_out.at[w, halves[0], :], [gf.at[w, x, r, halves[0], lanes(c)], f2a.at[w]], 16)
         fs2b[w].wait_recv()
-        sum_into(f_out.at[w, pl.ds(half, half), :], [gf.at[w, f_part(x, 1), lanes(c)], f2b.at[w]], 16)
+        sum_into(f_out.at[w, halves[1], :], [gf.at[w, x, r, halves[1], lanes(c)], f2b.at[w]], 16)
+        put(f_out.at[w], dest)
 
     f_grad(0)
     f_grad(1)
     f_stage1(0)
-    y_all = dot_nn(act[...], gf[2])
+    mirror(d_line, d_part, d_in)
+    y_all = dot_nn(act[...], weights(2))
     y_part[...] = y_all.astype(BF16).reshape(lay.planes, T, MODEL_WIDTH)
-    yz = {}
-    for s, k in enumerate(ORDER):
-        if k:
-            yz[s] = send(y_part.at[s], y_in.at[s - 1], lay.device(minus(k), x, r, c))
+    y_line.send(0, y_part.at[2 + inner])
+    y_line.send(1, y_part.at[1])
     f_grad(2)
     f_stage1(1)
     f_stage1(2)
     f_stage2(0)
-
-    for s in dnz:
-        dnz[s].wait_recv()
-    d_n2 = d_part[0].astype(F32)
-    for s in range(lay.planes - 1):
-        d_n2 = d_n2 + d_in[s].astype(F32)
+    f_stage2(1)
+
+    d_line.arrive(1)
+    d_line.arrive(2)
+    d_n2 = d_part[0].astype(F32) + d_in[1].astype(F32) + d_in[2].astype(F32)
     res = resid[...]
     rstd2 = lax.rsqrt(jnp.sum(res * res, axis=1, keepdims=True) / MODEL_WIDTH + EPS)
     gain2_grad = jnp.sum(d_n2 * res * rstd2, axis=0, keepdims=True)
@@ -467,7 +611,71 @@
                     tile = jnp.concatenate([grad[dp * 8 : dp * 8 + 8], grad[D + dp * 8 : D + dp * 8 + 8]], axis=0)
                     ga[dp, rr, base + m * 16 : base + m * 16 + 16, :] = tile.astype(BF16)
 
+    to_plane = (planes[2] + inner * (planes[3] - planes[2]), planes[3] + inner * (planes[2] - planes[3]), planes[1], z)
+    ac, as1a, as1b, as2a, as2b = {}, {}, {}, {}, {}
+
+    def a_pair(zz, rr, rows):
+        return ga.at[pl.ds(zz * lay.lines, lay.lines), rr, rows]
+
+    def a_core_sums(i):
+        for t in line:
+            ac[i, t] = send(a_pair(to_plane[t], r_other, a_rows(i)), ac_in.at[t, :, a_rows(i), :], sibling)
+
+    def ends(i):
+        return a_rows(i, 0, lay.cuts[i]), a_rows(i, lay.cuts[i], lay.parts[i][1] - lay.cuts[i])
+
+    def a_stage1(i, t):
+        top, low = ends(i)
+        zz = to_plane[t]
+        ac[i, t].wait_recv()
+        for xx in range(lay.lines):
+            add_into(block(zz, xx, r).at[a_rows(i), :], ac_in.at[t, xx, a_rows(i), :], 16)
+        as1a[i, t] = send(block(zz, x_other, r).at[top, :], a1a.at[t, top, :], x_peer)
+        as1b[i, t] = send(a_pair(zz, r, low).at[:, :, lanes(c_other)], a1b.at[t, :, low, :], y_peer)
+
+    def a_stage2(i, t):
+        top, low = ends(i)
+        zz = to_plane[t]
+        as1a[i, t].wait_recv()
+        add_into(block(zz, x, r).at[top, :], a1a.at[t, top, :], 16)
+        as2a[i, t] = send(block(zz, x, r).at[top, lanes(c_other)], a2.at[t, top, :], y_peer)
+        as1b[i, t].wait_recv()
+        for xx in range(lay.lines):
+            add_into(block(zz, xx, r).at[low, lanes(c)], a1b.at[t, xx, low, :], 16)
+        as2b[i, t] = send(block(zz, x_other, r).at[low, lanes(c)], a2.at[t, low, :], x_peer)
+
+    def a_line_sum(i, t):
+        here = a_here(i, to_plane[t])
+        as2a[i, t].wait_recv()
+        as2b[i, t].wait_recv()
+        add_into(here, a2.at[t, a_rows(i), :], 16)
+        if t == 1:
+            g_line[i].arrive(0)
+            add_into(here, az_in.at[0, a_rows(i), :], 16)
+        if t < 3:
+            g_line[i].send((0, 2, 1)[t], here)
+
+    def a_total(i):
+        g_line[i].arrive(1)
+        g_line[i].arrive(2)
+        parts = [a_here(i, z), az_in.at[1, a_rows(i), :], az_in.at[2, a_rows(i), :]]
+        sum_into(a_out.at[a_rows(i), :], parts, 16)
+        if i == 0:
+            put(a_out.at[pl.ds(0, lay.qrows), :], q_hbm)
+            put(a_out.at[pl.ds(lay.kv_at, lay.kvrows), :], kv_hbm)
+        else:
+            put(a_out.at[pl.ds(lay.out_at, lay.qrows), :], o_hbm)
+
     place_heads(mix, d_attn, lay.out_at)
+    a_core_sums(1)
+    f_stage2(2)
+    between = {
+        0: [lambda: a_stage1(1, 0), lambda: a_stage1(1, 1)],
+        1: [lambda: a_stage1(1, 2), lambda: a_stage1(1, 3)],
+        2: [lambda: mirror(y_line, y_part, y_in)],
+        3: [lambda: a_stage2(1, 0)],
+        4: [lambda: a_stage2(1, 1)],
+    }
     for g in range(groups):
         cols = slice(g * per * D, (g + 1) * per * D)
         dms = stack_heads(dot_nt(d_attn, wo[cols, :]), per).astype(BF16)
@@ -479,7 +687,8 @@
         dq[:, cols] = turn(d_query, rot_cos[...], -rot_sin[...]).astype(BF16)
         dk5[g] = dot_tn(ds_, qs[g]) * scale
         dv5[g] = dot_tn(share.astype(BF16), dms)
-    f_stage2(1)
+        for step in between[g]:
+            step()
     zeros = jnp.zeros((T, D), F32)
     dk_all = jnp.concatenate([dk5[g] for g in range(groups)] + [zeros], axis=1)
     dk = turn(dk_all, rot_cos[...], -rot_sin[...])[:, :kvw].astype(BF16)
@@ -491,107 +700,81 @@
         for dp in range(lay.dp):
             tile = jnp.concatenate([grad[dp * lay.kvrows : (dp + 1) * lay.kvrows], pad], axis=0)
             ga[dp, rr, lay.kv_at : lay.out_at, :] = tile.astype(BF16)
-
-    last_order = (2, 1, 3, 0)
-    ac, as1a, as1b, as2a, as2b, asz = {}, {}, {}, {}, {}, {}
-    for k in last_order:
-        for xx in range(lay.lines):
-            ac[k, xx] = send(block(plus(k), xx, r_other), ac_in.at[k, xx], sibling)
-
-    top = pl.ds(0, cut)
-    low = pl.ds(cut, lay.arows - cut)
-
-    def a_stage1(k):
-        for xx in range(lay.lines):
-            ac[k, xx].wait_recv()
-            add_into(block(plus(k), xx, r), ac_in.at[k, xx], 16)
-        as1a[k] = send(block(plus(k), x_other, r).at[top, :], a1a.at[k], x_peer)
-        for xx in range(lay.lines):
-            as1b[k, xx] = send(block(plus(k), xx, r).at[low, lanes(c_other)], a1b.at[k, xx], y_peer)
-
-    def a_stage2(k):
-        as1a[k].wait_recv()
-        add_into(block(plus(k), x, r).at[top, :], a1a.at[k], 16)
-        as2a[k] = send(block(plus(k), x, r).at[top, lanes(c_other)], a2a.at[k], y_peer)
-        for xx in range(lay.lines):
-            as1b[k, xx].wait_recv()
-            add_into(block(plus(k), xx, r).at[low, lanes(c)], a1b.at[k, xx], 16)
-        as2b[k] = send(block(plus(k), x_other, r).at[low, lanes(c)], a2b.at[k], x_peer)
-
-    def a_line(k):
-        as2a[k].wait_recv()
-        add_into(block(plus(k), x, r).at[top, lanes(c)], a2a.at[k], 16)
-        as2b[k].wait_recv()
-        add_into(block(plus(k), x, r).at[low, lanes(c)], a2b.at[k], 16)
-        if k:
-            asz[k] = send(block(plus(k), x, r).at[:, lanes(c)], az_in.at[k - 1], z_peer(k))
-
-    a_stage1(2)
+    a_core_sums(0)
+    a_stage2(1, 2)
+    a_stage2(1, 3)
+    a_stage1(0, 0)
+    a_line_sum(1, 0)
+    a_stage1(0, 1)
+    a_line_sum(1, 1)
     d_normed = dot_nn(dq[...], wq[...]) + dot_nn(dk, wkv[:kvw, :]) + dot_nn(dv, wkv[kvw:, :])
-    a_stage1(1)
-    f_stage2(2)
+    a_stage2(0, 0)
+    a_stage1(0, 2)
+    a_line_sum(1, 2)
     stream = tok_ref[...].astype(F32)
     rstd1 = lax.rsqrt(jnp.sum(stream * stream, axis=1, keepdims=True) / MODEL_WIDTH + EPS)
     gain1_grad = jnp.sum(d_normed * stream * rstd1, axis=0, keepdims=True)
     nsum[0] = jnp.concatenate([gain1_grad, gain2_grad, jnp.zeros((6, MODEL_WIDTH), F32)], axis=0)
     g_core = send(nsum.at[0], nin.at[0], sibling)
+    a_stage2(0, 1)
+    a_stage1(0, 3)
     scaled1 = d_normed * gfull[0:1, :]
     inner1 = jnp.sum(scaled1 * stream, axis=1, keepdims=True)
     in_grad = d_res + rstd1 * scaled1 - stream * (rstd1 * rstd1 * rstd1 * inner1 / MODEL_WIDTH)
     in_grad_ref[...] = in_grad.astype(BF16)
-    a_stage1(3)
-    a_stage1(0)
-    a_stage2(2)
+    put(in_grad_ref, in_grad_hbm)
+    a_line_sum(0, 0)
+    a_stage2(0, 2)
     g_core.wait_recv()
     nsum[1] = nsum[0] + nin[0]
     g_x = send(nsum.at[1], nin.at[1], x_peer)
-    for s in yz:
-        yz[s].wait_recv()
-    y = resid[...] + y_part[0].astype(F32)
-    for s in range(lay.planes - 1):
-        y = y + y_in[s].astype(F32)
+    a_line_sum(1, 3)
+    y_line.arrive(1)
+    y_line.arrive(2)
+    y = resid[...] + y_part[0].astype(F32) + y_in[1].astype(F32) + y_in[2].astype(F32)
     out_ref[...] = y.astype(BF16)
-    f_total(0)
-    f_total(1)
-    a_stage2(1)
-    a_line(2)
+    put(out_ref, out_hbm)
+    a_line_sum(0, 1)
+    a_stage2(0, 3)
     g_x.wait_recv()
     nsum[2] = nsum[1] + nin[1]
     g_y = send(nsum.at[2], nin.at[2], y_peer)
-    f_total(2)
-    a_stage2(3)
-    a_line(1)
+    f_total(0, gate_hbm)
+    f_total(1, up_hbm)
+    f_total(2, down_hbm)
+    a_total(1)
+    a_line_sum(0, 2)
     g_y.wait_recv()
     nsum[3] = nsum[2] + nin[2]
-    g_z = {k: send(nsum.at[3], nin.at[2 + k], z_peer(k)) for k in ORDER[1:]}
-    a_stage2(0)
-    a_line(3)
-    total = nsum[3]
-    for k in g_z:
-        g_z[k].wait_recv()
-        total = total + nin[2 + k]
-    nsum[4] = total
-    gain_out[...] = nsum[4, :, lanes(c)]
-    a_line(0)
-    for k in asz:
-        asz[k].wait_recv()
-    sum_into(a_out, [block(z, x, r).at[:, lanes(c)]] + [az_in.at[k] for k in range(lay.planes - 1)], 16)
+    n_sum.send(0, nsum.at[3])
+    n_sum.arrive(0)
+    nsum[4] = nsum[3] + nin[3]
+    n_sum.send(2, nsum.at[4])
+    n_sum.arrive(2)
+    nsum[5] = nsum[4] + nin[5]
+    gain_out[...] = nsum[5, :, lanes(c)]
+    a_line_sum(0, 3)
+    a_total(0)
     links.flush()
-
-
-def whole_layer(lay, a_shard, f_shard, tokens, cotangent, gains, seg_ids, parents):
+    for part in [dy_line, n_line, d_line, y_line, n_sum] + g_line:
+        part.flush()
+    for copy in outgoing:
+        copy.wait()
+
+
+def whole_layer(lay, blocks, tokens, cotangent, gains, seg_ids, parents):
     vm = lambda *shape: pltpu.VMEM(shape, BF16)
     vf = lambda *shape: pltpu.VMEM(shape, F32)
     M, T, D, W = MODEL_WIDTH, TREE_TOKENS, HEAD_SIZE, lay.width
-    frows = f_shard.shape[1]
+    frows = blocks[3].shape[0]
     hid = lay.lines * lay.cores * frows
     G, per = KEY_VALUE_HEADS, QUERY_HEADS // KEY_VALUE_HEADS
     n, nl, half = lay.planes, lay.lines, frows // 2
-    vmem = pl.BlockSpec(memory_space=pltpu.VMEM)
-    cut, rest = lay.acut, lay.arows - lay.acut
+    vmem, hbm = pl.BlockSpec(memory_space=pltpu.VMEM), pl.BlockSpec(memory_space=pl.ANY)
+    count = 184
     scratch = [
         vm(lay.dp, lay.cores, lay.arows, M),
-        vm(3, hid, M),
+        vm(3, nl, lay.cores, frows, M),
         vm(QUERY_HEADS * D, M),
         vm(2 * G * D, M),
         vm(QUERY_HEADS * D, M),
@@ -624,16 +807,20 @@
         vm(3, half, W),
         vm(3, half, W),
         vm(n, nl, lay.arows, M),
-        vm(n, cut, M),
-        vm(n, nl, rest, W),
-        vm(n, cut, W),
-        vm(n, rest, W),
+        vm(n, lay.arows, M),
+        vm(n, nl, lay.arows, W),
+        vm(n, lay.arows, W),
         vm(n - 1, lay.arows, W),
-        vf(5, 8, M),
+        vf(6, 8, M),
         vf(2 + n, 8, M),
-        pltpu.SemaphoreType.DMA((144,)),
-        pltpu.SemaphoreType.DMA((144,)),
+        vm(T, M),
+        vm(T, M),
+        vf(lay.arows, W),
+        vf(3, frows, W),
+        pltpu.SemaphoreType.DMA((count,)),
+        pltpu.SemaphoreType.DMA((count,)),
         pltpu.SemaphoreType.DMA((6,)),
+        pltpu.SemaphoreType.DMA((8,)),
     ]
     return pl.pallas_call(
         functools.partial(layer_kernel, lay),
@@ -641,50 +828,73 @@
             jax.ShapeDtypeStruct((T, M), BF16),
             jax.ShapeDtypeStruct((T, M), BF16),
             jax.ShapeDtypeStruct((8, W), F32),
-            jax.ShapeDtypeStruct((lay.arows, W), F32),
-            jax.ShapeDtypeStruct((3, frows, W), F32),
-        ),
-        in_specs=[vmem] * 7,
-        out_specs=(vmem,) * 5,
+        )
+        + tuple(jax.ShapeDtypeStruct(b.shape, F32) for b in blocks),
+        in_specs=[hbm, vmem, hbm, hbm, hbm, hbm, vmem, vmem, vmem, vmem, vmem],
+        out_specs=(hbm, hbm, vmem) + (hbm,) * 6,
         scratch_shapes=scratch,
         compiler_params=pltpu.CompilerParams(collective_id=0, has_side_effects=True, vmem_limit_bytes=62 * 2**20),
         name="whole_layer",
-    )(a_shard, f_shard, tokens, cotangent, gains, seg_ids, parents)
+    )(*blocks, tokens, cotangent, gains, seg_ids, parents)
+
+
+def finish_kernel(count, *refs):
+    held, (into, back) = refs[2 * count : 3 * count], refs[3 * count :]
+    first = [pltpu.make_async_copy(refs[i], held[i], into.at[i]) for i in range(count)]
+    last = [pltpu.make_async_copy(held[i], refs[count + i], back.at[i]) for i in range(count)]
+    for copy in first:
+        copy.start()
+    for i in range(count):
+        first[i].wait()
+        last[i].start()
+    for copy in last:
+        copy.wait()
+
+
+def finish(results):
+    hbm = pl.BlockSpec(memory_space=pl.ANY)
+    count = len(results)
+    dma = pltpu.SemaphoreType.DMA((count,))
+    return pl.pallas_call(
+        functools.partial(finish_kernel, count),
+        out_shape=tuple(jax.ShapeDtypeStruct(v.shape, v.dtype) for v in results),
+        in_specs=[hbm] * count,
+        out_specs=(hbm,) * count,
+        scratch_shapes=[pltpu.VMEM(v.shape, v.dtype) for v in results] + [dma, dma],
+        name="finish",
+    )(*results)
 
 
 def body(lay, tokens, cotangent, seg_ids, parents, norm1_gain, w_query, key_value_weight, w_out, norm2_gain, w_gate, w_up, w_down):
     W = lay.width
-    a_shard = jnp.concatenate(
-        [
-            jnp.transpose(w_query, (1, 2, 0)).reshape(lay.qrows, W),
-            jnp.transpose(key_value_weight[:, 0, :]),
-            jnp.zeros((lay.out_at - lay.kv_at - lay.kvrows, W), BF16),
-            w_out.reshape(lay.qrows, W),
-            jnp.zeros((lay.arows - lay.out_at - lay.qrows, W), BF16),
-        ],
-        axis=0,
+    blocks = (
+        jnp.transpose(w_query, (1, 2, 0)).reshape(lay.qrows, W),
+        jnp.transpose(key_value_weight[:, 0, :]),
+        w_out.reshape(lay.qrows, W),
+        w_gate.T,
+        w_up.T,
+        w_down,
     )
-    f_shard = jnp.stack([w_gate.T, w_up.T, w_down], axis=0)
     gains = jnp.concatenate([norm1_gain[None], norm2_gain[None], jnp.zeros((6, W), F32)], axis=0)
-    layer_out, in_grad, gain_sum, a_out, f_out = whole_layer(
-        lay, a_shard, f_shard, tokens, cotangent, gains, seg_ids, parents
+    layer_out, in_grad, gain_sum, query, keyval, out, gate, up, down = whole_layer(
+        lay, blocks, tokens, cotangent, gains, seg_ids, parents
+    )
+    layer_out, in_grad, query, keyval, out, gate, up, down = finish(
+        (layer_out, in_grad, query, keyval, out, gate, up, down)
     )
     heads = QUERY_HEADS // lay.cores
     shape = (heads, HEAD_SIZE // lay.dp, W)
-    query_grad = jnp.transpose(a_out[: lay.qrows].reshape(shape), (2, 0, 1))
-    keyval_grad = jnp.transpose(a_out[lay.kv_at : lay.kv_at + lay.kvrows])[:, None, :]
-    out_grad = a_out[lay.out_at : lay.out_at + lay.qrows].reshape(shape)
     return (
         layer_out,
         in_grad,
         gain_sum[0],
-        query_grad,
-        keyval_grad,
-        out_grad,
+        jnp.transpose(query.reshape(shape), (2, 0, 1)),
+        keyval.T[:, None, :],
+        out.reshape(shape),
         gain_sum[1],
-        f_out[0].T,
-        f_out[1].T,
-        f_out[2],
+        gate.T,
+        up.T,
+        down,
     )
 
 

time: 215 us -> 181 us (0.84)
  Pallas kernels: 198 us -> 177 us
  local copies, waits for them, and re-layouts: 10.4 us -> 2.11 us
  other arithmetic: 4.62 us -> 0.68 us
    pallas_call x1, Pallas kernels: 198 us -> 174 us  [whole_layer(): pl.pallas_call(functools.partial(layer_kernel, lay), out_shape=(jax.Shape...]
    pallas_call x0 -> x1, Pallas kernels: none -> 2.74 us  [finish(): pl.pallas_call(functools.partial(finish_kernel, count), out_shape=tuple((...]
    squeeze x1 -> x0, local copies, waits for them, and re-layouts: 2.69 us -> none  [body(): f_out[2]]
    another operation x1 -> x0, other arithmetic: 2.15 us -> none  [body(): f_shard = jnp.stack([w_gate.T, w_up.T, w_down], axis=0)]
where the time goes in v3:
time: 181 us; the launch traced here: 180 us
  Pallas kernels  177 us (98%)
  local copies, waits for them, and re-layouts  2.11 us (1%)
    pallas_call x1, Pallas kernels, whole_layer(): pl.pallas_call(functools.partial(layer_kernel, lay), out_shape=(jax.Shape...  174 us

profile of v3, /device:TPU:0, one launch (start us, length us, event | category | flops | bytes accessed | tf_op | source)
XLA Modules:
  0.0 180.3 jit_solution(14802236122311279218)
XLA Ops:
  0.6 0.0 copy-start
  0.7 0.0 copy-start.1
  0.7 0.1 pad.2.clone
  0.7 0.6 copy-done
  1.3 0.0 copy-done.1
  1.4 0.7 maximum_maximum_fusion.gain_ref
  2.0 174.1 %whole_layer.1 = (bf16[128,1280]{1,0:T(8,128)(2,1)}, bf16[128,1280]{1,0:T(8,128)(2,1)}, f32[8,640]{1,0:T(8,128)}, f32[80,640]{1,0:T(8,128)}, f32[40,640]{1,0:T(8...) custom-call(bf16[80,640]{1,0:T(8,128)(2,1)} %bitcast.20, ...), custom_call_target="tpu_custom_call" | custom-call | tf_op jit(solution)/shard_map/whole_layer/pallas_call | solution.py:825
  176.1 2.7 %finish.1 = (bf16[128,1280]{1,0:T(8,128)(2,1)}, bf16[128,1280]{1,0:T(8,128)(2,1)}, f32[80,640]{1,0:T(8,128)}, f32[40,640]{1,0:T(8,128)}, f32[80,640]{1,0:T(8,128...) custom-call(bf16[128,1280]{1,0:T(8,128)(2,1)} %get-tuple-element.27.refs_0_, ...), custom_call_target="tpu_custom_call" | custom-call | tf_op jit(solution)/shard_map/finish/pallas_call | solution.py:858
  178.9 1.4 slice_reduce_fusion
  (3 shorter events, 0.0 us)
Async XLA Ops:
  0.6 0.7 copy-start
  0.7 0.7 copy-start.1

commit v4 on v3

--- a/solution.py
+++ b/solution.py
@@ -231,7 +231,7 @@
     lay,
     q_ref, kv_ref, o_ref, gate_ref, up_ref, down_ref, tok_ref, cot_ref, gain_ref, seg_ref, par_ref,
     out_hbm, in_grad_hbm, gain_out, q_hbm, kv_hbm, o_hbm, gate_hbm, up_hbm, down_hbm,
-    ga, gf, wq, wkv, wo, gn, gdy, act, dgate, dup, d_act, gfull, normed, qs, ks, vs, probs, mix, resid,
+    ga, gf, wq, wkv, wo, gn, gdy, act, dgate, dup, d_act, gate_s, down_grad, gfull, normed, qs, ks, vs, probs, mix, resid,
     rot_cos, rot_sin, dq, dk5, dv5, d_part, d_in, y_part, y_in,
     fc_in, f1a, f1b, f2a, f2b, ac_in, a1a, a1b, a2, az_in, nsum, nin,
     out_ref, in_grad_ref, a_out, f_out,
@@ -304,7 +304,11 @@
         Line(lay, links, a_here(i, z), lambda p, i=i: a_here(i, planes[p]), a_here(i, z), a_here(i, z)) for i in range(2)
     ]
     dy_line = Line(lay, links, gdy.at[0], lambda p: gdy.at[p], gdy.at[1], gdy.at[3 - inner])
-    n_line = Line(lay, links, gn.at[0], lambda p: gn.at[p], gn.at[1], gn.at[3 - inner])
+    n_line = []
+    for rows in (pl.ds(0, T // 2), pl.ds(T // 2, T // 2)):
+        n_line.append(
+            Line(lay, links, gn.at[0, rows], lambda p, rows=rows: gn.at[p, rows], gn.at[1, rows], gn.at[3 - inner, rows])
+        )
     d_line, y_line, n_sum = (LineSum(lay, links, landing) for landing in (d_in, y_in, nin.at[pl.ds(3, 3)]))
     g_line = [LineSum(lay, links, az_in.at[:, a_rows(i), :]) for i in range(2)]
 
@@ -360,6 +364,7 @@
 
     a_own(0, 0)
     a_line[0].start()
+    a_own(1, 0)
 
     stream = tok_ref[...].astype(F32)
     rstd1 = lax.rsqrt(jnp.sum(stream * stream, axis=1, keepdims=True) / MODEL_WIDTH + EPS)
@@ -389,46 +394,49 @@
     a_own(0, 1)
     a_relay(0, 0)
     a_line[0].relay(3)
+    a_own(0, 2)
+    a_finish(0, 0)
     a_line[1].start()
-    a_finish(0, 0)
     a_relay(0, 1)
-    a_own(0, 2)
+    a_own(0, 3)
     a_finish(0, 1)
+    a_relay(0, 2)
+    a_line[1].relay(2)
     a_unpack(0, 0)
-    a_own(0, 3)
-    a_line[1].relay(2)
-    a_relay(0, 2)
-    a_own(1, 0)
-    a_finish(0, 2)
     a_line[1].relay(3)
     dy_line.start()
+    a_relay(0, 3)
+    a_own(1, 1)
+    a_own(1, 2)
+    a_finish(0, 2)
     a_unpack(0, 1)
-    a_own(1, 1)
-    a_relay(0, 3)
-    a_own(1, 2)
+    a_finish(0, 3)
     a_unpack(0, 2)
-    a_relay(1, 0)
+    a_unpack(0, 3)
     a_own(1, 3)
-    a_finish(0, 3)
-    a_unpack(0, 3)
 
     fx, fy, frx, fry, fcore = {}, {}, {}, {}, {}
 
     def f_send(w):
-        here = gf.at[w, x, r, :, lanes(c)]
-        fx[w] = send(here, here, x_peer, "gf")
-        fy[w] = send(here, here, y_peer, "gf")
+        for h in range(2):
+            here = gf.at[w, x, r, halves[h], lanes(c)]
+            fx[w, h] = send(here, here, x_peer, "gf")
+            fy[w, 1 - h] = send(gf.at[w, x, r, halves[1 - h], lanes(c)], gf.at[w, x, r, halves[1 - h], lanes(c)], y_peer, "gf")
 
     def f_relay(w):
-        fx[w].wait_recv()
+        fx[w, 0].wait_recv()
         top = gf.at[w, x_other, r, halves[0], lanes(c)]
         fry[w] = send(top, top, y_peer, "gf")
-        fy[w].wait_recv()
+        fy[w, 1].wait_recv()
         low = gf.at[w, x, r, halves[1], lanes(c_other)]
         frx[w] = send(low, low, x_peer, "gf")
+
+    def f_core(w):
+        fy[w, 0].wait_recv()
         fcore[w, 0] = send(gf.at[w, x, r], gf.at[w, x, r], sibling, "gf")
 
     def f_finish(w):
+        fx[w, 1].wait_recv()
         fry[w].wait_recv()
         frx[w].wait_recv()
         fcore[w, 1] = send(gf.at[w, x_other, r], gf.at[w, x_other, r], sibling, "gf")
@@ -444,11 +452,11 @@
         vs[g] = kv[:, kvw + g * D : kvw + (g + 1) * D].astype(BF16)
     allowed4 = jnp.concatenate([allowed] * per, axis=0) > 0.5
     between = {
-        0: [lambda: a_relay(1, 1)],
-        1: [lambda: a_finish(1, 0)],
-        2: [lambda: a_relay(1, 2), lambda: a_unpack(1, 0)],
-        3: [lambda: a_finish(1, 1), lambda: dy_line.relay(2)],
-        4: [lambda: a_relay(1, 3), lambda: [f_send(w) for w in (2, 0, 1)]],
+        0: [lambda: dy_line.relay(2)],
+        1: [lambda: a_relay(1, 0)],
+        2: [lambda: a_relay(1, 1)],
+        3: [lambda: a_relay(1, 2), lambda: a_finish(1, 0)],
+        4: [lambda: a_relay(1, 3), lambda: dy_line.relay(3), lambda: f_send(2), lambda: a_unpack(1, 0)],
     }
     for g in range(groups):
         cols = slice(g * per * D, (g + 1) * per * D)
@@ -462,40 +470,54 @@
         mix[:, cols] = spread_heads(mixed, per).astype(BF16)
         for step in between[g]:
             step()
+    a_finish(1, 1)
     a_unpack(1, 1)
     a_finish(1, 2)
+    f_send(0)
     a_unpack(1, 2)
     a_finish(1, 3)
+    f_relay(2)
     a_unpack(1, 3)
     res = stream + dot_nn(mix[...], wo[...])
     resid[...] = res
     rstd2 = lax.rsqrt(jnp.sum(res * res, axis=1, keepdims=True) / MODEL_WIDTH + EPS)
     gn[0] = (res * rstd2 * gfull[1:2, :]).astype(BF16)
-    n_line.start()
-    dy_line.relay(3)
-    f_relay(2)
+    for part in n_line:
+        part.start()
+    f_send(1)
+    f_core(2)
+    n_line[0].relay(2)
+    n_line[1].relay(2)
     f_relay(0)
+    n_line[0].relay(3)
     f_finish(2)
-    n_line.relay(2)
+    f_core(0)
+    n_line[1].relay(3)
+    f_relay(1)
     for p in line[1:]:
         dy_line.arrive(p)
     f_ready(2)
     n_rows = lay.planes * T
     dy_all = lambda: gdy[...].reshape(n_rows, MODEL_WIDTH)
     d_act[...] = dot_nt(dy_all(), weights(2))
-    f_relay(1)
     f_finish(0)
-    n_line.relay(3)
+    f_core(1)
+    for part in n_line:
+        part.arrive(1)
+        part.arrive(2)
+    f_finish(1)
     f_ready(0)
-    f_finish(1)
+    gate_s[: 3 * T, :] = dot_nt(gn[:3].reshape(3 * T, MODEL_WIDTH), weights(0))
+    for part in n_line:
+        part.arrive(3)
+    gate_s[3 * T :, :] = dot_nt(gn[3], weights(0))
     f_ready(1)
 
     def feed(first, last):
         count = (last - first) * T
         rows = slice(first * T, last * T)
-        n2 = gn[first:last].reshape(count, MODEL_WIDTH)
-        gate = dot_nt(n2, weights(0))
-        up = dot_nt(n2, weights(1))
+        up = dot_nt(gn[first:last].reshape(count, MODEL_WIDTH), weights(1))
+        gate = gate_s[rows, :]
         sig = 1.0 / (1.0 + jnp.exp(-gate))
         silu = gate * sig
         act[rows, :] = (silu * up).astype(BF16)
@@ -503,33 +525,10 @@
         dup[rows, :] = (da * silu).astype(BF16)
         dgate[rows, :] = (da * up * sig * (1.0 + gate * (1.0 - sig))).astype(BF16)
 
-    def back(first, last):
-        count = (last - first) * T
-        rows = slice(first * T, last * T)
+    def back(p):
+        rows = pl.ds(pl.multiple_of(p * T, T), T)
         part = dot_nn(dgate[rows, :], weights(0)) + dot_nn(dup[rows, :], weights(1))
-        d_part[first:last] = part.astype(BF16).reshape(last - first, T, MODEL_WIDTH)
-
-    n_line.arrive(1)
-    n_line.arrive(2)
-    feed(1, 3)
-    back(1, 3)
-
-    @pl.when(inner == 0)
-    def _():
-        d_line.send(0, d_part.at[2])
-        d_line.send(1, d_part.at[1])
-
-    n_line.arrive(3)
-    feed(3, 4)
-    back(3, 4)
-
-    @pl.when(inner == 1)
-    def _():
-        d_line.send(0, d_part.at[3])
-        d_line.send(1, d_part.at[1])
-
-    feed(0, 1)
-    back(0, 1)
+        d_part[p] = part.astype(BF16)
 
     def mirror(line_sum, terms, landing):
         line_sum.arrive(0)
@@ -541,6 +540,9 @@
     for part in a_line:
         part.flush()
     fc, fs1a, fs1b, fs2a, fs2b = {}, {}, {}, {}, {}
+
+    def fg(w):
+        return gf.at[w] if w < 2 else down_grad
 
     def f_grad(w):
         n2 = gn[...].reshape(n_rows, MODEL_WIDTH)
@@ -550,48 +552,54 @@
             grad = dot_tn(dup[...], n2)
         else:
             grad = dot_tn(act[...], dy_all())
-        gf[w] = grad.astype(BF16).reshape(lay.lines, lay.cores, frows, MODEL_WIDTH)
-        fc[w] = send(gf.at[w, :, r_other], fc_in.at[w], sibling)
+        fg(w)[...] = grad.astype(BF16).reshape(lay.lines, lay.cores, frows, MODEL_WIDTH)
+        fc[w] = send(fg(w).at[:, r_other], fc_in.at[w], sibling)
 
     def f_stage1(w):
         fc[w].wait_recv()
         for xx in range(lay.lines):
-            add_into(gf.at[w, xx, r], fc_in.at[w, xx], 32)
-        fs1a[w] = send(gf.at[w, x_other, r, halves[0], :], f1a.at[w], x_peer)
-        fs1b[w] = send(gf.at[w, :, r, halves[1], lanes(c_other)], f1b.at[w], y_peer)
+            add_into(fg(w).at[xx, r], fc_in.at[w, xx], 32)
+        fs1a[w] = send(fg(w).at[x_other, r, halves[0], :], f1a.at[w], x_peer)
+        fs1b[w] = send(fg(w).at[:, r, halves[1], lanes(c_other)], f1b.at[w], y_peer)
 
     def f_stage2(w):
         fs1a[w].wait_recv()
-        add_into(gf.at[w, x, r, halves[0], :], f1a.at[w], 16)
-        fs2a[w] = send(gf.at[w, x, r, halves[0], lanes(c_other)], f2a.at[w], y_peer)
+        add_into(fg(w).at[x, r, halves[0], :], f1a.at[w], 16)
+        fs2a[w] = send(fg(w).at[x, r, halves[0], lanes(c_other)], f2a.at[w], y_peer)
         fs1b[w].wait_recv()
         for xx in range(lay.lines):
-            add_into(gf.at[w, xx, r, halves[1], lanes(c)], f1b.at[w, xx], 16)
-        fs2b[w] = send(gf.at[w, x_other, r, halves[1], lanes(c)], f2b.at[w], x_peer)
+            add_into(fg(w).at[xx, r, halves[1], lanes(c)], f1b.at[w, xx], 16)
+        fs2b[w] = send(fg(w).at[x_other, r, halves[1], lanes(c)], f2b.at[w], x_peer)
 
     def f_total(w, dest):
         fs2a[w].wait_recv()
-        sum_into(f_out.at[w, halves[0], :], [gf.at[w, x, r, halves[0], lanes(c)], f2a.at[w]], 16)
+        sum_into(f_out.at[w, halves[0], :], [fg(w).at[x, r, halves[0], lanes(c)], f2a.at[w]], 16)
         fs2b[w].wait_recv()
-        sum_into(f_out.at[w, halves[1], :], [gf.at[w, x, r, halves[1], lanes(c)], f2b.at[w]], 16)
+        sum_into(f_out.at[w, halves[1], :], [fg(w).at[x, r, halves[1], lanes(c)], f2b.at[w]], 16)
         put(f_out.at[w], dest)
 
+    feed(0, 4)
+    f_grad(2)
+    back(2 + inner)
+    d_line.send(0, d_part.at[2 + inner])
+    back(1)
+    d_line.send(1, d_part.at[1])
+    f_stage1(2)
+    back(3 - inner)
+    back(0)
     f_grad(0)
     f_grad(1)
+    mirror(d_line, d_part, d_in)
     f_stage1(0)
-    mirror(d_line, d_part, d_in)
-    y_all = dot_nn(act[...], weights(2))
-    y_part[...] = y_all.astype(BF16).reshape(lay.planes, T, MODEL_WIDTH)
+    f_stage1(1)
+    f_stage2(2)
+    y_part[...] = dot_nn(act[...], weights(2)).astype(BF16).reshape(lay.planes, T, MODEL_WIDTH)
+    f_stage2(0)
+
+    d_line.arrive(1)
+    d_line.arrive(2)
     y_line.send(0, y_part.at[2 + inner])
     y_line.send(1, y_part.at[1])
-    f_grad(2)
-    f_stage1(1)
-    f_stage1(2)
-    f_stage2(0)
-    f_stage2(1)
-
-    d_line.arrive(1)
-    d_line.arrive(2)
     d_n2 = d_part[0].astype(F32) + d_in[1].astype(F32) + d_in[2].astype(F32)
     res = resid[...]
     rstd2 = lax.rsqrt(jnp.sum(res * res, axis=1, keepdims=True) / MODEL_WIDTH + EPS)
@@ -604,11 +612,11 @@
     def place_heads(source, other, base):
         heads = QUERY_HEADS // lay.cores
         for rr in range(lay.cores):
+            grad = dot_tn(source[:, rr * heads * D : (rr + 1) * heads * D], other)
             for m in range(heads // 2):
-                at = (rr * heads + 2 * m) * D
-                grad = dot_tn(source[:, at : at + 2 * D], other)
+                at = 2 * m * D
                 for dp in range(lay.dp):
-                    tile = jnp.concatenate([grad[dp * 8 : dp * 8 + 8], grad[D + dp * 8 : D + dp * 8 + 8]], axis=0)
+                    tile = jnp.concatenate([grad[at + dp * 8 : at + dp * 8 + 8], grad[at + D + dp * 8 : at + D + dp * 8 + 8]], axis=0)
                     ga[dp, rr, base + m * 16 : base + m * 16 + 16, :] = tile.astype(BF16)
 
     to_plane = (planes[2] + inner * (planes[3] - planes[2]), planes[3] + inner * (planes[2] - planes[3]), planes[1], z)
@@ -624,24 +632,30 @@
     def ends(i):
         return a_rows(i, 0, lay.cuts[i]), a_rows(i, lay.cuts[i], lay.parts[i][1] - lay.cuts[i])
 
+    def landed(i):
+        tops, lows = lay.cuts[0] * i, (lay.parts[0][1] - lay.cuts[0]) * i
+        return pl.ds(tops, lay.cuts[i]), pl.ds(lows, lay.parts[i][1] - lay.cuts[i])
+
     def a_stage1(i, t):
         top, low = ends(i)
+        top_in, low_in = landed(i)
         zz = to_plane[t]
         ac[i, t].wait_recv()
         for xx in range(lay.lines):
             add_into(block(zz, xx, r).at[a_rows(i), :], ac_in.at[t, xx, a_rows(i), :], 16)
-        as1a[i, t] = send(block(zz, x_other, r).at[top, :], a1a.at[t, top, :], x_peer)
-        as1b[i, t] = send(a_pair(zz, r, low).at[:, :, lanes(c_other)], a1b.at[t, :, low, :], y_peer)
+        as1a[i, t] = send(block(zz, x_other, r).at[top, :], a1a.at[t, top_in, :], x_peer)
+        as1b[i, t] = send(a_pair(zz, r, low).at[:, :, lanes(c_other)], a1b.at[t, :, low_in, :], y_peer)
 
     def a_stage2(i, t):
         top, low = ends(i)
+        top_in, low_in = landed(i)
         zz = to_plane[t]
         as1a[i, t].wait_recv()
-        add_into(block(zz, x, r).at[top, :], a1a.at[t, top, :], 16)
+        add_into(block(zz, x, r).at[top, :], a1a.at[t, top_in, :], 16)
         as2a[i, t] = send(block(zz, x, r).at[top, lanes(c_other)], a2.at[t, top, :], y_peer)
         as1b[i, t].wait_recv()
         for xx in range(lay.lines):
-            add_into(block(zz, xx, r).at[low, lanes(c)], a1b.at[t, xx, low, :], 16)
+            add_into(block(zz, xx, r).at[low, lanes(c)], a1b.at[t, xx, low_in, :], 16)
         as2b[i, t] = send(block(zz, x_other, r).at[low, lanes(c)], a2.at[t, low, :], x_peer)
 
     def a_line_sum(i, t):
@@ -649,11 +663,14 @@
         as2a[i, t].wait_recv()
         as2b[i, t].wait_recv()
         add_into(here, a2.at[t, a_rows(i), :], 16)
-        if t == 1:
-            g_line[i].arrive(0)
-            add_into(here, az_in.at[0, a_rows(i), :], 16)
-        if t < 3:
+        if t in (0, 2):
             g_line[i].send((0, 2, 1)[t], here)
+
+    def a_mirror(i):
+        here = a_here(i, to_plane[1])
+        g_line[i].arrive(0)
+        add_into(here, az_in.at[0, a_rows(i), :], 16)
+        g_line[i].send(2, here)
 
     def a_total(i):
         g_line[i].arrive(1)
@@ -668,7 +685,7 @@
 
     place_heads(mix, d_attn, lay.out_at)
     a_core_sums(1)
-    f_stage2(2)
+    f_stage2(1)
     between = {
         0: [lambda: a_stage1(1, 0), lambda: a_stage1(1, 1)],
         1: [lambda: a_stage1(1, 2), lambda: a_stage1(1, 3)],
@@ -701,62 +718,64 @@
             tile = jnp.concatenate([grad[dp * lay.kvrows : (dp + 1) * lay.kvrows], pad], axis=0)
             ga[dp, rr, lay.kv_at : lay.out_at, :] = tile.astype(BF16)
     a_core_sums(0)
-    a_stage2(1, 2)
-    a_stage2(1, 3)
-    a_stage1(0, 0)
-    a_line_sum(1, 0)
-    a_stage1(0, 1)
-    a_line_sum(1, 1)
     d_normed = dot_nn(dq[...], wq[...]) + dot_nn(dk, wkv[:kvw, :]) + dot_nn(dv, wkv[kvw:, :])
-    a_stage2(0, 0)
-    a_stage1(0, 2)
-    a_line_sum(1, 2)
     stream = tok_ref[...].astype(F32)
     rstd1 = lax.rsqrt(jnp.sum(stream * stream, axis=1, keepdims=True) / MODEL_WIDTH + EPS)
     gain1_grad = jnp.sum(d_normed * stream * rstd1, axis=0, keepdims=True)
     nsum[0] = jnp.concatenate([gain1_grad, gain2_grad, jnp.zeros((6, MODEL_WIDTH), F32)], axis=0)
     g_core = send(nsum.at[0], nin.at[0], sibling)
-    a_stage2(0, 1)
-    a_stage1(0, 3)
+    a_stage2(1, 2)
+    a_stage2(1, 3)
+    a_stage1(0, 0)
+    a_line_sum(1, 0)
+    g_core.wait_recv()
+    nsum[1] = nsum[0] + nin[0]
+    g_x = send(nsum.at[1], nin.at[1], x_peer)
+    a_stage1(0, 1)
+    a_line_sum(1, 1)
+    a_stage2(0, 0)
+    g_x.wait_recv()
+    nsum[2] = nsum[1] + nin[1]
+    g_y = send(nsum.at[2], nin.at[2], y_peer)
+    a_stage1(0, 2)
+    a_line_sum(1, 2)
     scaled1 = d_normed * gfull[0:1, :]
     inner1 = jnp.sum(scaled1 * stream, axis=1, keepdims=True)
     in_grad = d_res + rstd1 * scaled1 - stream * (rstd1 * rstd1 * rstd1 * inner1 / MODEL_WIDTH)
     in_grad_ref[...] = in_grad.astype(BF16)
     put(in_grad_ref, in_grad_hbm)
+    a_stage2(0, 1)
+    g_y.wait_recv()
+    nsum[3] = nsum[2] + nin[2]
+    n_sum.send(0, nsum.at[3])
+    a_stage1(0, 3)
     a_line_sum(0, 0)
-    a_stage2(0, 2)
-    g_core.wait_recv()
-    nsum[1] = nsum[0] + nin[0]
-    g_x = send(nsum.at[1], nin.at[1], x_peer)
-    a_line_sum(1, 3)
+    a_mirror(1)
     y_line.arrive(1)
     y_line.arrive(2)
     y = resid[...] + y_part[0].astype(F32) + y_in[1].astype(F32) + y_in[2].astype(F32)
     out_ref[...] = y.astype(BF16)
     put(out_ref, out_hbm)
+    a_stage2(0, 2)
     a_line_sum(0, 1)
-    a_stage2(0, 3)
-    g_x.wait_recv()
-    nsum[2] = nsum[1] + nin[1]
-    g_y = send(nsum.at[2], nin.at[2], y_peer)
-    f_total(0, gate_hbm)
-    f_total(1, up_hbm)
-    f_total(2, down_hbm)
-    a_total(1)
-    a_line_sum(0, 2)
-    g_y.wait_recv()
-    nsum[3] = nsum[2] + nin[2]
-    n_sum.send(0, nsum.at[3])
     n_sum.arrive(0)
     nsum[4] = nsum[3] + nin[3]
     n_sum.send(2, nsum.at[4])
+    a_line_sum(1, 3)
+    f_total(2, down_hbm)
+    a_mirror(0)
+    a_stage2(0, 3)
+    a_line_sum(0, 2)
+    f_total(0, gate_hbm)
+    f_total(1, up_hbm)
+    a_total(1)
     n_sum.arrive(2)
     nsum[5] = nsum[4] + nin[5]
     gain_out[...] = nsum[5, :, lanes(c)]
     a_line_sum(0, 3)
     a_total(0)
     links.flush()
-    for part in [dy_line, n_line, d_line, y_line, n_sum] + g_line:
+    for part in [dy_line, d_line, y_line, n_sum] + n_line + g_line:
         part.flush()
     for copy in outgoing:
         copy.wait()
@@ -771,7 +790,7 @@
     G, per = KEY_VALUE_HEADS, QUERY_HEADS // KEY_VALUE_HEADS
     n, nl, half = lay.planes, lay.lines, frows // 2
     vmem, hbm = pl.BlockSpec(memory_space=pltpu.VMEM), pl.BlockSpec(memory_space=pl.ANY)
-    count = 184
+    count = 200
     scratch = [
         vm(lay.dp, lay.cores, lay.arows, M),
         vm(3, nl, lay.cores, frows, M),
@@ -784,6 +803,8 @@
         vm(n * T, hid),
         vm(n * T, hid),
         vf(n * T, hid),
+        vf(n * T, hid),
+        vm(nl, lay.cores, frows, M),
         vf(8, M),
         vm(T, M),
         vm(G, per * T, D),
@@ -807,8 +828,8 @@
         vm(3, half, W),
         vm(3, half, W),
         vm(n, nl, lay.arows, M),
-        vm(n, lay.arows, M),
-        vm(n, nl, lay.arows, W),
+        vm(n, sum(lay.cuts), M),
+        vm(n, nl, lay.arows - sum(lay.cuts), W),
         vm(n, lay.arows, W),
         vm(n - 1, lay.arows, W),
         vf(6, 8, M),

time: 181 us -> 163 us (0.901)
  Pallas kernels: 177 us -> 159 us
    pallas_call x1, Pallas kernels: 174 us -> 157 us  [whole_layer(): pl.pallas_call(functools.partial(layer_kernel, lay), out_shape=(jax.Shape...]
where the time goes in v4:
time: 163 us
  Pallas kernels  159 us (98%)
  local copies, waits for them, and re-layouts  2.11 us (1%)
    pallas_call x1, Pallas kernels, whole_layer(): pl.pallas_call(functools.partial(layer_kernel, lay), out_shape=(jax.Shape...  157 us

profile of v4, /device:TPU:0, one launch (start us, length us, event | category | flops | bytes accessed | tf_op | source)
XLA Modules:
  0.0 163.0 jit_solution(16647941259939547190)
XLA Ops:
  0.6 0.0 copy-start
  0.7 0.0 copy-start.1
  0.7 0.1 pad.2.clone
  0.7 0.6 copy-done
  1.3 0.0 copy-done.1
  1.4 0.7 maximum_maximum_fusion.gain_ref
  2.0 156.7 %whole_layer.1 = (bf16[128,1280]{1,0:T(8,128)(2,1)}, bf16[128,1280]{1,0:T(8,128)(2,1)}, f32[8,640]{1,0:T(8,128)}, f32[80,640]{1,0:T(8,128)}, f32[40,640]{1,0:T(8...) custom-call(bf16[80,640]{1,0:T(8,128)(2,1)} %bitcast.20, ...), custom_call_target="tpu_custom_call" | custom-call | tf_op jit(solution)/shard_map/whole_layer/pallas_call | solution.py:846
  158.8 2.7 %finish.1 = (bf16[128,1280]{1,0:T(8,128)(2,1)}, bf16[128,1280]{1,0:T(8,128)(2,1)}, f32[80,640]{1,0:T(8,128)}, f32[40,640]{1,0:T(8,128)}, f32[80,640]{1,0:T(8,128...) custom-call(bf16[128,1280]{1,0:T(8,128)(2,1)} %get-tuple-element.27.refs_0_, ...), custom_call_target="tpu_custom_call" | custom-call | tf_op jit(solution)/shard_map/finish/pallas_call | solution.py:879
  161.5 1.4 slice_reduce_fusion
  (3 shorter events, 0.0 us)
Async XLA Ops:
  0.6 0.7 copy-start
  0.7 0.7 copy-start.1

commit v5 on v4

--- a/solution.py
+++ b/solution.py
@@ -57,11 +57,14 @@
         return (z * self.lines + x, r, c)
 
 
-def greet(lay, peers):
+def greet(peers):
     barrier = pltpu.get_barrier_semaphore()
     for peer in peers:
         pl.semaphore_signal(barrier, inc=1, device_id=peer, device_id_type=MESH)
-    pl.semaphore_wait(barrier, len(peers))
+
+
+def greeted(peers):
+    pl.semaphore_wait(pltpu.get_barrier_semaphore(), len(peers))
 
 
 def dot_nt(left, right):
@@ -229,12 +232,12 @@
 
 def layer_kernel(
     lay,
-    q_ref, kv_ref, o_ref, gate_ref, up_ref, down_ref, tok_ref, cot_ref, gain_ref, seg_ref, par_ref,
-    out_hbm, in_grad_hbm, gain_out, q_hbm, kv_hbm, o_hbm, gate_hbm, up_hbm, down_hbm,
-    ga, gf, wq, wkv, wo, gn, gdy, act, dgate, dup, d_act, gate_s, down_grad, gfull, normed, qs, ks, vs, probs, mix, resid,
-    rot_cos, rot_sin, dq, dk5, dv5, d_part, d_in, y_part, y_in,
+    q_ref, kv_ref, o_ref, gate_ref, up_ref, down_ref, tok_ref, cot_ref, gain1_ref, gain2_ref, seg_ref, par_ref,
+    out_hbm, in_grad_hbm, gain_hbm, q_hbm, kv_hbm, o_hbm, gate_hbm, up_hbm, down_hbm,
+    ga, gf, wq, wkv, wo, gn, gdy, act, dgate, dup, d_act, gate_s, down_grad, gate_grad, gfull, normed, qs, ks, vs, probs, mix, resid,
+    rot_cos, rot_sin, dq, dkv, dk5, dv5, d_in, y_in,
     fc_in, f1a, f1b, f2a, f2b, ac_in, a1a, a1b, a2, az_in, nsum, nin,
-    out_ref, in_grad_ref, a_out, f_out,
+    out_ref, in_grad_ref, gain_out,
     send_sems, recv_sems, own_sems, out_sems,
 ):
     z, x, r, c = lay.here()
@@ -269,6 +272,9 @@
     halves = (pl.ds(0, half), pl.ds(half, half))
     weights = lambda w: gf[w].reshape(hid, MODEL_WIDTH)
 
+    peers = [lay.device(planes[p], x, r, c) for p in line[1:]] + [x_peer, y_peer, sibling]
+    greet(peers)
+
     mine = block(z, x, r).at[:, lanes(c)]
     f_refs = (gate_ref, up_ref, down_ref)
     own = [
@@ -281,16 +287,18 @@
     for copy in own:
         copy.start()
     pad = jnp.zeros((lay.out_at - lay.kv_at - lay.kvrows, W), BF16)
+    gfull[:, lanes(c)] = jnp.concatenate(
+        [gain1_ref[...].reshape(1, W), gain2_ref[...].reshape(1, W), jnp.zeros((6, W), F32)], axis=0
+    )
     mine[lay.kv_at : lay.out_at, :] = jnp.concatenate([kv_ref[...], pad], axis=0)
     if lay.arows > lay.out_at + lay.qrows:
         mine[lay.out_at + lay.qrows :, :] = jnp.zeros((lay.arows - lay.out_at - lay.qrows, W), BF16)
 
-    greet(lay, [lay.device(planes[p], x, r, c) for p in line[1:]] + [x_peer, y_peer, sibling])
+    greeted(peers)
     for copy in own[:2]:
         copy.wait()
 
-    gfull[:, lanes(c)] = gain_ref[...]
-    gain_y = send(gain_ref, gfull.at[:, lanes(c)], y_peer)
+    gain_y = send(gfull.at[:, lanes(c)], gfull.at[:, lanes(c)], y_peer)
     ax, ay, arx, ary, acore = {}, {}, {}, {}, {}
 
     def a_rows(part, first=0, rows=None):
@@ -390,30 +398,8 @@
     gain_y.wait_recv()
     normed[...] = (stream * rstd1 * gfull[0:1, :]).astype(BF16)
 
-    a_line[0].relay(2)
-    a_own(0, 1)
-    a_relay(0, 0)
-    a_line[0].relay(3)
-    a_own(0, 2)
-    a_finish(0, 0)
-    a_line[1].start()
-    a_relay(0, 1)
-    a_own(0, 3)
-    a_finish(0, 1)
-    a_relay(0, 2)
-    a_line[1].relay(2)
-    a_unpack(0, 0)
-    a_line[1].relay(3)
-    dy_line.start()
-    a_relay(0, 3)
-    a_own(1, 1)
-    a_own(1, 2)
-    a_finish(0, 2)
-    a_unpack(0, 1)
-    a_finish(0, 3)
-    a_unpack(0, 2)
-    a_unpack(0, 3)
-    a_own(1, 3)
+    def a_step(i, p):
+        a_line[i].relay(p)
 
     fx, fy, frx, fry, fcore = {}, {}, {}, {}, {}
 
@@ -445,20 +431,16 @@
         fcore[w, 0].wait_recv()
         fcore[w, 1].wait_recv()
 
-    kv = dot_nt(normed[...], wkv[...])
-    turned = turn(kv, rot_cos[...], rot_sin[...])
-    for g in range(groups):
-        ks[g] = turned[:, g * D : (g + 1) * D].astype(BF16)
-        vs[g] = kv[:, kvw + g * D : kvw + (g + 1) * D].astype(BF16)
     allowed4 = jnp.concatenate([allowed] * per, axis=0) > 0.5
-    between = {
-        0: [lambda: dy_line.relay(2)],
-        1: [lambda: a_relay(1, 0)],
-        2: [lambda: a_relay(1, 1)],
-        3: [lambda: a_relay(1, 2), lambda: a_finish(1, 0)],
-        4: [lambda: a_relay(1, 3), lambda: dy_line.relay(3), lambda: f_send(2), lambda: a_unpack(1, 0)],
-    }
-    for g in range(groups):
+
+    def kv_project():
+        kv = dot_nt(normed[...], wkv[...])
+        turned = turn(kv, rot_cos[...], rot_sin[...])
+        for g in range(groups):
+            ks[g] = turned[:, g * D : (g + 1) * D].astype(BF16)
+            vs[g] = kv[:, kvw + g * D : kvw + (g + 1) * D].astype(BF16)
+
+    def forward(g):
         cols = slice(g * per * D, (g + 1) * per * D)
         pre = turn(dot_nt(normed[...], wq[cols, :]), rot_cos[...], rot_sin[...])
         qs[g] = stack_heads(pre, per).astype(BF16)
@@ -468,50 +450,34 @@
         probs[g] = share
         mixed = dot_nn(share.astype(BF16), vs[g])
         mix[:, cols] = spread_heads(mixed, per).astype(BF16)
-        for step in between[g]:
-            step()
-    a_finish(1, 1)
-    a_unpack(1, 1)
-    a_finish(1, 2)
-    f_send(0)
-    a_unpack(1, 2)
-    a_finish(1, 3)
-    f_relay(2)
-    a_unpack(1, 3)
-    res = stream + dot_nn(mix[...], wo[...])
-    resid[...] = res
-    rstd2 = lax.rsqrt(jnp.sum(res * res, axis=1, keepdims=True) / MODEL_WIDTH + EPS)
-    gn[0] = (res * rstd2 * gfull[1:2, :]).astype(BF16)
-    for part in n_line:
-        part.start()
-    f_send(1)
-    f_core(2)
-    n_line[0].relay(2)
-    n_line[1].relay(2)
-    f_relay(0)
-    n_line[0].relay(3)
-    f_finish(2)
-    f_core(0)
-    n_line[1].relay(3)
-    f_relay(1)
-    for p in line[1:]:
-        dy_line.arrive(p)
-    f_ready(2)
+
+    def out_project():
+        res = stream + dot_nn(mix[...], wo[...])
+        resid[...] = res
+        rstd2 = lax.rsqrt(jnp.sum(res * res, axis=1, keepdims=True) / MODEL_WIDTH + EPS)
+        gn[0] = (res * rstd2 * gfull[1:2, :]).astype(BF16)
+
+    def n_start():
+        for part in n_line:
+            part.start()
+
+    def n_arrive(*positions):
+        for part in n_line:
+            for p in positions:
+                part.arrive(p)
+
+    def dy_arrive():
+        for p in line[1:]:
+            dy_line.arrive(p)
+
     n_rows = lay.planes * T
     dy_all = lambda: gdy[...].reshape(n_rows, MODEL_WIDTH)
-    d_act[...] = dot_nt(dy_all(), weights(2))
-    f_finish(0)
-    f_core(1)
-    for part in n_line:
-        part.arrive(1)
-        part.arrive(2)
-    f_finish(1)
-    f_ready(0)
-    gate_s[: 3 * T, :] = dot_nt(gn[:3].reshape(3 * T, MODEL_WIDTH), weights(0))
-    for part in n_line:
-        part.arrive(3)
-    gate_s[3 * T :, :] = dot_nt(gn[3], weights(0))
-    f_ready(1)
+
+    def hidden_back():
+        d_act[...] = dot_nt(dy_all(), weights(2))
+
+    def gates(first, last):
+        gate_s[first * T : last * T, :] = dot_nt(gn[first:last].reshape((last - first) * T, MODEL_WIDTH), weights(0))
 
     def feed(first, last):
         count = (last - first) * T
@@ -525,6 +491,8 @@
         dup[rows, :] = (da * silu).astype(BF16)
         dgate[rows, :] = (da * up * sig * (1.0 + gate * (1.0 - sig))).astype(BF16)
 
+    d_part = gdy
+
     def back(p):
         rows = pl.ds(pl.multiple_of(p * T, T), T)
         part = dot_nn(dgate[rows, :], weights(0)) + dot_nn(dup[rows, :], weights(1))
@@ -536,13 +504,15 @@
         terms[p] = (terms[p].astype(F32) + landing[0].astype(F32)).astype(BF16)
         line_sum.send(2, terms.at[p])
 
-    links.flush("ga", "gf")
-    for part in a_line:
-        part.flush()
+    def release():
+        links.flush("ga", "gf")
+        for part in a_line:
+            part.flush()
+
     fc, fs1a, fs1b, fs2a, fs2b = {}, {}, {}, {}, {}
 
     def fg(w):
-        return gf.at[w] if w < 2 else down_grad
+        return (gate_grad, gf.at[1], down_grad)[w]
 
     def f_grad(w):
         n2 = gn[...].reshape(n_rows, MODEL_WIDTH)
@@ -553,71 +523,78 @@
         else:
             grad = dot_tn(act[...], dy_all())
         fg(w)[...] = grad.astype(BF16).reshape(lay.lines, lay.cores, frows, MODEL_WIDTH)
-        fc[w] = send(fg(w).at[:, r_other], fc_in.at[w], sibling)
+        for xx in (x_other, x):
+            fc[w, xx is x] = send(fg(w).at[xx, r_other], fc_in.at[w, xx], sibling)
 
     def f_stage1(w):
-        fc[w].wait_recv()
-        for xx in range(lay.lines):
+        for xx in (x_other, x):
+            fc[w, xx is x].wait_recv()
             add_into(fg(w).at[xx, r], fc_in.at[w, xx], 32)
-        fs1a[w] = send(fg(w).at[x_other, r, halves[0], :], f1a.at[w], x_peer)
-        fs1b[w] = send(fg(w).at[:, r, halves[1], lanes(c_other)], f1b.at[w], y_peer)
+            if xx is x_other:
+                fs1a[w] = send(fg(w).at[xx, r, halves[0], :], f1a.at[w], x_peer)
+            fs1b[w, xx is x] = send(fg(w).at[xx, r, halves[1], lanes(c_other)], f1b.at[w, xx], y_peer)
 
     def f_stage2(w):
         fs1a[w].wait_recv()
         add_into(fg(w).at[x, r, halves[0], :], f1a.at[w], 16)
         fs2a[w] = send(fg(w).at[x, r, halves[0], lanes(c_other)], f2a.at[w], y_peer)
-        fs1b[w].wait_recv()
-        for xx in range(lay.lines):
+        for xx in (x_other, x):
+            fs1b[w, xx is x].wait_recv()
             add_into(fg(w).at[xx, r, halves[1], lanes(c)], f1b.at[w, xx], 16)
         fs2b[w] = send(fg(w).at[x_other, r, halves[1], lanes(c)], f2b.at[w], x_peer)
 
+    f_out = [d_act.at[pl.ds(i * frows, frows), pl.ds(0, W)] for i in range(2)] + [gate_s.at[pl.ds(0, frows), pl.ds(0, W)]]
+
     def f_total(w, dest):
         fs2a[w].wait_recv()
-        sum_into(f_out.at[w, halves[0], :], [fg(w).at[x, r, halves[0], lanes(c)], f2a.at[w]], 16)
+        total = f_out[w]
+        sum_into(total.at[halves[0], :], [fg(w).at[x, r, halves[0], lanes(c)], f2a.at[w]], 16)
         fs2b[w].wait_recv()
-        sum_into(f_out.at[w, halves[1], :], [fg(w).at[x, r, halves[1], lanes(c)], f2b.at[w]], 16)
-        put(f_out.at[w], dest)
-
-    feed(0, 4)
-    f_grad(2)
-    back(2 + inner)
-    d_line.send(0, d_part.at[2 + inner])
-    back(1)
-    d_line.send(1, d_part.at[1])
-    f_stage1(2)
-    back(3 - inner)
-    back(0)
-    f_grad(0)
-    f_grad(1)
-    mirror(d_line, d_part, d_in)
-    f_stage1(0)
-    f_stage1(1)
-    f_stage2(2)
-    y_part[...] = dot_nn(act[...], weights(2)).astype(BF16).reshape(lay.planes, T, MODEL_WIDTH)
-    f_stage2(0)
-
-    d_line.arrive(1)
-    d_line.arrive(2)
-    y_line.send(0, y_part.at[2 + inner])
-    y_line.send(1, y_part.at[1])
-    d_n2 = d_part[0].astype(F32) + d_in[1].astype(F32) + d_in[2].astype(F32)
-    res = resid[...]
-    rstd2 = lax.rsqrt(jnp.sum(res * res, axis=1, keepdims=True) / MODEL_WIDTH + EPS)
-    gain2_grad = jnp.sum(d_n2 * res * rstd2, axis=0, keepdims=True)
-    scaled2 = d_n2 * gfull[1:2, :]
-    inner2 = jnp.sum(scaled2 * res, axis=1, keepdims=True)
-    d_res = cot_ref[...].astype(F32) + rstd2 * scaled2 - res * (rstd2 * rstd2 * rstd2 * inner2 / MODEL_WIDTH)
-    d_attn = d_res.astype(BF16)
-
-    def place_heads(source, other, base):
+        sum_into(total.at[halves[1], :], [fg(w).at[x, r, halves[1], lanes(c)], f2b.at[w]], 16)
+        put(total, dest)
+
+    y_part = gn
+
+    def y_terms():
+        for part in n_line:
+            part.flush()
+        y_part[...] = dot_nn(act[...], weights(2)).astype(BF16).reshape(lay.planes, T, MODEL_WIDTH)
+
+    def y_send():
+        y_line.send(0, y_part.at[2 + inner])
+        y_line.send(1, y_part.at[1])
+
+    def y_total():
+        y_line.arrive(1)
+        y_line.arrive(2)
+        y = resid[...] + y_part[0].astype(F32) + y_in[1].astype(F32) + y_in[2].astype(F32)
+        out_ref[...] = y.astype(BF16)
+        put(out_ref, out_hbm)
+
+    kept = {}
+
+    def residual_back():
+        d_line.arrive(1)
+        d_line.arrive(2)
+        d_n2 = d_part[0].astype(F32) + d_in[1].astype(F32) + d_in[2].astype(F32)
+        res = resid[...]
+        rstd2 = lax.rsqrt(jnp.sum(res * res, axis=1, keepdims=True) / MODEL_WIDTH + EPS)
+        gain2_grad = jnp.sum(d_n2 * res * rstd2, axis=0, keepdims=True)
+        scaled2 = d_n2 * gfull[1:2, :]
+        inner2 = jnp.sum(scaled2 * res, axis=1, keepdims=True)
+        d_res = cot_ref[...].astype(F32) + rstd2 * scaled2 - res * (rstd2 * rstd2 * rstd2 * inner2 / MODEL_WIDTH)
+        d_attn = d_res.astype(BF16)
+
+        kept.update(d_res=d_res, d_attn=d_attn, gain2_grad=gain2_grad)
+
+    def place_heads(source, other, base, rr):
         heads = QUERY_HEADS // lay.cores
-        for rr in range(lay.cores):
-            grad = dot_tn(source[:, rr * heads * D : (rr + 1) * heads * D], other)
-            for m in range(heads // 2):
-                at = 2 * m * D
-                for dp in range(lay.dp):
-                    tile = jnp.concatenate([grad[at + dp * 8 : at + dp * 8 + 8], grad[at + D + dp * 8 : at + D + dp * 8 + 8]], axis=0)
-                    ga[dp, rr, base + m * 16 : base + m * 16 + 16, :] = tile.astype(BF16)
+        grad = dot_tn(source[:, pl.ds(pl.multiple_of(rr * heads * D, 128), heads * D)], other)
+        for m in range(heads // 2):
+            at = 2 * m * D
+            for dp in range(lay.dp):
+                tile = jnp.concatenate([grad[at + dp * 8 : at + dp * 8 + 8], grad[at + D + dp * 8 : at + D + dp * 8 + 8]], axis=0)
+                ga[dp, rr, base + m * 16 : base + m * 16 + 16, :] = tile.astype(BF16)
 
     to_plane = (planes[2] + inner * (planes[3] - planes[2]), planes[3] + inner * (planes[2] - planes[3]), planes[1], z)
     ac, as1a, as1b, as2a, as2b = {}, {}, {}, {}, {}
@@ -672,6 +649,8 @@
         add_into(here, az_in.at[0, a_rows(i), :], 16)
         g_line[i].send(2, here)
 
+    a_out = gate_s.at[pl.ds(frows, lay.arows), pl.ds(0, W)]
+
     def a_total(i):
         g_line[i].arrive(1)
         g_line[i].arrive(2)
@@ -683,19 +662,9 @@
         else:
             put(a_out.at[pl.ds(lay.out_at, lay.qrows), :], o_hbm)
 
-    place_heads(mix, d_attn, lay.out_at)
-    a_core_sums(1)
-    f_stage2(1)
-    between = {
-        0: [lambda: a_stage1(1, 0), lambda: a_stage1(1, 1)],
-        1: [lambda: a_stage1(1, 2), lambda: a_stage1(1, 3)],
-        2: [lambda: mirror(y_line, y_part, y_in)],
-        3: [lambda: a_stage2(1, 0)],
-        4: [lambda: a_stage2(1, 1)],
-    }
-    for g in range(groups):
+    def backward(g):
         cols = slice(g * per * D, (g + 1) * per * D)
-        dms = stack_heads(dot_nt(d_attn, wo[cols, :]), per).astype(BF16)
+        dms = stack_heads(dot_nt(kept["d_attn"], wo[cols, :]), per).astype(BF16)
         share = probs[g]
         dp_ = dot_nt(dms, vs[g])
         delta = jnp.sum(share * dp_, axis=1, keepdims=True)
@@ -704,78 +673,208 @@
         dq[:, cols] = turn(d_query, rot_cos[...], -rot_sin[...]).astype(BF16)
         dk5[g] = dot_tn(ds_, qs[g]) * scale
         dv5[g] = dot_tn(share.astype(BF16), dms)
-        for step in between[g]:
-            step()
-    zeros = jnp.zeros((T, D), F32)
-    dk_all = jnp.concatenate([dk5[g] for g in range(groups)] + [zeros], axis=1)
-    dk = turn(dk_all, rot_cos[...], -rot_sin[...])[:, :kvw].astype(BF16)
-    dv = jnp.concatenate([dv5[g] for g in range(groups)], axis=1).astype(BF16)
-    place_heads(dq, normed[...], 0)
-    for rr, rows in enumerate((dk, dv)):
-        grad = dot_tn(rows, normed[...])
+
+    def keys_back():
+        zeros = jnp.zeros((T, D), F32)
+        dk_all = jnp.concatenate([dk5[g] for g in range(groups)] + [zeros], axis=1)
+        dkv[0] = turn(dk_all, rot_cos[...], -rot_sin[...])[:, :kvw].astype(BF16)
+        dkv[1] = jnp.concatenate([dv5[g] for g in range(groups)], axis=1).astype(BF16)
+
+
+    def place_kv(rr):
+        grad = dot_tn(dkv[rr], normed[...])
         pad = jnp.zeros((lay.out_at - lay.kv_at - lay.kvrows, MODEL_WIDTH), F32)
         for dp in range(lay.dp):
             tile = jnp.concatenate([grad[dp * lay.kvrows : (dp + 1) * lay.kvrows], pad], axis=0)
             ga[dp, rr, lay.kv_at : lay.out_at, :] = tile.astype(BF16)
+
+    def input_back():
+        d_normed = dot_nn(dq[...], wq[...]) + dot_nn(dkv[0], wkv[:kvw, :]) + dot_nn(dkv[1], wkv[kvw:, :])
+        rows = tok_ref[...].astype(F32)
+        rstd = lax.rsqrt(jnp.sum(rows * rows, axis=1, keepdims=True) / MODEL_WIDTH + EPS)
+        gain1_grad = jnp.sum(d_normed * rows * rstd, axis=0, keepdims=True)
+        nsum[0] = jnp.concatenate([gain1_grad, kept["gain2_grad"], jnp.zeros((6, MODEL_WIDTH), F32)], axis=0)
+        scaled1 = d_normed * gfull[0:1, :]
+        inner1 = jnp.sum(scaled1 * rows, axis=1, keepdims=True)
+        in_grad = kept["d_res"] + rstd * scaled1 - rows * (rstd * rstd * rstd * inner1 / MODEL_WIDTH)
+        in_grad_ref[...] = in_grad.astype(BF16)
+        put(in_grad_ref, in_grad_hbm)
+        kept["gains"] = send(nsum.at[0], nin.at[0], sibling)
+
+    def gains_core():
+        kept["gains"].wait_recv()
+        nsum[1] = nsum[0] + nin[0]
+        n_sum.send(0, nsum.at[1])
+
+    def gains_side():
+        n_sum.arrive(0)
+        nsum[2] = nsum[1] + nin[3]
+        n_sum.send(2, nsum.at[2])
+
+    def gains_mirror():
+        n_sum.arrive(2)
+        nsum[3] = nsum[2] + nin[5]
+        kept["gains"] = send(nsum.at[3], nin.at[1], x_peer)
+
+    def gains_x():
+        kept["gains"].wait_recv()
+        nsum[4] = nsum[3] + nin[1]
+        kept["gains"] = send(nsum.at[4], nin.at[2], y_peer)
+
+    def gains_y():
+        kept["gains"].wait_recv()
+        nsum[5] = nsum[4] + nin[2]
+        gain_out[...] = nsum[5, :, lanes(c)]
+        put(gain_out, gain_hbm)
+
+    a_step(0, 2)
+    a_line[1].start()
+    a_own(0, 1)
+    a_relay(0, 0)
+    a_step(0, 3)
+    a_relay(0, 1)
+    dy_line.start()
+    a_own(0, 2)
+    a_step(1, 3)
+    a_step(1, 2)
+    a_own(0, 3)
+    a_relay(0, 2)
+    a_own(1, 1)
+    dy_line.relay(2)
+    a_relay(1, 0)
+    a_relay(0, 3)
+    a_own(1, 3)
+    a_finish(0, 1)
+    a_finish(0, 2)
+    a_own(1, 2)
+    a_unpack(0, 1)
+    dy_line.relay(3)
+    a_finish(0, 3)
+    a_finish(0, 0)
+    a_relay(1, 1)
+    a_finish(1, 0)
+    a_unpack(0, 2)
+    a_relay(1, 2)
+    a_relay(1, 3)
+    a_unpack(0, 0)
+    a_unpack(0, 3)
+    a_finish(1, 1)
+    kv_project()
+    f_send(0)
+    a_unpack(1, 1)
+    a_finish(1, 2)
+    a_unpack(1, 0)
+    f_send(2)
+    forward(3)
+    a_finish(1, 3)
+    a_unpack(1, 2)
+    forward(1)
+    forward(4)
+    forward(0)
+    a_unpack(1, 3)
+    forward(2)
+    out_project()
+    n_start()
+    f_relay(2)
+    f_send(1)
+    f_relay(0)
+    n_line[0].relay(2)
+    f_core(0)
+    f_finish(2)
+    n_line[1].relay(2)
+    dy_arrive()
+    f_relay(1)
+    n_line[0].relay(3)
+    f_core(2)
+    n_arrive(1, 2)
+    f_ready(2)
+    f_core(1)
+    n_line[1].relay(3)
+    f_finish(0)
+    hidden_back()
+    f_ready(0)
+    f_finish(1)
+    n_arrive(3)
+    gates(0, 3)
+    gates(3, 4)
+    f_ready(1)
+    feed(0, 4)
+    f_grad(2)
+    dy_line.flush()
+    back(2 + inner)
+    d_line.send(0, d_part.at[2 + inner])
+    back(3 - inner)
+    f_stage1(2)
+    f_grad(0)
+    back(1)
+    f_stage1(0)
+    d_line.send(1, d_part.at[1])
+    mirror(d_line, d_part, d_in)
+    back(0)
+    release()
+    f_grad(1)
+    f_stage1(1)
+    f_stage2(2)
+    f_stage2(0)
+    f_stage2(1)
+    y_terms()
+    y_send()
+    residual_back()
+    place_heads(mix, kept["d_attn"], lay.out_at, r)
+    place_heads(mix, kept["d_attn"], lay.out_at, r_other)
+    a_core_sums(1)
+    backward(1)
+    backward(4)
+    a_stage1(1, 0)
+    backward(0)
+    a_stage1(1, 2)
+    backward(2)
+    backward(3)
+    keys_back()
+    a_stage2(1, 0)
+    place_kv(r_other)
+    mirror(y_line, y_part, y_in)
+    a_stage1(1, 1)
+    place_heads(dq, normed[...], 0, r_other)
+    f_total(0, gate_hbm)
+    place_heads(dq, normed[...], 0, r)
     a_core_sums(0)
-    d_normed = dot_nn(dq[...], wq[...]) + dot_nn(dk, wkv[:kvw, :]) + dot_nn(dv, wkv[kvw:, :])
-    stream = tok_ref[...].astype(F32)
-    rstd1 = lax.rsqrt(jnp.sum(stream * stream, axis=1, keepdims=True) / MODEL_WIDTH + EPS)
-    gain1_grad = jnp.sum(d_normed * stream * rstd1, axis=0, keepdims=True)
-    nsum[0] = jnp.concatenate([gain1_grad, gain2_grad, jnp.zeros((6, MODEL_WIDTH), F32)], axis=0)
-    g_core = send(nsum.at[0], nin.at[0], sibling)
     a_stage2(1, 2)
+    a_line_sum(1, 0)
+    place_kv(r)
+    a_stage1(0, 0)
+    a_stage1(0, 1)
+    input_back()
+    gains_core()
+    a_stage2(0, 0)
+    a_stage2(1, 1)
+    a_line_sum(1, 2)
+    a_stage1(0, 2)
+    a_stage1(1, 3)
+    a_line_sum(1, 1)
+    gains_side()
+    a_stage2(0, 1)
+    a_mirror(1)
+    f_total(1, up_hbm)
+    a_line_sum(0, 0)
+    a_stage2(0, 2)
+    a_stage1(0, 3)
     a_stage2(1, 3)
-    a_stage1(0, 0)
-    a_line_sum(1, 0)
-    g_core.wait_recv()
-    nsum[1] = nsum[0] + nin[0]
-    g_x = send(nsum.at[1], nin.at[1], x_peer)
-    a_stage1(0, 1)
-    a_line_sum(1, 1)
-    a_stage2(0, 0)
-    g_x.wait_recv()
-    nsum[2] = nsum[1] + nin[1]
-    g_y = send(nsum.at[2], nin.at[2], y_peer)
-    a_stage1(0, 2)
-    a_line_sum(1, 2)
-    scaled1 = d_normed * gfull[0:1, :]
-    inner1 = jnp.sum(scaled1 * stream, axis=1, keepdims=True)
-    in_grad = d_res + rstd1 * scaled1 - stream * (rstd1 * rstd1 * rstd1 * inner1 / MODEL_WIDTH)
-    in_grad_ref[...] = in_grad.astype(BF16)
-    put(in_grad_ref, in_grad_hbm)
-    a_stage2(0, 1)
-    g_y.wait_recv()
-    nsum[3] = nsum[2] + nin[2]
-    n_sum.send(0, nsum.at[3])
-    a_stage1(0, 3)
-    a_line_sum(0, 0)
-    a_mirror(1)
-    y_line.arrive(1)
-    y_line.arrive(2)
-    y = resid[...] + y_part[0].astype(F32) + y_in[1].astype(F32) + y_in[2].astype(F32)
-    out_ref[...] = y.astype(BF16)
-    put(out_ref, out_hbm)
-    a_stage2(0, 2)
+    f_total(2, down_hbm)
+    y_total()
     a_line_sum(0, 1)
-    n_sum.arrive(0)
-    nsum[4] = nsum[3] + nin[3]
-    n_sum.send(2, nsum.at[4])
+    gains_mirror()
+    a_mirror(0)
+    a_line_sum(0, 2)
+    a_stage2(0, 3)
+    gains_x()
     a_line_sum(1, 3)
-    f_total(2, down_hbm)
-    a_mirror(0)
-    a_stage2(0, 3)
-    a_line_sum(0, 2)
-    f_total(0, gate_hbm)
-    f_total(1, up_hbm)
+    a_line_sum(0, 3)
     a_total(1)
-    n_sum.arrive(2)
-    nsum[5] = nsum[4] + nin[5]
-    gain_out[...] = nsum[5, :, lanes(c)]
-    a_line_sum(0, 3)
     a_total(0)
+    gains_y()
     links.flush()
-    for part in [dy_line, d_line, y_line, n_sum] + n_line + g_line:
+    for part in [d_line, y_line, n_sum] + g_line:
         part.flush()
     for copy in outgoing:
         copy.wait()
@@ -805,6 +904,7 @@
         vf(n * T, hid),
         vf(n * T, hid),
         vm(nl, lay.cores, frows, M),
+        vm(nl, lay.cores, frows, M),
         vf(8, M),
         vm(T, M),
         vm(G, per * T, D),
@@ -816,11 +916,10 @@
         vf(T, T),
         vf(T, T),
         vm(T, M),
+        vm(2, T, G * D),
         vf(G, T, D),
         vf(G, T, D),
-        vm(n, T, M),
         vm(n - 1, T, M),
-        vm(n, T, M),
         vm(n - 1, T, M),
         vm(3, nl, frows, M),
         vm(3, half, M),
@@ -836,12 +935,11 @@
         vf(2 + n, 8, M),
         vm(T, M),
         vm(T, M),
-        vf(lay.arows, W),
-        vf(3, frows, W),
+        vf(8, W),
         pltpu.SemaphoreType.DMA((count,)),
         pltpu.SemaphoreType.DMA((count,)),
         pltpu.SemaphoreType.DMA((6,)),
-        pltpu.SemaphoreType.DMA((8,)),
+        pltpu.SemaphoreType.DMA((9,)),
     ]
     return pl.pallas_call(
         functools.partial(layer_kernel, lay),
@@ -851,39 +949,46 @@
             jax.ShapeDtypeStruct((8, W), F32),
         )
         + tuple(jax.ShapeDtypeStruct(b.shape, F32) for b in blocks),
-        in_specs=[hbm, vmem, hbm, hbm, hbm, hbm, vmem, vmem, vmem, vmem, vmem],
-        out_specs=(hbm, hbm, vmem) + (hbm,) * 6,
+        in_specs=[hbm, vmem, hbm, hbm, hbm, hbm] + [vmem] * 6,
+        out_specs=(hbm,) * 9,
         scratch_shapes=scratch,
-        compiler_params=pltpu.CompilerParams(collective_id=0, has_side_effects=True, vmem_limit_bytes=62 * 2**20),
+        compiler_params=pltpu.CompilerParams(collective_id=0, has_side_effects=True, vmem_limit_bytes=63 * 2**20),
         name="whole_layer",
-    )(*blocks, tokens, cotangent, gains, seg_ids, parents)
+    )(*blocks, tokens, cotangent, *gains, seg_ids, parents)
 
 
 def finish_kernel(count, *refs):
-    held, (into, back) = refs[2 * count : 3 * count], refs[3 * count :]
-    first = [pltpu.make_async_copy(refs[i], held[i], into.at[i]) for i in range(count)]
-    last = [pltpu.make_async_copy(held[i], refs[count + i], back.at[i]) for i in range(count)]
+    sources, results, held = refs[:count], refs[count : 2 * count + 1], refs[2 * count + 1 : 3 * count + 1]
+    into, back = refs[3 * count + 1 :]
+    first = [pltpu.make_async_copy(sources[i], held[i], into.at[i]) for i in range(count)]
+    last = [pltpu.make_async_copy(held[i], results[i], back.at[i]) for i in range(count - 1)]
     for copy in first:
         copy.start()
-    for i in range(count):
+    for i in range(count - 1):
         first[i].wait()
         last[i].start()
+    first[-1].wait()
+    for i in range(2):
+        results[count - 1 + i][...] = held[-1][i]
     for copy in last:
         copy.wait()
 
 
-def finish(results):
+def finish(results, gain_rows):
     hbm = pl.BlockSpec(memory_space=pl.ANY)
-    count = len(results)
+    vmem = pl.BlockSpec(memory_space=pltpu.VMEM)
+    given = (*results, gain_rows)
+    count = len(given)
     dma = pltpu.SemaphoreType.DMA((count,))
+    vector = jax.ShapeDtypeStruct((gain_rows.shape[1],), gain_rows.dtype)
     return pl.pallas_call(
         functools.partial(finish_kernel, count),
-        out_shape=tuple(jax.ShapeDtypeStruct(v.shape, v.dtype) for v in results),
+        out_shape=tuple(jax.ShapeDtypeStruct(v.shape, v.dtype) for v in results) + (vector, vector),
         in_specs=[hbm] * count,
-        out_specs=(hbm,) * count,
-        scratch_shapes=[pltpu.VMEM(v.shape, v.dtype) for v in results] + [dma, dma],
+        out_specs=(hbm,) * len(results) + (vmem, vmem),
+        scratch_shapes=[pltpu.VMEM(v.shape, v.dtype) for v in given] + [dma, dma],
         name="finish",
-    )(*results)
+    )(*given)
 
 
 def body(lay, tokens, cotangent, seg_ids, parents, norm1_gain, w_query, key_value_weight, w_out, norm2_gain, w_gate, w_up, w_down):
@@ -896,23 +1001,22 @@
         w_up.T,
         w_down,
     )
-    gains = jnp.concatenate([norm1_gain[None], norm2_gain[None], jnp.zeros((6, W), F32)], axis=0)
     layer_out, in_grad, gain_sum, query, keyval, out, gate, up, down = whole_layer(
-        lay, blocks, tokens, cotangent, gains, seg_ids, parents
+        lay, blocks, tokens, cotangent, (norm1_gain, norm2_gain), seg_ids, parents
     )
-    layer_out, in_grad, query, keyval, out, gate, up, down = finish(
-        (layer_out, in_grad, query, keyval, out, gate, up, down)
+    layer_out, in_grad, query, keyval, out, gate, up, down, gain1_grad, gain2_grad = finish(
+        (layer_out, in_grad, query, keyval, out, gate, up, down), gain_sum
     )
     heads = QUERY_HEADS // lay.cores
     shape = (heads, HEAD_SIZE // lay.dp, W)
     return (
         layer_out,
         in_grad,
-        gain_sum[0],
+        gain1_grad,
         jnp.transpose(query.reshape(shape), (2, 0, 1)),
         keyval.T[:, None, :],
         out.reshape(shape),
-        gain_sum[1],
+        gain2_grad,
         gate.T,
         up.T,
         down,

time: 163 us -> 158 us (0.969)
  local copies, waits for them, and re-layouts: 2.11 us -> 0 us
  Pallas kernels: 159 us -> 157 us
    pallas_call x1, Pallas kernels: 157 us -> 154 us  [whole_layer(): pl.pallas_call(functools.partial(layer_kernel, lay), out_shape=(jax.Shape...]
where the time goes in v5:
time: 158 us
  Pallas kernels  157 us (99%)
    pallas_call x1, Pallas kernels, whole_layer(): pl.pallas_call(functools.partial(layer_kernel, lay), out_shape=(jax.Shape...  154 us
    pallas_call x1, Pallas kernels, finish(): pl.pallas_call(functools.partial(finish_kernel, count), out_shape=tuple((...  3.35 us

profile of v5, /device:TPU:0, one launch (start us, length us, event | category | flops | bytes accessed | tf_op | source)
XLA Modules:
  0.0 158.0 jit_solution(3076963992642859875)
XLA Ops:
  0.6 153.8 %whole_layer.1 = (bf16[128,1280]{1,0:T(8,128)(2,1)}, bf16[128,1280]{1,0:T(8,128)(2,1)}, f32[8,640]{1,0:T(8,128)}, f32[80,640]{1,0:T(8,128)}, f32[40,640]{1,0:T(8...) custom-call(bf16[80,640]{1,0:T(8,128)(2,1)} %bitcast.20, ...), custom_call_target="tpu_custom_call" | custom-call | tf_op jit(solution)/shard_map/whole_layer/pallas_call | solution.py:944
  154.5 3.3 %finish.1 = (bf16[128,1280]{1,0:T(8,128)(2,1)}, bf16[128,1280]{1,0:T(8,128)(2,1)}, f32[80,640]{1,0:T(8,128)}, f32[40,640]{1,0:T(8,128)}, f32[80,640]{1,0:T(8,128...) custom-call(bf16[128,1280]{1,0:T(8,128)(2,1)} %get-tuple-element.29.refs_0_,, ...), custom_call_target="tpu_custom_call" | custom-call | tf_op jit(solution)/shard_map/finish/pallas_call | solution.py:984
